TPU v7x, 128 devices: a whole 4x4x4 slice. The times are simulated.
128 devices in a mesh: seq: 8 (over x_lo, z), exp: 16 (over x_hi, y, core).
Axes of the slice: x: 4 (x_hi: 2, x_lo: 2; x = x_hi * 2 + x_lo), y: 4, z: 4, core: 2. Of those that a mesh axis runs over, the one named last changes fastest.
Arguments:
- queries: bfloat16 [64, 4096], P('exp'), may hold values from -80 to 80
- new_kv: bfloat16 [2, 64, 512], P(None, 'exp'), may hold values from -4 to 4
- kv_cache: bfloat16 [2, 64, 4096, 512], P(None, 'exp', 'seq'), may hold values from -4 to 4
- lengths: int32 [64], P('exp'), may hold values from 1 to 4096, as said below
- out_proj: bfloat16 [4096, 2048], P('seq'), may hold values from -0.09375 to 0.09375
- hidden_in: float32 [64, 2048], P('exp'), may hold values from -6 to 6
- norm_gain: float32 [2048], replicated, may hold values from 0.1 to 1.9
- router: bfloat16 [2048, 128], replicated, may hold values from -0.125 to 0.125
- expert_ids: int32 [64, 8], replicated, may hold values from 0 to 127, all different within a row; in each aligned block of 64 rows (0 to 63, 64 to 127, ...) at most 8 rows name the same one
- w_gate_up: bfloat16 [128, 2048, 1536], P(('seq', 'exp')), may hold values from -0.125 to 0.125
- w_down: bfloat16 [128, 768, 2048], P(('seq', 'exp')), may hold values from -0.21875 to 0.21875
- talk_proj: bfloat16 [2048, 1024], replicated, may hold values from -0.125 to 0.125
- talk_gain: float32 [1024], replicated, may hold values from 0.1 to 1.9
- talk_router: bfloat16 [1024, 128], replicated, may hold values from -0.1875 to 0.1875
- talk_ids: int32 [64, 8], replicated, may hold values from 0 to 127, all different within a row; in each aligned block of 64 rows (0 to 63, 64 to 127, ...) at most 8 rows name the same one
- talk_gate_up: bfloat16 [128, 1024, 768], P(('seq', 'exp')), may hold values from -0.1875 to 0.1875
- talk_down: bfloat16 [128, 384, 1024], P(('seq', 'exp')), may hold values from -0.3125 to 0.3125
Outputs:
- thinker_out: float32 [64, 2048], P('exp')
- talker_out: float32 [64, 1024], P('exp')
Inputs may be any that keep to these rules, and one draw needn't show every extreme that they name: `lengths`: some conversation uses all 4096 positions and some uses only one. `expert_ids`: each row names 8 different experts. Over all 64 rows no expert is named more than 8 times, and in every draw some expert is named exactly 8 times. `talk_ids`: as for expert_ids.
All inputs are finite; a program needn't handle non-finite values.
Results may differ from a plain program's by a relative error of at most 0.011.
Values may be sent and summed in bfloat16 or wider, within the bound.
No kernel may reach another device: no remote copies, remote signals or barrier semaphores. Data moves between devices by JAX's collectives and lax.ppermute only.
A program may use at most 128 MiB of HBM per device.

v0:
```python
import jax
import jax.numpy as jnp
from jax import lax
from jax.sharding import PartitionSpec as P

H = 32
KVH = 4
HD = 128


def joined(shard, axis, combine):
    everything = jax.tree.map(lambda part: lax.all_gather(part, axis), shard)
    first = jax.tree.map(lambda part: part[0], everything)

    def turn(k, so_far):
        return combine(so_far, jax.tree.map(lambda part: part[k], everything))

    return lax.fori_loop(1, lax.axis_size(axis), turn, first)


def merge_pair(former, latter):
    peak_a, total_a, mixed_a = former
    peak_b, total_b, mixed_b = latter
    peak = jnp.maximum(peak_a, peak_b)
    scale_a = jnp.exp(peak_a - peak)
    scale_b = jnp.exp(peak_b - peak)
    return (
        peak,
        total_a * scale_a + total_b * scale_b,
        mixed_a * scale_a[..., None] + mixed_b * scale_b[..., None],
    )


def expert_layer(stream, gain, router_w, picks, gate_up, down_w):
    own_rows, width = stream.shape
    all_rows, top_count = picks.shape
    experts = router_w.shape[1]
    local_experts = gate_up.shape[0]
    inner_width = down_w.shape[1]
    capacity = max(2, 2 * all_rows * top_count // experts)
    normed = (
        stream * lax.rsqrt(jnp.mean(stream * stream, axis=1, keepdims=True) + 1e-06) * gain
    ).astype(jnp.bfloat16)
    first_expert = (
        lax.axis_index("seq") * lax.axis_size("exp") + lax.axis_index("exp")
    ) * local_experts
    mine = first_expert + jnp.arange(local_experts, dtype=jnp.int32)
    flat_ids = picks.reshape(-1)
    match = (flat_ids[:, None] == mine[None, :]).astype(jnp.int32)
    rank = jnp.cumsum(match, axis=0) - 1
    slot_marks = jnp.logical_and(
        rank[:, :, None] == jnp.arange(capacity, dtype=jnp.int32)[None, None, :],
        match[:, :, None] == 1,
    ).astype(jnp.float32)
    placing = jnp.sum(slot_marks.reshape(all_rows, top_count, local_experts, capacity), axis=1)
    placing_bf = placing.astype(jnp.bfloat16)
    block = placing_bf
    slot_rows = jnp.einsum(
        "rec,rw->ecw",
        block,
        lax.all_gather(normed, "exp", axis=0, tiled=True),
        preferred_element_type=jnp.float32,
    ).astype(jnp.bfloat16)
    logits = jnp.einsum("ecw,wx->ecx", slot_rows, router_w, preferred_element_type=jnp.float32)
    labels = jnp.arange(experts, dtype=jnp.int32)
    pick_marks = (picks[:, :, None] == labels[None, None, :]).astype(jnp.float32)
    slot_picks = jnp.einsum("rec,rkx->eckx", placing, pick_marks, precision=lax.Precision.HIGHEST)
    picked = jnp.sum(slot_picks * logits[:, :, None, :], axis=-1)
    sigmoid_total = jnp.sum(jax.nn.sigmoid(picked), axis=-1)
    own_marks = (labels[None, :] == mine[:, None]).astype(jnp.float32)
    own_logit = jnp.sum(logits * own_marks[:, None, :], axis=-1)
    gates = jax.nn.sigmoid(own_logit) / sigmoid_total
    both = jnp.einsum("ecw,ewf->ecf", slot_rows, gate_up, preferred_element_type=jnp.float32)
    inner = (jax.nn.silu(both[..., :inner_width]) * both[..., inner_width:]).astype(jnp.bfloat16)
    replies = jnp.einsum("ecf,efw->ecw", inner, down_w, preferred_element_type=jnp.float32).astype(
        jnp.bfloat16
    )
    weighted = gates[:, :, None] * replies.astype(jnp.float32)
    block = placing
    summed = lax.psum(
        jnp.einsum("rec,ecw->rw", block, weighted, precision=lax.Precision.HIGHEST), ("seq", "exp")
    )
    gathered = lax.dynamic_slice_in_dim(summed, lax.axis_index("exp") * own_rows, own_rows, 0)
    return stream + gathered


def local_attention(queries, new_kv, kv_cache, lengths):
    count = queries.shape[0]
    span = kv_cache.shape[2]
    groups = H // KVH
    scale = HD ** (-0.5)
    query_b = queries.reshape(count, KVH, groups, HD)
    keys = kv_cache[0].reshape(count, span, KVH, HD)
    values = kv_cache[1].reshape(count, span, KVH, HD)
    fresh_keys = new_kv[0].reshape(count, KVH, HD)
    fresh_values = new_kv[1].reshape(count, KVH, HD)
    cached = (
        jnp.einsum("ckjd,cpkd->ckjp", query_b, keys, preferred_element_type=jnp.float32) * scale
    )
    fresh = (
        jnp.einsum("ckjd,ckd->ckj", query_b, fresh_keys, preferred_element_type=jnp.float32) * scale
    )
    seq_index = lax.axis_index("seq")
    places = seq_index * span + jnp.arange(span, dtype=jnp.int32)
    valid = places[None, :] < lengths[:, None]
    owner = seq_index == 0
    masked = jnp.where(valid[:, None, None, :], cached, -1e30)
    fresh_masked = jnp.where(owner, fresh, -1e30)
    peak = jnp.maximum(jnp.max(masked, axis=-1), fresh_masked)
    weights = jnp.where(valid[:, None, None, :], jnp.exp(masked - peak[..., None]), 0.0)
    fresh_weight = jnp.where(owner, jnp.exp(fresh_masked - peak), 0.0)
    totals = jnp.sum(weights, axis=-1) + fresh_weight
    upper = weights.astype(jnp.bfloat16)
    lower = (weights - upper.astype(jnp.float32)).astype(jnp.bfloat16)
    mixed = jnp.einsum("ckjp,cpkd->ckjd", upper, values, preferred_element_type=jnp.float32)
    mixed = mixed + jnp.einsum("ckjp,cpkd->ckjd", lower, values, preferred_element_type=jnp.float32)
    mixed = mixed + fresh_weight[..., None] * fresh_values[:, :, None, :].astype(jnp.float32)
    return (peak.reshape(count, H), totals.reshape(count, H), mixed.reshape(count, H, HD))


def on_device(
    queries,
    new_kv,
    kv_cache,
    lengths,
    out_proj,
    hidden_in,
    norm_gain,
    router,
    expert_ids,
    w_gate_up,
    w_down,
    talk_proj,
    talk_gain,
    talk_router,
    talk_ids,
    talk_gate_up,
    talk_down,
):
    count = queries.shape[0]
    seq_ways = lax.axis_size("seq")
    own_heads = H // seq_ways
    peak, totals, mixed = local_attention(queries, new_kv, kv_cache, lengths)
    peak, totals, mixed = joined((peak, totals, mixed), "seq", merge_pair)
    first_head = lax.axis_index("seq") * own_heads
    totals = lax.dynamic_slice_in_dim(totals, first_head, own_heads, 1)
    mixed = lax.dynamic_slice_in_dim(mixed, first_head, own_heads, 1)
    attn = (mixed / totals[..., None]).reshape(count, own_heads * HD).astype(jnp.bfloat16)
    head_term = jnp.dot(attn, out_proj, preferred_element_type=jnp.float32)
    projected = lax.psum(head_term, "seq")
    state = hidden_in + projected
    thinker = expert_layer(state, norm_gain, router, expert_ids, w_gate_up, w_down)
    talk_in = jnp.dot(thinker.astype(jnp.bfloat16), talk_proj, preferred_element_type=jnp.float32)
    talker = expert_layer(talk_in, talk_gain, talk_router, talk_ids, talk_gate_up, talk_down)
    return (thinker, talker)


def solution(mesh):
    placed = (
        P("exp", None),
        P(None, "exp", None),
        P(None, "exp", "seq", None),
        P("exp"),
        P("seq", None),
        P("exp", None),
        P(),
        P(),
        P(),
        P(("seq", "exp"), None, None),
        P(("seq", "exp"), None, None),
        P(),
        P(),
        P(),
        P(),
        P(("seq", "exp"), None, None),
        P(("seq", "exp"), None, None),
    )
    return jax.shard_map(
        on_device,
        mesh=mesh,
        in_specs=placed,
        out_specs=(P("exp", None), P("exp", None)),
        check_vma=False,
    )
```

profile of v0, /device:TPU:0, one launch (start us, length us, event | category | flops | bytes accessed | tf_op | source)
XLA Modules:
  0.0 509.1 jit_solution(3766259248674176018)
XLA Ops:
  7.2 1.4 broadcast_compare_fusion.1
  9.3 0.7 slice_reduce_fusion.1
  10.0 0.6 compare_convert_fusion.2
  10.6 4.4 fusion.77
  15.0 4.2 copy.66
  19.2 0.6 slice_convert_fusion
  20.0 2.1 fusion.78
  22.2 25.0 %all_gather.15 = f32[8,4,32]{2,1,0:T(4,128)S(1)} all-gather(f32[1,4,32]{2,1,0:T(4,128)S(1)} %all_gather_reshape.9), channel_id=1, replica_groups=mesh['seq'=8,'exp'=16] {'seq'}, dimensions={0}, use_global_device_ids=true | all-gather | bytes 4608 | tf_op jit(solution)/shard_map/all_gather | solution.py:12
  47.3 0.6 fusion.76
  48.0 23.6 %all_gather.16 = f32[8,4,32]{2,1,0:T(4,128)S(1)} all-gather(f32[1,4,32]{2,1,0:T(4,128)S(1)} %all_gather_reshape.10), channel_id=1, replica_groups=mesh['seq'=8,'exp'=16] {'seq'}, dimensions={0}, use_global_device_ids=true | all-gather | bytes 4608 | tf_op jit(solution)/shard_map/all_gather | solution.py:12
  71.7 4.2 copy.67
  75.8 2.3 fusion.34
  78.1 0.7 reshape.477
  78.8 2.3 fusion.23
  81.1 29.2 %all_gather.17 = f32[8,4,32,128]{3,2,1,0:T(8,128)S(1)} all-gather(f32[1,4,32,128]{3,2,1,0:T(8,128)S(1)} %fusion.23), channel_id=1, replica_groups=mesh['seq'=8,'exp'=16] {'seq'}, dimensions={0}, use_global_device_ids=true | all-gather | bytes 589824 | tf_op jit(solution)/shard_map/all_gather | solution.py:12
  110.3 0.8 copy-done.1
  111.1 11.8 %while.19 = (s32[]{:T(128)}, f32[4,32]{1,0:T(4,128)S(1)}, f32[4,32]{1,0:T(4,128)S(1)}, f32[4,32,128]{2,1,0:T(8,128)S(1)}, f32[8,4,32]{2,1,0:T(4,128)S(1)}, /*ind...) while((s32[]{:T(128)}, f32[4,32]{1,0:T(4,128)S(1)}, ...), condition=%wide.region_3.4_spmd, body=%wide.region_2.3_spmd.sunk | while | flops 49925 | bytes 201879 | solution.py:18
  111.1 0.7 fusion.101
  111.8 0.9 fusion.102
  112.8 0.7 fusion.101
  113.5 0.9 fusion.102
  114.5 0.7 fusion.101
  115.2 0.9 fusion.102
  116.2 0.7 fusion.101
  116.9 0.9 fusion.102
  117.8 0.7 fusion.101
  118.5 0.9 fusion.102
  119.5 0.7 fusion.101
  120.2 0.9 fusion.102
  121.2 0.7 fusion.101
  121.9 0.9 fusion.102
  123.1 2.0 fusion.63
  125.0 31.0 %psum.21 = f32[4,2048]{1,0:T(4,128)S(1)} all-reduce(f32[4,2048]{1,0:T(4,128)S(1)} %fusion.63), channel_id=1, replica_groups=mesh['seq'=8,'exp'=16] {'seq'}, use_global_device_ids=true, to_apply=%region_4.5 | all-reduce | flops 8192 | bytes 65536 | tf_op jit(solution)/shard_map/psum | solution.py:150
  156.7 26.2 %all-gather = bf16[16,4,2048]{2,1,0:T(4,128)(2,1)} all-gather(bf16[1,4,2048]{2,1,0:T(4,128)(2,1)S(1)} %fusion.52), channel_id=1, replica_groups=mesh['seq'=8,'exp'=16] {'exp'}, dimensions={0}, use_global_device_ids=true | all-gather | bytes 278528 | tf_op jit(solution)/shard_map/all_gather | solution.py:61
  182.9 1.0 reshape.481
  184.1 1.3 multiply_reduce_fusion.3
  185.9 3.7 fusion.7
  189.6 0.5 fusion.16
  190.1 1.4 fusion.79
  192.9 137.9 %all-reduce.3.cloned.1.call-done = f32[64,2048]{1,0:T(8,128)} async-done(((f32[64,2048]{1,0:T(8,128)}), f32[64,2048]{1,0:T(8,128)}) %all-reduce.3.cloned.1.call-update) | async-done | bytes 524304 | tf_op jit(solution)/shard_map/psum | solution.py:80
  330.7 0.8 dynamic-slice_add_fusion
  331.6 3.0 multiply_reduce_fusion.1
  334.7 23.2 %all-gather.1 = bf16[16,4,1024]{2,1,0:T(4,128)(2,1)S(1)} all-gather(bf16[1,4,1024]{2,1,0:T(4,128)(2,1)S(1)} %fusion.58), channel_id=1, replica_groups=mesh['seq'=8,'exp'=16] {'exp'}, dimensions={0}, use_global_device_ids=true | all-gather | bytes 139264 | tf_op jit(solution)/shard_map/all_gather | solution.py:61
  358.1 1.3 multiply_reduce_fusion.2
  359.8 1.7 fusion.24
  361.7 1.1 fusion.80
  362.9 138.0 %all-reduce.5.cloned.1.call-done = f32[64,1024]{1,0:T(8,128)} async-done(((f32[64,1024]{1,0:T(8,128)}), f32[64,1024]{1,0:T(8,128)}) %all-reduce.5.cloned.1.call-update) | async-done | bytes 262160 | tf_op jit(solution)/shard_map/psum | solution.py:80
  500.9 1.4 dynamic-slice_add_fusion.1
  (88 shorter events, 4.7 us)
Async XLA Ops:
  7.2 182.4 %copy-start = (bf16[1,768,2048]{2,1,0:T(8,128)(2,1)S(1)}, bf16[1,768,2048]{2,1,0:T(8,128)(2,1)}, u32[]{:S(2)}) copy-start(bf16[1,768,2048]{2,1,0:T(8,128)(2,1)} %param.29) | copy-start | bytes 9437188
  7.2 323.5 %all-reduce.3.cloned.1.call-start = ((), (), s32[]{:S(2)}) async-start(), calls=%async_computation | async-start | bytes 1048576 | tf_op jit(solution)/shard_map/psum | solution.py:80
  15.0 4.2 copy-start.8
  15.0 4.8 copy-start.15
  15.0 4.9 copy-start.5
  71.7 4.2 copy-start.4
  81.1 75.0 %copy-start.16 = (s32[4]{0:T(128)S(1)}, s32[4]{0:T(128)}, u32[]{:S(2)}) copy-start(s32[4]{0:T(128)} %slice_reduce_fusion.1) | copy-start | bytes 52
  81.1 75.4 %copy-start.6 = (f32[4,2048]{1,0:T(4,128)S(1)}, f32[4,2048]{1,0:T(4,128)}, u32[]{:S(2)}) copy-start(f32[4,2048]{1,0:T(4,128)} %param.24) | copy-start | bytes 98308
  110.3 0.8 copy-start.1
  110.3 46.3 %copy-start.7 = (f32[2048]{0:T(1024)S(1)}, f32[2048]{0:T(1024)}, u32[]{:S(2)}) copy-start(f32[2048]{0:T(1024)} %param.25) | copy-start | bytes 24580
  111.1 72.8 %copy-start.13 = (pred[64,8]{0,1:T(8,128)(4,1)S(1)}, pred[64,8]{0,1:T(8,128)(4,1)}, u32[]{:S(2)}) copy-start(pred[64,8]{0,1:T(8,128)(4,1)} %get-tuple-element.219) | copy-start | bytes 1540
  122.9 61.3 %copy-start.14 = (f32[128]{0:T(128)S(1)}, f32[128]{0:T(128)}, u32[]{:S(2)}) copy-start(f32[128]{0:T(128)} %compare_convert_fusion.2) | copy-start | bytes 1540
  123.0 62.4 %copy-start.9 = (s32[64,8]{0,1:T(8,128)S(1)}, s32[64,8]{0,1:T(8,128)}, u32[]{:S(2)}) copy-start(s32[64,8]{0,1:T(8,128)} %param.27) | copy-start | bytes 6148
  189.6 3.2 copy-start.12
  191.6 309.3 %all-reduce.5.cloned.1.call-start = ((), (), s32[]{:S(2)}) async-start(), calls=%async_computation.1 | async-start | bytes 524288 | tf_op jit(solution)/shard_map/psum | solution.py:80
  331.6 3.0 copy-start.3
  331.6 3.0 copy-start.10
  331.6 27.8 %copy-start.11 = (s32[64,8]{0,1:T(8,128)S(1)}, s32[64,8]{0,1:T(8,128)}, u32[]{:S(2)}) copy-start(s32[64,8]{0,1:T(8,128)} %param.33) | copy-start | bytes 6148
  357.9 3.6 copy-start.2
Sparse Core Ops, SparseCore 0:
  191.7 138.9 all-reduce.2
  363.0 137.8 all-reduce.4
where the time goes:
time: 511 us; the launch traced here: 509 us
  waiting for transfers between devices  276 us (54%)
  blocking collectives  158 us (31%)
  matrix products  24.1 us (5%)
  other arithmetic  18.8 us (4%)
  local copies, waits for them, and re-layouts  17.5 us (3%)
  between operations  14.3 us (3%)
    psum x2, waiting for transfers between devices, expert_layer(): lax.psum(jnp.einsum('rec,ecw->rw', block, weighted, precision=lax.Precisi...  276 us
    all_gather x3, blocking collectives, joined(): everything = jax.tree.map(lambda part: lax.all_gather(part, axis), shard)  77.8 us
    all_gather x2, blocking collectives, expert_layer(): lax.all_gather(normed, 'exp', axis=0, tiled=True)  49.4 us
    psum x1, blocking collectives, on_device(): projected = lax.psum(head_term, 'seq')  31 us
    unnamed x38, local copies, waits for them, and re-layouts  10.2 us
  transfers between devices with their start and end apart: 2, of which 2 were waited for; matrix products, arithmetic and copies ran while one was open for 0% of the time, Pallas kernels for 0%

commit v1 on v0

v1 whole, which is shorter than its diff:
```python
import functools
import jax
import jax.numpy as jnp
from jax import lax
from jax.experimental import pallas as pl
from jax.experimental.pallas import tpu as pltpu
from jax.sharding import PartitionSpec as P

F32 = jnp.float32
BF16 = jnp.bfloat16
HEADS = 32
KVH = 4
HD = 128
D = 2048
DT = 1024
FF = 768
FT = 384
EXPERTS = 128
ROWS = 64
SEQ = 8
EXP = 16
OWN = 4
SPAN = 512
EPS = 1e-6
NEG = -1e30


def iota(shape, dim):
    return lax.broadcasted_iota(jnp.int32, shape, dim)


def dot(a, b):
    return jnp.dot(a, b, preferred_element_type=F32)


def dot_t(a, b):
    return lax.dot_general(a, b, (((1,), (1,)), ((), ())), preferred_element_type=F32)


def start_all(pairs, sems):
    copies = []
    for k, (src, dst) in enumerate(pairs):
        copy = pltpu.make_async_copy(src, dst, sems.at[k])
        copy.start()
        copies.append(copy)
    return copies


def my_expert():
    return lax.axis_index("seq") * EXP + lax.axis_index("exp")


def slots_by_row(ids, me):
    eq = (ids == me).astype(F32)
    match = dot_t(jnp.ones((8, 8), F32), eq)
    before = (iota((ROWS, ROWS), 0) < iota((ROWS, ROWS), 1)).astype(F32)
    rank = dot(match, before)
    hit = jnp.logical_and(rank == iota((8, ROWS), 0).astype(F32), match > 0.5)
    return jnp.where(hit, 1.0, 0.0)


def rows_by_slot(ids, me, lanes):
    eq = (ids == me).astype(F32)
    match = dot(eq, jnp.ones((8, lanes), F32))
    before = (iota((ROWS, ROWS), 1) < iota((ROWS, ROWS), 0)).astype(F32)
    rank = dot(before, match)
    slot = jnp.bitwise_and(iota((ROWS, lanes), 1), 7).astype(F32)
    hit = jnp.logical_and(rank == slot, match > 0.5)
    return jnp.where(hit, 1.0, 0.0)


def spread_marks(count, bits, group=None):
    r = iota((ROWS, count), 0)
    i = iota((ROWS, count), 1)
    owner = i >> (2 + bits)
    if group is not None:
        owner = 2 * owner + group
    same = jnp.logical_and(owner == (r >> 2), (i & 3) == (r & 3))
    return jnp.where(same, 1.0, 0.0)


def spread_marks_t(count, bits, group=None):
    i = iota((count, ROWS), 0)
    r = iota((count, ROWS), 1)
    owner = i >> (2 + bits)
    if group is not None:
        owner = 2 * owner + group
    same = jnp.logical_and(owner == (r >> 2), (i & 3) == (r & 3))
    return jnp.where(same, 1.0, 0.0)


def by_chunk(marks, chunks):
    i = iota(marks.shape, 1)
    return jnp.concatenate(
        [jnp.where(((i >> 2) & (chunks - 1)) == j, marks, 0.0) for j in range(chunks)], axis=0
    )


def placing(ids, me, count, bits, group=None):
    chunks = 1 << bits
    lanes = 8 * chunks
    marks = dot(spread_marks_t(count, bits, group), rows_by_slot(ids, me, lanes))
    chunk = (iota((count, lanes), 0) >> 2) & (chunks - 1)
    return jnp.where((iota((count, lanes), 1) >> 3) == chunk, marks, 0.0).astype(BF16)


def pick_marks(slots, ids):
    lane = iota((ROWS, EXPERTS), 1)
    named = jnp.zeros((ROWS, EXPERTS), F32)
    for k in range(ids.shape[1]):
        named = named + (ids[:, k : k + 1] == lane).astype(F32)
    return dot(slots, named)


def gates_of(logits, picks, me):
    sig = 1.0 / (1.0 + jnp.exp(-logits))
    total = jnp.sum(sig * picks, axis=1, keepdims=True)
    own = jnp.sum(jnp.where(iota(sig.shape, 1) == me, sig, 0.0), axis=1, keepdims=True)
    return jnp.where(total > 0.0, own / total, 0.0)


def silu(a):
    return a / (1.0 + jnp.exp(-a))


def attend_kernel(len_ref, q_ref, new_ref, kv_ref, out_ref, k_buf, v_buf, q_buf, o_buf, t_buf, sems):
    pairs = []
    for c in range(OWN):
        pairs += [(kv_ref.at[0, c], k_buf.at[c]), (kv_ref.at[1, c], v_buf.at[c])]
    copies = start_all(pairs, sems)
    seq = lax.axis_index("seq")
    scale = HD ** (-0.5)
    query = q_ref[...].astype(F32)
    for h in range(HEADS):
        q_buf[4 * h : 4 * h + 4, :] = query[:, HD * h : HD * h + HD]
    lane = iota((HEADS, KVH * HD), 1)
    diag = (iota((HEADS, KVH * HD), 0) >> 3) == (lane >> 7)
    place = lane + seq * SPAN
    tail_lane = iota((HEADS, HD), 1)
    for c in range(OWN):
        q = q_buf[pl.ds(c, HEADS, stride=4), :]
        wide = jnp.where(diag, jnp.concatenate([q] * KVH, axis=1), 0.0)
        fresh_key = new_ref[0, c : c + 1, :].astype(F32)
        fresh_value = new_ref[1, c : c + 1, :].astype(F32)
        fresh = jnp.sum(wide * fresh_key, axis=1, keepdims=True) * scale
        fresh = jnp.where(seq == 0, fresh, NEG)
        copies[2 * c].wait()
        scores = dot_t(wide.astype(BF16), k_buf[c]) * scale
        valid = place < len_ref[c]
        scores = jnp.where(valid, scores, NEG)
        peak = jnp.maximum(jnp.max(scores, axis=1, keepdims=True), fresh)
        peak = peak.astype(BF16).astype(F32)
        weights = jnp.where(valid, jnp.exp(scores - peak), 0.0).astype(BF16)
        fresh_weight = jnp.where(seq == 0, jnp.exp(fresh - peak), 0.0)
        total = jnp.sum(weights.astype(F32), axis=1, keepdims=True) + fresh_weight
        copies[2 * c + 1].wait()
        mixed = dot(weights, v_buf[c]) + fresh_weight * fresh_value
        mixed = jnp.where(diag, mixed, 0.0)
        mixed = (mixed[:, :HD] + mixed[:, HD : 2 * HD]) + (
            mixed[:, 2 * HD : 3 * HD] + mixed[:, 3 * HD :]
        )
        upper = total.astype(BF16).astype(F32)
        tail = jnp.where(tail_lane == 0, peak, jnp.where(tail_lane == 1, upper, total - upper))
        o_buf[pl.ds(c, HEADS, stride=4), :] = mixed
        t_buf[pl.ds(c, HEADS, stride=4), :] = tail
    out_ref[:, :, :HD] = o_buf[...].reshape(SEQ, 16, HD).astype(BF16)
    out_ref[:, :, HD:] = t_buf[...].reshape(SEQ, 16, HD).astype(BF16)


def project_kernel(recv_ref, proj_ref, out_ref, p_buf, row_buf, sems):
    copies = start_all([(proj_ref, p_buf)], sems)
    got = recv_ref[...].astype(F32)
    peak = got[:, :, HD : HD + 1]
    total = got[:, :, HD + 1 : HD + 2] + got[:, :, HD + 2 : HD + 3]
    scale = jnp.exp(peak - jnp.max(peak, axis=0, keepdims=True))
    total = jnp.sum(scale * total, axis=0)
    mixed = jnp.sum(scale * got[:, :, :HD], axis=0) / total
    attn = jnp.concatenate([mixed[4 * h : 4 * h + 4] for h in range(4)], axis=1).astype(BF16)
    copies[0].wait()
    part = dot(attn, p_buf[...])
    for j in range(4):
        row_buf[4 * j : 4 * j + 4, :] = part[:, 512 * j : 512 * j + 512]
    msg = row_buf[...].astype(BF16)
    for d in range(SEQ):
        out_ref[d] = msg


def norm_kernel(recv_ref, hidden_ref, gain_ref, out_ref, state_ref, buf, gain_buf):
    for j in range(4):
        cols = slice(512 * j, 512 * j + 512)
        buf[4 * j : 4 * j + 4, :] = hidden_ref[:, cols]
        gain_buf[4 * j : 4 * j + 4, :] = jnp.broadcast_to(gain_ref[:, cols], (OWN, 512))
    state = buf[...] + jnp.sum(recv_ref[...].astype(F32), axis=0)
    square = jnp.sum(state * state, axis=1, keepdims=True)
    square = (square[0:4] + square[4:8]) + (square[8:12] + square[12:16])
    inv = lax.rsqrt(square * (1.0 / D) + EPS)
    normed = (state * jnp.concatenate([inv] * 4, axis=0) * gain_buf[...]).astype(BF16)
    for d in range(EXP):
        out_ref[d] = normed
    buf[...] = state
    for s in range(SEQ):
        for k in range(2):
            first = (s % 2) * 256 + k * 128
            state_ref[s, 4 * k : 4 * k + 4, :] = buf[4 * (s // 2) : 4 * (s // 2) + 4, first : first + 128]


def expert_kernel(
    recv_ref, ids_ref, router_ref, up_ref, down_ref, out_ref, r_buf, a_buf, b_buf, d_buf, sems
):
    parts = FF // 256
    pairs = [(router_ref, r_buf)]
    for f in range(parts):
        pairs += [
            (up_ref.at[0, :, pl.ds(256 * f, 256)], a_buf.at[f]),
            (up_ref.at[0, :, pl.ds(FF + 256 * f, 256)], b_buf.at[f]),
            (down_ref.at[0, pl.ds(256 * f, 256), :], d_buf.at[f]),
        ]
    copies = start_all(pairs, sems)
    me = my_expert()
    ids = ids_ref[...]
    slots = slots_by_row(ids, me)
    picks = pick_marks(slots, ids)
    place = placing(ids, me, 128, 1)
    chosen = by_chunk(dot(slots, spread_marks(256, 2)), 4).astype(BF16)
    rows = dot(chosen, recv_ref[...])
    rows = jnp.concatenate([rows[8 * j : 8 * j + 8] for j in range(4)], axis=1).astype(BF16)
    copies[0].wait()
    gates = gates_of(dot(rows, r_buf[...]), picks, me)
    reply = jnp.zeros((8, D), F32)
    for f in range(parts):
        copies[3 * f + 1].wait()
        a = dot(rows, a_buf[f])
        copies[3 * f + 2].wait()
        b = dot(rows, b_buf[f])
        inner = (silu(a) * b).astype(BF16)
        copies[3 * f + 3].wait()
        reply = reply + dot(inner, d_buf[f])
    reply = gates * reply.astype(BF16).astype(F32)
    halves = [
        jnp.concatenate(
            [reply[:, 256 * s + 128 * k : 256 * s + 128 * k + 128] for s in range(SEQ)], axis=1
        )
        for k in range(2)
    ]
    sent = dot(place, jnp.concatenate(halves, axis=0).astype(BF16))
    for s in range(SEQ):
        block = sent[:, 128 * s : 128 * s + 128].reshape(EXP, 8, 128)
        out_ref[EXP * s : EXP * s + EXP] = block.astype(BF16)


def total_kernel(recv_ref, state_ref, out_ref):
    total = jnp.sum(recv_ref[...].astype(F32), axis=0) + state_ref[lax.axis_index("seq")]
    out_ref[...] = jnp.broadcast_to(total.astype(BF16)[None], out_ref.shape)


def talker_kernel(
    recv_ref,
    ids_ref,
    gain_ref,
    proj_ref,
    router_ref,
    up_ref,
    down_ref,
    thinker_ref,
    talk_ref,
    keep_ref,
    give_ref,
    p_buf,
    r_buf,
    u_buf,
    d_buf,
    sems,
):
    pairs = [(proj_ref.at[pl.ds(512 * q, 512), :], p_buf.at[q]) for q in range(4)]
    pairs += [(router_ref, r_buf), (up_ref.at[0], u_buf), (down_ref.at[0], d_buf)]
    copies = start_all(pairs, sems)
    me = my_expert()
    group = lax.axis_index("exp")
    core = group & 1
    ids = ids_ref[...]
    slots = slots_by_row(ids, me)
    picks = pick_marks(slots, ids)
    keep_place = placing(ids, me, 128, 2, core)
    give_place = placing(ids, me, 128, 2, 1 - core)
    slot = iota((8, ROWS), 0)
    own = jnp.logical_and(iota((8, ROWS), 1) == OWN * group + slot, slot < OWN)
    wanted = jnp.concatenate([slots, jnp.where(own, 1.0, 0.0)], axis=0)
    chosen = by_chunk(dot(wanted, spread_marks(128, 1)), 2).astype(BF16)
    talk_in = jnp.zeros((16, DT), F32)
    for q in range(4):
        cols = []
        for s in (2 * q, 2 * q + 1):
            got = dot(chosen, recv_ref[128 * s : 128 * s + 128, :])
            cols += [got[:16], got[16:]]
        part = jnp.concatenate(cols, axis=1)
        thinker_ref[:, 512 * q : 512 * q + 512] = part[8 : 8 + OWN]
        copies[q].wait()
        talk_in = talk_in + dot(part.astype(BF16), p_buf[q])
    talk_ref[...] = talk_in[8 : 8 + OWN]
    talk_in = talk_in[:8]
    mean = jnp.mean(talk_in * talk_in, axis=1, keepdims=True)
    normed = (talk_in * lax.rsqrt(mean + EPS) * gain_ref[...]).astype(BF16)
    copies[4].wait()
    gates = gates_of(dot(normed, r_buf[...]), picks, me)
    copies[5].wait()
    both = dot(normed, u_buf[...])
    inner = (silu(both[:, :FT]) * both[:, FT:]).astype(BF16)
    copies[6].wait()
    reply = gates * dot(inner, d_buf[...]).astype(BF16).astype(F32)
    stacked = jnp.concatenate([reply[:, 256 * j : 256 * j + 256] for j in range(4)], axis=0)
    stacked = stacked.astype(BF16)
    keep_ref[...] = dot(keep_place, stacked).reshape(8, 16, 256).astype(BF16)
    give_ref[...] = dot(give_place, stacked).reshape(8, 16, 256).astype(BF16)


def pair_kernel(keep_ref, got_ref, out_ref):
    total = (keep_ref[...].astype(F32) + got_ref[...].astype(F32)).astype(BF16)
    for s in range(SEQ):
        out_ref[8 * s : 8 * s + 8] = total


def finish_kernel(recv_ref, talk_ref, out_ref, buf):
    buf[...] = jnp.sum(recv_ref[...].astype(F32), axis=0)
    for j in range(4):
        cols = slice(256 * j, 256 * j + 256)
        out_ref[:, cols] = talk_ref[:, cols] + buf[4 * j : 4 * j + 4, :]


def call(kernel, outs, args, where, scratch=(), mib=16):
    spaces = {"v": pltpu.VMEM, "s": pltpu.SMEM, "h": pl.ANY}
    many = isinstance(outs, list)
    whole = pl.BlockSpec(memory_space=pltpu.VMEM)
    return pl.pallas_call(
        kernel,
        out_shape=outs,
        in_specs=[pl.BlockSpec(memory_space=spaces[w]) for w in where],
        out_specs=[whole] * len(outs) if many else whole,
        scratch_shapes=list(scratch),
        compiler_params=pltpu.CompilerParams(vmem_limit_bytes=mib << 20),
    )(*args)


def array(shape, dtype):
    return jax.ShapeDtypeStruct(shape, dtype)


def exchange(msg, axis, groups=None):
    return lax.all_to_all(msg, axis, 0, 0, axis_index_groups=groups)


def on_device(
    queries,
    new_kv,
    kv_cache,
    lengths,
    out_proj,
    hidden_in,
    norm_gain,
    router,
    expert_ids,
    w_gate_up,
    w_down,
    talk_proj,
    talk_gain,
    talk_router,
    talk_ids,
    talk_gate_up,
    talk_down,
):
    both = ("seq", "exp")
    dma = pltpu.SemaphoreType.DMA
    msg = call(
        attend_kernel,
        array((SEQ, 16, 256), BF16),
        (lengths, queries, new_kv, kv_cache),
        "svvh",
        [
            pltpu.VMEM((OWN, SPAN, KVH * HD), BF16),
            pltpu.VMEM((OWN, SPAN, KVH * HD), BF16),
            pltpu.VMEM((HEADS * OWN, HD), F32),
            pltpu.VMEM((HEADS * OWN, HD), F32),
            pltpu.VMEM((HEADS * OWN, HD), F32),
            dma((2 * OWN,)),
        ],
    )
    msg = call(
        project_kernel,
        array((SEQ, 16, 512), BF16),
        (exchange(msg, "seq"), out_proj),
        "vh",
        [pltpu.VMEM((512, D), BF16), pltpu.VMEM((16, 512), F32), dma((1,))],
    )
    msg, state = call(
        norm_kernel,
        [array((EXP, 16, 512), BF16), array((SEQ, 8, 128), F32)],
        (exchange(msg, "seq"), hidden_in, norm_gain.reshape(1, D)),
        "vvv",
        [pltpu.VMEM((16, 512), F32), pltpu.VMEM((16, 512), F32)],
    )
    msg = call(
        expert_kernel,
        array((SEQ * EXP, 8, 128), BF16),
        (exchange(msg, "exp").reshape(256, 512), expert_ids, router, w_gate_up, w_down),
        "vvhhh",
        [
            pltpu.VMEM((D, EXPERTS), BF16),
            pltpu.VMEM((FF // 256, D, 256), BF16),
            pltpu.VMEM((FF // 256, D, 256), BF16),
            pltpu.VMEM((FF // 256, 256, D), BF16),
            dma((1 + 3 * (FF // 256),)),
        ],
    )
    msg = call(
        total_kernel,
        array((SEQ * EXP, 8, 128), BF16),
        (exchange(msg, both), state),
        "vv",
    )
    thinker, talk_in, keep, give = call(
        talker_kernel,
        [
            array((OWN, D), F32),
            array((OWN, DT), F32),
            array((8, 16, 256), BF16),
            array((8, 16, 256), BF16),
        ],
        (
            exchange(msg, both).reshape(1024, 128),
            talk_ids,
            talk_gain.reshape(1, DT),
            talk_proj,
            talk_router,
            talk_gate_up,
            talk_down,
        ),
        "vvvhhhh",
        [
            pltpu.VMEM((4, 512, DT), BF16),
            pltpu.VMEM((DT, EXPERTS), BF16),
            pltpu.VMEM((DT, 2 * FT), BF16),
            pltpu.VMEM((FT, DT), BF16),
            dma((7,)),
        ],
    )
    got = lax.ppermute(give, "exp", [(e, e ^ 1) for e in range(EXP)])
    msg = call(pair_kernel, array((64, 16, 256), BF16), (keep, got), "vv")
    same_core = [[2 * i + core for i in range(64)] for core in range(2)]
    talker = call(
        finish_kernel,
        array((OWN, DT), F32),
        (exchange(msg, both, same_core), talk_in),
        "vv",
        [pltpu.VMEM((16, 256), F32)],
    )
    return (thinker, talker)


def solution(mesh):
    placed = (
        P("exp", None),
        P(None, "exp", None),
        P(None, "exp", "seq", None),
        P("exp"),
        P("seq", None),
        P("exp", None),
        P(),
        P(),
        P(),
        P(("seq", "exp"), None, None),
        P(("seq", "exp"), None, None),
        P(),
        P(),
        P(),
        P(),
        P(("seq", "exp"), None, None),
        P(("seq", "exp"), None, None),
    )
    return jax.shard_map(
        on_device,
        mesh=mesh,
        in_specs=placed,
        out_specs=(P("exp", None), P("exp", None)),
        check_vma=False,
    )
```

time: 511 us -> 120 us (0.23)
  waiting for transfers between devices: 276 us -> 21.1 us
  blocking collectives: 158 us -> 54.4 us
  matrix products: 24.1 us -> 0 us
  other arithmetic: 18.8 us -> 0 us
  Pallas kernels: 0 us -> 14.4 us
  between operations: 14.3 us -> 0.75 us
  starting transfers between devices: 0.08 us -> 11.9 us
    psum x2 -> x0, waiting for transfers between devices: 276 us -> none  [expert_layer(): lax.psum(jnp.einsum('rec,ecw->rw', block, weighted, precision=lax.Precisi...]
    all_gather x5 -> x0, blocking collectives: 127 us -> none  [the longest x3 77.8 us: joined(): everything = jax.tree.map(lambda part: lax.all_gather(part, axis), shard)]
    all_to_all x0 -> x4, blocking collectives: none -> 54.4 us  [exchange(): return lax.all_to_all(msg, axis, 0, 0, axis_index_groups=groups)]
    psum x1 -> x0, blocking collectives: 31 us -> none  [on_device(): projected = lax.psum(head_term, 'seq')]
    dot_general x18 -> x0, matrix products: 24.1 us -> none  [the longest x2 5.45 us: expert_layer(): jnp.einsum('ecw,ewf->ecf', slot_rows, gate_up, preferred_element_type=jnp...]
    all_to_all x0 -> x2, waiting for transfers between devices: none -> 19.9 us  [exchange(): return lax.all_to_all(msg, axis, 0, 0, axis_index_groups=groups)]
    pallas_call x0 -> x8, Pallas kernels: none -> 14.4 us  [call(): pl.pallas_call(kernel, out_shape=outs, in_specs=[pl.BlockSpec(memory_spac...]
    add x18 -> x0, other arithmetic: 14.4 us -> none  [the longest x7 6.64 us: merge_pair(): mixed_a * scale_a[..., None] + mixed_b * scale_b[..., None]]
  transfers between devices with their start and end apart: 2 -> 3, of which waited for: 2 -> 3; matrix products, arithmetic and copies ran while one was open for 0% -> 0% of each run, Pallas kernels for 0% -> 0%
where the time goes in v1:
time: 120 us; the launch traced here: 119 us
  blocking collectives  54.4 us (45%)
  waiting for transfers between devices  21.1 us (18%)
  local copies, waits for them, and re-layouts  16.3 us (14%)
  Pallas kernels  14.4 us (12%)
  starting transfers between devices  11.9 us (10%)
    all_to_all x4, blocking collectives, exchange(): return lax.all_to_all(msg, axis, 0, 0, axis_index_groups=groups)  54.4 us
    all_to_all x2, waiting for transfers between devices, exchange(): return lax.all_to_all(msg, axis, 0, 0, axis_index_groups=groups)  19.9 us
    unnamed x38, local copies, waits for them, and re-layouts  16.3 us
    pallas_call x8, Pallas kernels, call(): pl.pallas_call(kernel, out_shape=outs, in_specs=[pl.BlockSpec(memory_spac...  14.4 us
    all_to_all x2, starting transfers between devices, exchange(): return lax.all_to_all(msg, axis, 0, 0, axis_index_groups=groups)  11.7 us
  transfers between devices with their start and end apart: 3, of which 3 were waited for; matrix products, arithmetic and copies ran while one was open for 0% of the time, Pallas kernels for 0%

profile of v1, /device:TPU:0, one launch (start us, length us, event | category | flops | bytes accessed | tf_op | source)
XLA Modules:
  0.0 118.9 jit_solution(9964197381489187555)
XLA Ops:
  0.6 0.0 copy-start.1
  0.6 2.2 %copy-done.1 = bf16[2,4,512,512]{3,2,1,0:T(8,128)(2,1)S(1)} copy-done((bf16[2,4,512,512]{3,2,1,0:T(8,128)(2,1)S(1)}, bf16[2,4,512,512]{3,2,1,0:T(8,128)(2,1)}, u32[]{:S(2)}) %copy-start.1) | copy-done | bytes 4194328
  2.8 0.0 copy-start.10
  2.8 0.8 copy-done.10
  3.6 0.0 copy-start.12
  3.6 0.7 copy-done.12
  4.3 0.0 copy-start.15
  4.3 0.7 copy-done.15
  4.9 0.0 copy-start.11
  4.9 0.0 copy-start.13
  4.9 0.0 copy-start.16
  4.9 0.0 copy-start.3
  4.9 3.6 %shard_map.176 = bf16[8,16,256]{2,1,0:T(8,128)(2,1)S(1)} custom-call(s32[4]{0:T(128)S(1)} %copy-done.15, bf16[4,4096]{1,0:T(4,128)(2,1)S(1)} %copy-done.10, bf16[2,4,512]{2,1,0:T(4,128)(2,1)S(1)} %copy-done.12, bf16[2,4,512,512]{3,2,1,0:T(8,128)(2,1)S(1)} %copy-done.1), custom_call_target="tpu_custom_call" | custom-call | tf_op jit(solution)/shard_map/pallas_call | solution.py:333
  8.5 12.5 %all_to_all.30.recv_ref = bf16[8,16,256]{2,1,0:T(8,128)(2,1)S(1)} all-to-all(bf16[8,16,256]{2,1,0:T(8,128)(2,1)S(1)} %shard_map.176), channel_id=1, replica_groups=mesh['seq'=8,'exp'=16] {'seq'}, dimensions={0} | all-to-all | bytes 131072 | tf_op jit(solution)/shard_map/all_to_all | solution.py:348
  21.0 0.0 copy-start.4
  21.0 1.6 %copy-done.4 = bf16[512,2048]{1,0:T(8,128)(2,1)S(1)} copy-done((bf16[512,2048]{1,0:T(8,128)(2,1)S(1)}, bf16[512,2048]{1,0:T(8,128)(2,1)}, u32[]{:S(2)}) %copy-start.4) | copy-done | bytes 2097176
  22.6 0.8 shard_map.177
  23.4 9.0 %all_to_all.31.recv_ref = bf16[8,16,512]{2,1,0:T(8,128)(2,1)S(1)} all-to-all(bf16[8,16,512]{2,1,0:T(8,128)(2,1)S(1)} %shard_map.177), channel_id=1, replica_groups=mesh['seq'=8,'exp'=16] {'seq'}, dimensions={0} | all-to-all | bytes 262144 | tf_op jit(solution)/shard_map/all_to_all | solution.py:348
  32.4 0.0 copy-done.11
  32.4 0.0 copy-done.13
  32.4 0.2 shard_map.178
  32.6 0.0 copy-start.9
  32.6 0.7 copy-done.9
  33.3 6.7 %all-to-all-start.2 = ((bf16[16,16,512]{2,1,0:T(8,128)(2,1)}), bf16[16,16,512]{2,1,0:T(8,128)(2,1)S(1)}, u32[]{:S(2)}, u32[]{:S(2)}) async-start(bf16[16,16,512]{2,1,0:T(8,128)(2,1)} %copy-done.9), calls=%async_computation.2 | async-start | bytes 524288 | tf_op jit(solution)/shard_map/all_to_all | solution.py:348
  40.1 0.0 copy-done.16
  40.1 0.1 copy.19.ids_ref
  40.2 9.5 %all-to-all-done.2 = bf16[16,16,512]{2,1,0:T(8,128)(2,1)S(1)} async-done(((bf16[16,16,512]{2,1,0:T(8,128)(2,1)}), bf16[16,16,512]{2,1,0:T(8,128)(2,1)S(1)}, u32[]{:S(2)}, u32[]{:S(2)}) %all-to-all-start.2) | async-done | bytes 262176 | tf_op jit(solution)/shard_map/all_to_all | solution.py:348
  49.6 0.0 copy-done.3
  49.7 2.8 %copy-done = bf16[1,2048,1536]{2,1,0:T(8,128)(2,1)S(1)} copy-done((bf16[1,2048,1536]{2,1,0:T(8,128)(2,1)S(1)}, bf16[1,2048,1536]{2,1,0:T(8,128)(2,1)}, u32[]{:S(2)}) %copy-start) | copy-done | bytes 6291480
  52.4 0.0 copy-start.7
  52.4 1.0 copy-done.7
  53.5 4.6 %shard_map.179 = bf16[128,8,128]{2,1,0:T(8,128)(2,1)S(1)} custom-call(bf16[256,512]{1,0:T(8,128)(2,1)S(1)} %bitcast.5, s32[64,8]{1,0:T(8,128)S(1)} %copy.19.ids_ref, bf16[2048,128]{1,0:T(8,128)(2,1)S(1)} %copy-done.7, bf16[1,2048,1536]{2,1,0:T(8,128)(2,1)S(1)} %copy-done, bf16[1,768,2048]{2,1,0:T(8,128)(2,1)S(1)} %copy-done.3), custom_call_target="tpu_custom_call" | custom-call | tf_op jit(solution)/shard_map/pallas_call | solution.py:333
  58.1 14.5 %all_to_all.32.recv_ref = bf16[128,8,128]{2,1,0:T(8,128)(2,1)S(1)} all-to-all(bf16[128,8,128]{2,1,0:T(8,128)(2,1)S(1)} %shard_map.179), channel_id=1, replica_groups=mesh['seq'=8,'exp'=16] {'seq','exp'}, dimensions={0} | all-to-all | bytes 524288 | tf_op jit(solution)/shard_map/all_to_all | solution.py:348
  72.7 0.9 shard_map.180
  73.5 5.0 %all-to-all-start.4 = ((bf16[128,8,128]{2,1,0:T(8,128)(2,1)}), bf16[128,8,128]{2,1,0:T(8,128)(2,1)S(1)}, u32[]{:S(2)}, u32[]{:S(2)}) async-start(bf16[128,8,128]{2,1,0:T(8,128)(2,1)} %shard_map.180), calls=%async_computation.4 | async-start | bytes 524288 | tf_op jit(solution)/shard_map/all_to_all | solution.py:348
  78.5 0.0 copy-done.17
  78.6 0.1 copy.20.ids_ref
  78.6 10.5 %all-to-all-done.4 = bf16[128,8,128]{2,1,0:T(8,128)(2,1)S(1)} async-done(((bf16[128,8,128]{2,1,0:T(8,128)(2,1)}), bf16[128,8,128]{2,1,0:T(8,128)(2,1)S(1)}, u32[]{:S(2)}, u32[]{:S(2)}) %all-to-all-start.4) | async-done | bytes 262176 | tf_op jit(solution)/shard_map/all_to_all | solution.py:348
  89.1 0.0 copy-done.14
  89.1 2.2 %copy-done.2 = bf16[2048,1024]{1,0:T(8,128)(2,1)S(1)} copy-done((bf16[2048,1024]{1,0:T(8,128)(2,1)S(1)}, bf16[2048,1024]{1,0:T(8,128)(2,1)}, u32[]{:S(2)}) %copy-start.2) | copy-done | bytes 4194328
  91.3 1.4 %copy-done.5 = bf16[1,1024,768]{2,1,0:T(8,128)(2,1)S(1)} copy-done((bf16[1,1024,768]{2,1,0:T(8,128)(2,1)S(1)}, bf16[1,1024,768]{2,1,0:T(8,128)(2,1)}, u32[]{:S(2)}) %copy-start.5) | copy-done | bytes 1572888
  92.7 1.1 copy-done.6
  93.8 0.9 copy-done.8
  94.8 3.6 %shard_map.181 = (f32[4,2048]{1,0:T(4,128)}, f32[4,1024]{1,0:T(4,128)S(1)}, bf16[8,16,256]{2,1,0:T(8,128)(2,1)S(1)}, bf16[8,16,256]{2,1,0:T(8,128)(2,1)S(1)}) custom-call(bf16[1024,128]{1,0:T(8,128)(2,1)S(1)} %bitcast.4, s32[64,8]{1,0:T(8,128)S(1)} %copy.20.ids_ref, f32[1,1024]{1,0:T(1,128)S(1)} %bitcast.7, bf16[2048,1024]{1,0:T(8,128)(2,1)S(1)} %copy-done.2, ...), custom_call_target="tpu_custom_call" | custom-call | tf_op jit(solution)/shard_map/pallas_call | solution.py:333
  98.4 0.2 collective-permute-start
  98.6 1.1 collective-permute-done.got_ref
  99.8 18.4 %all_to_all.33.recv_ref = bf16[64,16,256]{2,1,0:T(8,128)(2,1)S(1)} all-to-all(bf16[64,16,256]{2,1,0:T(8,128)(2,1)S(1)} %shard_map.182), channel_id=1, replica_groups={{0,2,4,6,8,10,12,14,16,18,20,22,24,26,28,30,32,34,36,38,40,42,44,46,48,..., dimensions={0} | all-to-all | bytes 1048576 | tf_op jit(solution)/shard_map/all_to_all | solution.py:348
  118.2 0.7 shard_map.183
  (8 shorter events, 0.0 us)
Async XLA Ops:
  0.6 2.2 %copy-start.1 = (bf16[2,4,512,512]{3,2,1,0:T(8,128)(2,1)S(1)}, bf16[2,4,512,512]{3,2,1,0:T(8,128)(2,1)}, u32[]{:S(2)}) copy-start(bf16[2,4,512,512]{3,2,1,0:T(8,128)(2,1)} %kv_ref.1) | copy-start | bytes 12582916
  2.8 0.8 copy-start.10
  3.6 0.7 copy-start.12
  4.3 0.7 copy-start.15
  4.9 27.5 %copy-start.11 = (f32[4,2048]{1,0:T(4,128)S(1)}, f32[4,2048]{1,0:T(4,128)}, u32[]{:S(2)}) copy-start(f32[4,2048]{1,0:T(4,128)} %hidden_ref.1) | copy-start | bytes 98308
  4.9 27.5 %copy-start.13 = (f32[2048]{0:T(1024)S(1)}, f32[2048]{0:T(1024)}, u32[]{:S(2)}) copy-start(f32[2048]{0:T(1024)} %param.23) | copy-start | bytes 24580
  4.9 35.2 %copy-start.16 = (s32[64,8]{0,1:T(8,128)S(1)}, s32[64,8]{0,1:T(8,128)}, u32[]{:S(2)}) copy-start(s32[64,8]{0,1:T(8,128)} %param.25) | copy-start | bytes 6148
  4.9 44.7 %copy-start.3 = (bf16[1,768,2048]{2,1,0:T(8,128)(2,1)S(1)}, bf16[1,768,2048]{2,1,0:T(8,128)(2,1)}, u32[]{:S(2)}) copy-start(bf16[1,768,2048]{2,1,0:T(8,128)(2,1)} %down_ref.2) | copy-start | bytes 9437188
  21.0 1.6 %copy-start.4 = (bf16[512,2048]{1,0:T(8,128)(2,1)S(1)}, bf16[512,2048]{1,0:T(8,128)(2,1)}, u32[]{:S(2)}) copy-start(bf16[512,2048]{1,0:T(8,128)(2,1)} %proj_ref.2) | copy-start | bytes 6291460
  32.6 0.7 copy-start.9
  33.3 16.3 %all-to-all-start.2 = ((bf16[16,16,512]{2,1,0:T(8,128)(2,1)}), bf16[16,16,512]{2,1,0:T(8,128)(2,1)S(1)}, u32[]{:S(2)}, u32[]{:S(2)}) async-start(bf16[16,16,512]{2,1,0:T(8,128)(2,1)} %copy-done.9), calls=%async_computation.2 | async-start | bytes 524288 | tf_op jit(solution)/shard_map/all_to_all | solution.py:348
  49.7 2.8 %copy-start = (bf16[1,2048,1536]{2,1,0:T(8,128)(2,1)S(1)}, bf16[1,2048,1536]{2,1,0:T(8,128)(2,1)}, u32[]{:S(2)}) copy-start(bf16[1,2048,1536]{2,1,0:T(8,128)(2,1)} %up_ref.2) | copy-start | bytes 18874372
  52.4 1.0 copy-start.7
  53.5 25.1 %copy-start.17 = (s32[64,8]{0,1:T(8,128)S(1)}, s32[64,8]{0,1:T(8,128)}, u32[]{:S(2)}) copy-start(s32[64,8]{0,1:T(8,128)} %param.31) | copy-start | bytes 6148
  53.5 35.6 %copy-start.14 = (f32[1024]{0:T(1024)S(1)}, f32[1024]{0:T(1024)}, u32[]{:S(2)}) copy-start(f32[1024]{0:T(1024)} %param.29) | copy-start | bytes 12292
  73.5 15.5 %all-to-all-start.4 = ((bf16[128,8,128]{2,1,0:T(8,128)(2,1)}), bf16[128,8,128]{2,1,0:T(8,128)(2,1)S(1)}, u32[]{:S(2)}, u32[]{:S(2)}) async-start(bf16[128,8,128]{2,1,0:T(8,128)(2,1)} %shard_map.180), calls=%async_computation.4 | async-start | bytes 524288 | tf_op jit(solution)/shard_map/all_to_all | solution.py:348
  89.1 2.2 %copy-start.2 = (bf16[2048,1024]{1,0:T(8,128)(2,1)S(1)}, bf16[2048,1024]{1,0:T(8,128)(2,1)}, u32[]{:S(2)}) copy-start(bf16[2048,1024]{1,0:T(8,128)(2,1)} %proj_ref.3) | copy-start | bytes 12582916
  91.3 1.4 %copy-start.5 = (bf16[1,1024,768]{2,1,0:T(8,128)(2,1)S(1)}, bf16[1,1024,768]{2,1,0:T(8,128)(2,1)}, u32[]{:S(2)}) copy-start(bf16[1,1024,768]{2,1,0:T(8,128)(2,1)} %up_ref.3) | copy-start | bytes 4718596
  92.7 1.1 copy-start.6
  93.8 0.9 copy-start.8
  98.4 1.3 %collective-permute-start = (bf16[8,16,256]{2,1,0:T(8,128)(2,1)S(1)}, bf16[8,16,256]{2,1,0:T(8,128)(2,1)S(1)}, u32[]{:S(2)}, u32[]{:S(2)}) collective-permute-start(bf16[8,16,256]{2,1,0:T(8,128)(2,1)S(1)} %get-tuple-element.12), channel_id=1, source_target_pairs={{0,1},{1,0},{2,3},{3,2},{4,5},{5,4},{6,7},{7,6},{8,9},{9,8},{10,11... | collective-permute-start | bytes 196616 | tf_op jit(solution)/shard_map/ppermute | solution.py:445

commit v2 on v1

--- a/solution.py
+++ b/solution.py
@@ -22,6 +22,7 @@
 OWN = 4
 SPAN = 512
 EPS = 1e-6
+COST = 10**11
 NEG = -1e30
 
 
@@ -37,35 +38,16 @@
     return lax.dot_general(a, b, (((1,), (1,)), ((), ())), preferred_element_type=F32)
 
 
-def start_all(pairs, sems):
-    copies = []
-    for k, (src, dst) in enumerate(pairs):
-        copy = pltpu.make_async_copy(src, dst, sems.at[k])
-        copy.start()
-        copies.append(copy)
-    return copies
-
-
 def my_expert():
     return lax.axis_index("seq") * EXP + lax.axis_index("exp")
 
 
 def slots_by_row(ids, me):
-    eq = (ids == me).astype(F32)
-    match = dot_t(jnp.ones((8, 8), F32), eq)
+    match = jnp.sum((ids == me).astype(F32), axis=0, keepdims=True)
+    match = jnp.broadcast_to(match, (8, ROWS))
     before = (iota((ROWS, ROWS), 0) < iota((ROWS, ROWS), 1)).astype(F32)
     rank = dot(match, before)
     hit = jnp.logical_and(rank == iota((8, ROWS), 0).astype(F32), match > 0.5)
-    return jnp.where(hit, 1.0, 0.0)
-
-
-def rows_by_slot(ids, me, lanes):
-    eq = (ids == me).astype(F32)
-    match = dot(eq, jnp.ones((8, lanes), F32))
-    before = (iota((ROWS, ROWS), 1) < iota((ROWS, ROWS), 0)).astype(F32)
-    rank = dot(before, match)
-    slot = jnp.bitwise_and(iota((ROWS, lanes), 1), 7).astype(F32)
-    hit = jnp.logical_and(rank == slot, match > 0.5)
     return jnp.where(hit, 1.0, 0.0)
 
 
@@ -96,20 +78,20 @@
     )
 
 
-def placing(ids, me, count, bits, group=None):
+def placing(slots, count, bits, group=None):
     chunks = 1 << bits
     lanes = 8 * chunks
-    marks = dot(spread_marks_t(count, bits, group), rows_by_slot(ids, me, lanes))
+    marks = dot_t(spread_marks_t(count, bits, group), jnp.concatenate([slots] * chunks, axis=0))
     chunk = (iota((count, lanes), 0) >> 2) & (chunks - 1)
     return jnp.where((iota((count, lanes), 1) >> 3) == chunk, marks, 0.0).astype(BF16)
 
 
 def pick_marks(slots, ids):
-    lane = iota((ROWS, EXPERTS), 1)
-    named = jnp.zeros((ROWS, EXPERTS), F32)
-    for k in range(ids.shape[1]):
-        named = named + (ids[:, k : k + 1] == lane).astype(F32)
-    return dot(slots, named)
+    expert = iota((EXPERTS, ROWS), 0)
+    named = jnp.zeros((EXPERTS, ROWS), F32)
+    for k in range(ids.shape[0]):
+        named = named + (ids[k : k + 1, :] == expert).astype(F32)
+    return dot_t(slots, named)
 
 
 def gates_of(logits, picks, me):
@@ -123,11 +105,24 @@
     return a / (1.0 + jnp.exp(-a))
 
 
-def attend_kernel(len_ref, q_ref, new_ref, kv_ref, out_ref, k_buf, v_buf, q_buf, o_buf, t_buf, sems):
-    pairs = []
+def start_all(pairs, sems):
+    copies = []
+    for k, (src, dst) in enumerate(pairs):
+        copy = pltpu.make_async_copy(src, dst, sems.at[k])
+        copy.start()
+        copies.append(copy)
+    return copies
+
+
+def attend_kernel(
+    len_hbm, q_hbm, new_hbm, kv_hbm, out_ref, len_ref, q_ref, new_ref, kv_ref, q_buf, o_buf, t_buf, sems
+):
+    pairs = [(q_hbm, q_ref), (new_hbm, new_ref), (len_hbm, len_ref)]
     for c in range(OWN):
-        pairs += [(kv_ref.at[0, c], k_buf.at[c]), (kv_ref.at[1, c], v_buf.at[c])]
+        pairs += [(kv_hbm.at[t, c], kv_ref.at[t, c]) for t in range(2)]
     copies = start_all(pairs, sems)
+    for copy in copies[:3]:
+        copy.wait()
     seq = lax.axis_index("seq")
     scale = HD ** (-0.5)
     query = q_ref[...].astype(F32)
@@ -144,8 +139,8 @@
         fresh_value = new_ref[1, c : c + 1, :].astype(F32)
         fresh = jnp.sum(wide * fresh_key, axis=1, keepdims=True) * scale
         fresh = jnp.where(seq == 0, fresh, NEG)
-        copies[2 * c].wait()
-        scores = dot_t(wide.astype(BF16), k_buf[c]) * scale
+        copies[2 * c + 3].wait()
+        scores = dot_t(wide.astype(BF16), kv_ref[0, c]) * scale
         valid = place < len_ref[c]
         scores = jnp.where(valid, scores, NEG)
         peak = jnp.maximum(jnp.max(scores, axis=1, keepdims=True), fresh)
@@ -153,8 +148,8 @@
         weights = jnp.where(valid, jnp.exp(scores - peak), 0.0).astype(BF16)
         fresh_weight = jnp.where(seq == 0, jnp.exp(fresh - peak), 0.0)
         total = jnp.sum(weights.astype(F32), axis=1, keepdims=True) + fresh_weight
-        copies[2 * c + 1].wait()
-        mixed = dot(weights, v_buf[c]) + fresh_weight * fresh_value
+        copies[2 * c + 4].wait()
+        mixed = dot(weights, kv_ref[1, c]) + fresh_weight * fresh_value
         mixed = jnp.where(diag, mixed, 0.0)
         mixed = (mixed[:, :HD] + mixed[:, HD : 2 * HD]) + (
             mixed[:, 2 * HD : 3 * HD] + mixed[:, 3 * HD :]
@@ -167,8 +162,7 @@
     out_ref[:, :, HD:] = t_buf[...].reshape(SEQ, 16, HD).astype(BF16)
 
 
-def project_kernel(recv_ref, proj_ref, out_ref, p_buf, row_buf, sems):
-    copies = start_all([(proj_ref, p_buf)], sems)
+def project_kernel(recv_ref, proj_ref, out_ref, row_buf):
     got = recv_ref[...].astype(F32)
     peak = got[:, :, HD : HD + 1]
     total = got[:, :, HD + 1 : HD + 2] + got[:, :, HD + 2 : HD + 3]
@@ -176,8 +170,7 @@
     total = jnp.sum(scale * total, axis=0)
     mixed = jnp.sum(scale * got[:, :, :HD], axis=0) / total
     attn = jnp.concatenate([mixed[4 * h : 4 * h + 4] for h in range(4)], axis=1).astype(BF16)
-    copies[0].wait()
-    part = dot(attn, p_buf[...])
+    part = dot(attn, proj_ref[...])
     for j in range(4):
         row_buf[4 * j : 4 * j + 4, :] = part[:, 512 * j : 512 * j + 512]
     msg = row_buf[...].astype(BF16)
@@ -204,37 +197,19 @@
             state_ref[s, 4 * k : 4 * k + 4, :] = buf[4 * (s // 2) : 4 * (s // 2) + 4, first : first + 128]
 
 
-def expert_kernel(
-    recv_ref, ids_ref, router_ref, up_ref, down_ref, out_ref, r_buf, a_buf, b_buf, d_buf, sems
-):
-    parts = FF // 256
-    pairs = [(router_ref, r_buf)]
-    for f in range(parts):
-        pairs += [
-            (up_ref.at[0, :, pl.ds(256 * f, 256)], a_buf.at[f]),
-            (up_ref.at[0, :, pl.ds(FF + 256 * f, 256)], b_buf.at[f]),
-            (down_ref.at[0, pl.ds(256 * f, 256), :], d_buf.at[f]),
-        ]
-    copies = start_all(pairs, sems)
+def expert_kernel(recv_ref, ids_ref, router_ref, up_ref, down_ref, out_ref):
     me = my_expert()
     ids = ids_ref[...]
     slots = slots_by_row(ids, me)
     picks = pick_marks(slots, ids)
-    place = placing(ids, me, 128, 1)
+    place = placing(slots, 128, 1)
     chosen = by_chunk(dot(slots, spread_marks(256, 2)), 4).astype(BF16)
     rows = dot(chosen, recv_ref[...])
     rows = jnp.concatenate([rows[8 * j : 8 * j + 8] for j in range(4)], axis=1).astype(BF16)
-    copies[0].wait()
-    gates = gates_of(dot(rows, r_buf[...]), picks, me)
-    reply = jnp.zeros((8, D), F32)
-    for f in range(parts):
-        copies[3 * f + 1].wait()
-        a = dot(rows, a_buf[f])
-        copies[3 * f + 2].wait()
-        b = dot(rows, b_buf[f])
-        inner = (silu(a) * b).astype(BF16)
-        copies[3 * f + 3].wait()
-        reply = reply + dot(inner, d_buf[f])
+    gates = gates_of(dot(rows, router_ref[...]), picks, me)
+    both = dot(rows, up_ref[0])
+    inner = (silu(both[:, :FF]) * both[:, FF:]).astype(BF16)
+    reply = dot(inner, down_ref[0])
     reply = gates * reply.astype(BF16).astype(F32)
     halves = [
         jnp.concatenate(
@@ -265,23 +240,15 @@
     talk_ref,
     keep_ref,
     give_ref,
-    p_buf,
-    r_buf,
-    u_buf,
-    d_buf,
-    sems,
 ):
-    pairs = [(proj_ref.at[pl.ds(512 * q, 512), :], p_buf.at[q]) for q in range(4)]
-    pairs += [(router_ref, r_buf), (up_ref.at[0], u_buf), (down_ref.at[0], d_buf)]
-    copies = start_all(pairs, sems)
     me = my_expert()
     group = lax.axis_index("exp")
     core = group & 1
     ids = ids_ref[...]
     slots = slots_by_row(ids, me)
     picks = pick_marks(slots, ids)
-    keep_place = placing(ids, me, 128, 2, core)
-    give_place = placing(ids, me, 128, 2, 1 - core)
+    keep_place = placing(slots, 128, 2, core)
+    give_place = placing(slots, 128, 2, 1 - core)
     slot = iota((8, ROWS), 0)
     own = jnp.logical_and(iota((8, ROWS), 1) == OWN * group + slot, slot < OWN)
     wanted = jnp.concatenate([slots, jnp.where(own, 1.0, 0.0)], axis=0)
@@ -294,19 +261,15 @@
             cols += [got[:16], got[16:]]
         part = jnp.concatenate(cols, axis=1)
         thinker_ref[:, 512 * q : 512 * q + 512] = part[8 : 8 + OWN]
-        copies[q].wait()
-        talk_in = talk_in + dot(part.astype(BF16), p_buf[q])
+        talk_in = talk_in + dot(part.astype(BF16), proj_ref[512 * q : 512 * q + 512, :])
     talk_ref[...] = talk_in[8 : 8 + OWN]
     talk_in = talk_in[:8]
     mean = jnp.mean(talk_in * talk_in, axis=1, keepdims=True)
     normed = (talk_in * lax.rsqrt(mean + EPS) * gain_ref[...]).astype(BF16)
-    copies[4].wait()
-    gates = gates_of(dot(normed, r_buf[...]), picks, me)
-    copies[5].wait()
-    both = dot(normed, u_buf[...])
+    gates = gates_of(dot(normed, router_ref[...]), picks, me)
+    both = dot(normed, up_ref[0])
     inner = (silu(both[:, :FT]) * both[:, FT:]).astype(BF16)
-    copies[6].wait()
-    reply = gates * dot(inner, d_buf[...]).astype(BF16).astype(F32)
+    reply = gates * dot(inner, down_ref[0]).astype(BF16).astype(F32)
     stacked = jnp.concatenate([reply[:, 256 * j : 256 * j + 256] for j in range(4)], axis=0)
     stacked = stacked.astype(BF16)
     keep_ref[...] = dot(keep_place, stacked).reshape(8, 16, 256).astype(BF16)
@@ -326,8 +289,8 @@
         out_ref[:, cols] = talk_ref[:, cols] + buf[4 * j : 4 * j + 4, :]
 
 
-def call(kernel, outs, args, where, scratch=(), mib=16):
-    spaces = {"v": pltpu.VMEM, "s": pltpu.SMEM, "h": pl.ANY}
+def call(kernel, outs, args, where, scratch=(), mib=16, flops=COST):
+    spaces = {"v": pltpu.VMEM, "s": pltpu.SMEM, "h": pltpu.HBM}
     many = isinstance(outs, list)
     whole = pl.BlockSpec(memory_space=pltpu.VMEM)
     return pl.pallas_call(
@@ -336,6 +299,7 @@
         in_specs=[pl.BlockSpec(memory_space=spaces[w]) for w in where],
         out_specs=[whole] * len(outs) if many else whole,
         scratch_shapes=list(scratch),
+        cost_estimate=pl.CostEstimate(flops=flops, bytes_accessed=1 << 20, transcendentals=0),
         compiler_params=pltpu.CompilerParams(vmem_limit_bytes=mib << 20),
     )(*args)
 
@@ -368,27 +332,29 @@
     talk_down,
 ):
     both = ("seq", "exp")
-    dma = pltpu.SemaphoreType.DMA
     msg = call(
         attend_kernel,
         array((SEQ, 16, 256), BF16),
         (lengths, queries, new_kv, kv_cache),
-        "svvh",
+        "hhhh",
         [
-            pltpu.VMEM((OWN, SPAN, KVH * HD), BF16),
-            pltpu.VMEM((OWN, SPAN, KVH * HD), BF16),
+            pltpu.SMEM((OWN,), jnp.int32),
+            pltpu.VMEM((OWN, HEADS * HD), BF16),
+            pltpu.VMEM((2, OWN, KVH * HD), BF16),
+            pltpu.VMEM((2, OWN, SPAN, KVH * HD), BF16),
             pltpu.VMEM((HEADS * OWN, HD), F32),
             pltpu.VMEM((HEADS * OWN, HD), F32),
             pltpu.VMEM((HEADS * OWN, HD), F32),
-            dma((2 * OWN,)),
+            pltpu.SemaphoreType.DMA((3 + 2 * OWN,)),
         ],
+        mib=60,
     )
     msg = call(
         project_kernel,
         array((SEQ, 16, 512), BF16),
         (exchange(msg, "seq"), out_proj),
-        "vh",
-        [pltpu.VMEM((512, D), BF16), pltpu.VMEM((16, 512), F32), dma((1,))],
+        "vv",
+        [pltpu.VMEM((16, 512), F32)],
     )
     msg, state = call(
         norm_kernel,
@@ -400,15 +366,8 @@
     msg = call(
         expert_kernel,
         array((SEQ * EXP, 8, 128), BF16),
-        (exchange(msg, "exp").reshape(256, 512), expert_ids, router, w_gate_up, w_down),
-        "vvhhh",
-        [
-            pltpu.VMEM((D, EXPERTS), BF16),
-            pltpu.VMEM((FF // 256, D, 256), BF16),
-            pltpu.VMEM((FF // 256, D, 256), BF16),
-            pltpu.VMEM((FF // 256, 256, D), BF16),
-            dma((1 + 3 * (FF // 256),)),
-        ],
+        (exchange(msg, "exp").reshape(256, 512), expert_ids.T, router, w_gate_up, w_down),
+        "vvvvv",
     )
     msg = call(
         total_kernel,
@@ -426,21 +385,14 @@
         ],
         (
             exchange(msg, both).reshape(1024, 128),
-            talk_ids,
+            talk_ids.T,
             talk_gain.reshape(1, DT),
             talk_proj,
             talk_router,
             talk_gate_up,
             talk_down,
         ),
-        "vvvhhhh",
-        [
-            pltpu.VMEM((4, 512, DT), BF16),
-            pltpu.VMEM((DT, EXPERTS), BF16),
-            pltpu.VMEM((DT, 2 * FT), BF16),
-            pltpu.VMEM((FT, DT), BF16),
-            dma((7,)),
-        ],
+        "vvvvvvv",
     )
     got = lax.ppermute(give, "exp", [(e, e ^ 1) for e in range(EXP)])
     msg = call(pair_kernel, array((64, 16, 256), BF16), (keep, got), "vv")

time: 120 us -> 99.3 us (0.83)
  blocking collectives: 54.4 us -> 86.3 us
  waiting for transfers between devices: 21.1 us -> 1.16 us
  local copies, waits for them, and re-layouts: 16.3 us -> 0.06 us
  starting transfers between devices: 11.9 us -> 0.09 us
  Pallas kernels: 14.4 us -> 10.6 us
    all_to_all x4 -> x6, blocking collectives: 54.4 us -> 86.3 us  [exchange(): return lax.all_to_all(msg, axis, 0, 0, axis_index_groups=groups)]
    all_to_all x2 -> x0, waiting for transfers between devices: 19.9 us -> none  [exchange(): return lax.all_to_all(msg, axis, 0, 0, axis_index_groups=groups)]
    unnamed x38 -> x26, local copies, waits for them, and re-layouts: 16.3 us -> 0.06 us
    all_to_all x2 -> x0, starting transfers between devices: 11.7 us -> none  [exchange(): return lax.all_to_all(msg, axis, 0, 0, axis_index_groups=groups)]
    pallas_call x8, Pallas kernels: 14.4 us -> 10.6 us  [call(): pl.pallas_call(kernel, out_shape=outs, in_specs=[pl.BlockSpec(memory_spac...]
  transfers between devices with their start and end apart: 3 -> 1, of which waited for: 3 -> 1; matrix products, arithmetic and copies ran while one was open for 0% -> 0% of each run, Pallas kernels for 0% -> 0%
where the time goes in v2:
time: 99.3 us; the launch traced here: 99 us
  blocking collectives  86.3 us (87%)
  Pallas kernels  10.6 us (11%)
  waiting for transfers between devices  1.16 us (1%)
    all_to_all x6, blocking collectives, exchange(): return lax.all_to_all(msg, axis, 0, 0, axis_index_groups=groups)  86.3 us
    pallas_call x8, Pallas kernels, call(): pl.pallas_call(kernel, out_shape=outs, in_specs=[pl.BlockSpec(memory_spac...  10.6 us
  transfers between devices with their start and end apart: 1, of which 1 were waited for; matrix products, arithmetic and copies ran while one was open for 0% of the time, Pallas kernels for 0%

profile of v2, /device:TPU:0, one launch (start us, length us, event | category | flops | bytes accessed | tf_op | source)
XLA Modules:
  0.0 99.0 jit_solution(6628476672770783737)
XLA Ops:
  0.6 0.0 copy-start.3
  0.6 4.5 %shard_map.176 = bf16[8,16,256]{2,1,0:T(8,128)(2,1)} custom-call(s32[4]{0:T(128)} %len_hbm.1, bf16[4,4096]{1,0:T(4,128)(2,1)} %q_hbm.1, bf16[2,4,512]{2,1,0:T(4,128)(2,1)} %new_hbm.1, bf16[2,4,512,512]{3,2,1,0:T(8,128)(2,1)} %kv_hbm.1), custom_call_target="tpu_custom_call" | custom-call | flops 99999997952 | bytes 1048576 | tf_op jit(solution)/shard_map/pallas_call | solution.py:296
  5.2 12.7 %all_to_all.30.recv_ref = bf16[8,16,256]{2,1,0:T(8,128)(2,1)S(1)} all-to-all(bf16[8,16,256]{2,1,0:T(8,128)(2,1)} %shard_map.176), channel_id=1, replica_groups=mesh['seq'=8,'exp'=16] {'seq'}, dimensions={0} | all-to-all | bytes 131072 | tf_op jit(solution)/shard_map/all_to_all | solution.py:312
  17.8 0.0 copy-done.3
  17.8 0.0 copy-start.8
  17.9 0.0 copy-start.9
  17.9 0.6 shard_map.177
  18.5 9.0 %all_to_all.31.recv_ref = bf16[8,16,512]{2,1,0:T(8,128)(2,1)S(1)} all-to-all(bf16[8,16,512]{2,1,0:T(8,128)(2,1)S(1)} %shard_map.177), channel_id=1, replica_groups=mesh['seq'=8,'exp'=16] {'seq'}, dimensions={0} | all-to-all | bytes 262144 | tf_op jit(solution)/shard_map/all_to_all | solution.py:312
  27.5 0.0 copy-done.8
  27.5 0.0 copy-done.9
  27.5 0.0 copy-start
  27.5 0.0 copy-start.2
  27.5 0.0 copy-start.6
  27.5 0.0 copy-start.10
  27.5 0.2 shard_map.178
  27.7 16.4 %all_to_all.32 = bf16[16,16,512]{2,1,0:T(8,128)(2,1)S(1)} all-to-all(bf16[16,16,512]{2,1,0:T(8,128)(2,1)S(1)} %get-tuple-element.8), channel_id=1, replica_groups=mesh['seq'=8,'exp'=16] {'exp'}, dimensions={0} | all-to-all | bytes 524288 | tf_op jit(solution)/shard_map/all_to_all | solution.py:312
  44.1 0.0 copy-done
  44.1 0.0 copy-done.2
  44.1 0.0 copy-done.6
  44.1 0.0 copy-done.10
  44.1 2.0 %shard_map.179 = bf16[128,8,128]{2,1,0:T(8,128)(2,1)S(1)} custom-call(bf16[256,512]{1,0:T(8,128)(2,1)S(1)} %bitcast.7, s32[8,64]{1,0:T(8,128)S(1)} %bitcast.9, bf16[2048,128]{1,0:T(8,128)(2,1)S(1)} %copy-done.6, bf16[1,2048,1536]{2,1,0:T(8,128)(2,1)S(1)} %copy-done, bf16[1,768,2048]{2,1,0:T(8,128)(2,1)S(1)} %copy-done.2), custom_call_target="tpu_custom_call" | custom-call | flops 99999997952 | bytes 1048576 | tf_op jit(solution)/shard_map/pallas_call | solution.py:296
  46.1 14.5 %all_to_all.33.recv_ref = bf16[128,8,128]{2,1,0:T(8,128)(2,1)S(1)} all-to-all(bf16[128,8,128]{2,1,0:T(8,128)(2,1)S(1)} %shard_map.179), channel_id=1, replica_groups=mesh['seq'=8,'exp'=16] {'seq','exp'}, dimensions={0} | all-to-all | bytes 524288 | tf_op jit(solution)/shard_map/all_to_all | solution.py:312
  60.6 0.0 copy-start.1
  60.6 0.0 copy-start.4
  60.6 0.0 copy-start.5
  60.7 0.0 copy-start.7
  60.7 0.0 copy-start.11
  60.7 0.0 copy-start.12
  60.7 0.2 shard_map.180
  60.8 15.4 %all_to_all.34 = bf16[128,8,128]{2,1,0:T(8,128)(2,1)S(1)} all-to-all(bf16[128,8,128]{2,1,0:T(8,128)(2,1)S(1)} %shard_map.180), channel_id=1, replica_groups=mesh['seq'=8,'exp'=16] {'seq','exp'}, dimensions={0} | all-to-all | bytes 524288 | tf_op jit(solution)/shard_map/all_to_all | solution.py:312
  76.2 0.0 copy-done.1
  76.2 0.0 copy-done.4
  76.2 0.0 copy-done.5
  76.2 0.0 copy-done.7
  76.2 0.0 copy-done.11
  76.2 0.0 copy-done.12
  76.3 2.4 %shard_map.181 = (f32[4,2048]{1,0:T(4,128)}, f32[4,1024]{1,0:T(4,128)S(1)}, bf16[8,16,256]{2,1,0:T(8,128)(2,1)S(1)}, bf16[8,16,256]{2,1,0:T(8,128)(2,1)S(1)}) custom-call(bf16[1024,128]{1,0:T(8,128)(2,1)S(1)} %bitcast.6, s32[8,64]{1,0:T(8,128)S(1)} %bitcast.10, f32[1,1024]{1,0:T(1,128)S(1)} %bitcast.11, bf16[2048,1024]{1,0:T(8,128)(2,1)S(1)} %copy-done.1, ...), custom_call_target="tpu_custom_call" | custom-call | flops 99999997952 | bytes 1048576 | tf_op jit(solution)/shard_map/pallas_call | solution.py:296
  78.7 0.1 collective-permute-start
  78.8 1.2 %collective-permute-done.got_ref = bf16[8,16,256]{2,1,0:T(8,128)(2,1)S(1)} collective-permute-done((bf16[8,16,256]{2,1,0:T(8,128)(2,1)S(1)}, bf16[8,16,256]{2,1,0:T(8,128)(2,1)S(1)}, u32[]{:S(2)}, u32[]{:S(2)}) %collective-permute-start) | collective-permute-done | bytes 65568 | tf_op jit(solution)/shard_map/ppermute | solution.py:397
  80.0 18.4 %all_to_all.35.recv_ref = bf16[64,16,256]{2,1,0:T(8,128)(2,1)S(1)} all-to-all(bf16[64,16,256]{2,1,0:T(8,128)(2,1)S(1)} %shard_map.182), channel_id=1, replica_groups={{0,2,4,6,8,10,12,14,16,18,20,22,24,26,28,30,32,34,36,38,40,42,44,46,48,..., dimensions={0} | all-to-all | bytes 1048576 | tf_op jit(solution)/shard_map/all_to_all | solution.py:312
  98.3 0.7 shard_map.183
  (1 shorter events, 0.0 us)
Async XLA Ops:
  0.6 17.2 %copy-start.3 = (bf16[512,2048]{1,0:T(8,128)(2,1)S(1)}, bf16[512,2048]{1,0:T(8,128)(2,1)}, u32[]{:S(2)}) copy-start(bf16[512,2048]{1,0:T(8,128)(2,1)} %proj_ref.2) | copy-start | bytes 6291460
  17.8 9.6 %copy-start.8 = (f32[4,2048]{1,0:T(4,128)S(1)}, f32[4,2048]{1,0:T(4,128)}, u32[]{:S(2)}) copy-start(f32[4,2048]{1,0:T(4,128)} %hidden_ref.1) | copy-start | bytes 98308
  17.9 9.6 %copy-start.9 = (f32[2048]{0:T(1024)S(1)}, f32[2048]{0:T(1024)}, u32[]{:S(2)}) copy-start(f32[2048]{0:T(1024)} %param.23) | copy-start | bytes 24580
  27.5 16.6 %copy-start = (bf16[1,2048,1536]{2,1,0:T(8,128)(2,1)S(1)}, bf16[1,2048,1536]{2,1,0:T(8,128)(2,1)}, u32[]{:S(2)}) copy-start(bf16[1,2048,1536]{2,1,0:T(8,128)(2,1)} %up_ref.2) | copy-start | bytes 18874372
  27.5 16.6 %copy-start.2 = (bf16[1,768,2048]{2,1,0:T(8,128)(2,1)S(1)}, bf16[1,768,2048]{2,1,0:T(8,128)(2,1)}, u32[]{:S(2)}) copy-start(bf16[1,768,2048]{2,1,0:T(8,128)(2,1)} %down_ref.2) | copy-start | bytes 9437188
  27.5 16.6 %copy-start.6 = (bf16[2048,128]{1,0:T(8,128)(2,1)S(1)}, bf16[2048,128]{1,0:T(8,128)(2,1)}, u32[]{:S(2)}) copy-start(bf16[2048,128]{1,0:T(8,128)(2,1)} %router_ref.2) | copy-start | bytes 1572868
  27.5 16.6 %copy-start.10 = (s32[64,8]{0,1:T(8,128)S(1)}, s32[64,8]{0,1:T(8,128)}, u32[]{:S(2)}) copy-start(s32[64,8]{0,1:T(8,128)} %param.25) | copy-start | bytes 6148
  60.6 15.6 %copy-start.1 = (bf16[2048,1024]{1,0:T(8,128)(2,1)S(1)}, bf16[2048,1024]{1,0:T(8,128)(2,1)}, u32[]{:S(2)}) copy-start(bf16[2048,1024]{1,0:T(8,128)(2,1)} %proj_ref.3) | copy-start | bytes 12582916
  60.6 15.6 %copy-start.4 = (bf16[1,1024,768]{2,1,0:T(8,128)(2,1)S(1)}, bf16[1,1024,768]{2,1,0:T(8,128)(2,1)}, u32[]{:S(2)}) copy-start(bf16[1,1024,768]{2,1,0:T(8,128)(2,1)} %up_ref.3) | copy-start | bytes 4718596
  60.6 15.6 %copy-start.5 = (bf16[1,384,1024]{2,1,0:T(8,128)(2,1)S(1)}, bf16[1,384,1024]{2,1,0:T(8,128)(2,1)}, u32[]{:S(2)}) copy-start(bf16[1,384,1024]{2,1,0:T(8,128)(2,1)} %down_ref.3) | copy-start | bytes 2359300
  60.7 15.6 %copy-start.7 = (bf16[1024,128]{1,0:T(8,128)(2,1)S(1)}, bf16[1024,128]{1,0:T(8,128)(2,1)}, u32[]{:S(2)}) copy-start(bf16[1024,128]{1,0:T(8,128)(2,1)} %router_ref.3) | copy-start | bytes 786436
  60.7 15.6 %copy-start.11 = (s32[64,8]{0,1:T(8,128)S(1)}, s32[64,8]{0,1:T(8,128)}, u32[]{:S(2)}) copy-start(s32[64,8]{0,1:T(8,128)} %param.31) | copy-start | bytes 6148
  60.7 15.6 %copy-start.12 = (f32[1024]{0:T(1024)S(1)}, f32[1024]{0:T(1024)}, u32[]{:S(2)}) copy-start(f32[1024]{0:T(1024)} %param.29) | copy-start | bytes 12292
  78.7 1.3 %collective-permute-start = (bf16[8,16,256]{2,1,0:T(8,128)(2,1)S(1)}, bf16[8,16,256]{2,1,0:T(8,128)(2,1)S(1)}, u32[]{:S(2)}, u32[]{:S(2)}) collective-permute-start(bf16[8,16,256]{2,1,0:T(8,128)(2,1)S(1)} %get-tuple-element.12), channel_id=1, source_target_pairs={{0,1},{1,0},{2,3},{3,2},{4,5},{5,4},{6,7},{7,6},{8,9},{9,8},{10,11... | collective-permute-start | bytes 196616 | tf_op jit(solution)/shard_map/ppermute | solution.py:397

commit v3 on v2

--- a/solution.py
+++ b/solution.py
@@ -115,49 +115,96 @@
 
 
 def attend_kernel(
-    len_hbm, q_hbm, new_hbm, kv_hbm, out_ref, len_ref, q_ref, new_ref, kv_ref, q_buf, o_buf, t_buf, sems
+    len_hbm,
+    q_hbm,
+    new_hbm,
+    ids_hbm,
+    talk_hbm,
+    kv_hbm,
+    out_ref,
+    chosen_ref,
+    wanted_ref,
+    picks_ref,
+    place_ref,
+    keep_ref,
+    give_ref,
+    len_ref,
+    q_ref,
+    new_ref,
+    ids_ref,
+    talk_ref,
+    kv_ref,
+    q_buf,
+    o_buf,
+    t_buf,
+    sems,
 ):
-    pairs = [(q_hbm, q_ref), (new_hbm, new_ref), (len_hbm, len_ref)]
-    for c in range(OWN):
-        pairs += [(kv_hbm.at[t, c], kv_ref.at[t, c]) for t in range(2)]
+    pairs = [(q_hbm, q_ref), (ids_hbm, ids_ref), (talk_hbm, talk_ref), (new_hbm, new_ref), (len_hbm, len_ref)]
+    pairs += [(kv_hbm.at[t, c], kv_ref.at[t, c]) for t in range(2) for c in range(OWN)]
     copies = start_all(pairs, sems)
-    for copy in copies[:3]:
+    small, keys, values = copies[:5], copies[5 : 5 + OWN], copies[5 + OWN :]
+    for copy in small:
         copy.wait()
     seq = lax.axis_index("seq")
     scale = HD ** (-0.5)
     query = q_ref[...].astype(F32)
     for h in range(HEADS):
         q_buf[4 * h : 4 * h + 4, :] = query[:, HD * h : HD * h + HD]
+
+    me = my_expert()
+    group = lax.axis_index("exp")
+    core = group & 1
+    slots = slots_by_row(ids_ref[...], me)
+    chosen_ref[...] = by_chunk(dot(slots, spread_marks(256, 2)), 4).astype(BF16)
+    picks_ref[0] = pick_marks(slots, ids_ref[...])
+    place_ref[...] = placing(slots, 128, 1)
+    slots = slots_by_row(talk_ref[...], me)
+    picks_ref[1] = pick_marks(slots, talk_ref[...])
+    keep_ref[...] = placing(slots, 128, 2, core)
+    give_ref[...] = placing(slots, 128, 2, 1 - core)
+    slot = iota((8, ROWS), 0)
+    own = jnp.logical_and(iota((8, ROWS), 1) == OWN * group + slot, slot < OWN)
+    wanted = jnp.concatenate([slots, jnp.where(own, 1.0, 0.0)], axis=0)
+    wanted_ref[...] = by_chunk(dot(wanted, spread_marks(128, 1)), 2).astype(BF16)
+
     lane = iota((HEADS, KVH * HD), 1)
     diag = (iota((HEADS, KVH * HD), 0) >> 3) == (lane >> 7)
     place = lane + seq * SPAN
     tail_lane = iota((HEADS, HD), 1)
+    parts = []
     for c in range(OWN):
         q = q_buf[pl.ds(c, HEADS, stride=4), :]
         wide = jnp.where(diag, jnp.concatenate([q] * KVH, axis=1), 0.0)
         fresh_key = new_ref[0, c : c + 1, :].astype(F32)
-        fresh_value = new_ref[1, c : c + 1, :].astype(F32)
         fresh = jnp.sum(wide * fresh_key, axis=1, keepdims=True) * scale
-        fresh = jnp.where(seq == 0, fresh, NEG)
-        copies[2 * c + 3].wait()
-        scores = dot_t(wide.astype(BF16), kv_ref[0, c]) * scale
+        parts.append((wide.astype(BF16), jnp.where(seq == 0, fresh, NEG)))
+    for copy in keys:
+        copy.wait()
+    done = []
+    for c in range(OWN):
+        wide, fresh = parts[c]
         valid = place < len_ref[c]
-        scores = jnp.where(valid, scores, NEG)
+        scores = jnp.where(valid, dot_t(wide, kv_ref[0, c]) * scale, NEG)
         peak = jnp.maximum(jnp.max(scores, axis=1, keepdims=True), fresh)
         peak = peak.astype(BF16).astype(F32)
         weights = jnp.where(valid, jnp.exp(scores - peak), 0.0).astype(BF16)
         fresh_weight = jnp.where(seq == 0, jnp.exp(fresh - peak), 0.0)
         total = jnp.sum(weights.astype(F32), axis=1, keepdims=True) + fresh_weight
-        copies[2 * c + 4].wait()
+        upper = total.astype(BF16).astype(F32)
+        tail = jnp.where(tail_lane == 0, peak, jnp.where(tail_lane == 1, upper, total - upper))
+        t_buf[pl.ds(c, HEADS, stride=4), :] = tail
+        done.append((weights, fresh_weight))
+    for copy in values:
+        copy.wait()
+    for c in range(OWN):
+        weights, fresh_weight = done[c]
+        fresh_value = new_ref[1, c : c + 1, :].astype(F32)
         mixed = dot(weights, kv_ref[1, c]) + fresh_weight * fresh_value
         mixed = jnp.where(diag, mixed, 0.0)
         mixed = (mixed[:, :HD] + mixed[:, HD : 2 * HD]) + (
             mixed[:, 2 * HD : 3 * HD] + mixed[:, 3 * HD :]
         )
-        upper = total.astype(BF16).astype(F32)
-        tail = jnp.where(tail_lane == 0, peak, jnp.where(tail_lane == 1, upper, total - upper))
         o_buf[pl.ds(c, HEADS, stride=4), :] = mixed
-        t_buf[pl.ds(c, HEADS, stride=4), :] = tail
     out_ref[:, :, :HD] = o_buf[...].reshape(SEQ, 16, HD).astype(BF16)
     out_ref[:, :, HD:] = t_buf[...].reshape(SEQ, 16, HD).astype(BF16)
 
@@ -197,16 +244,11 @@
             state_ref[s, 4 * k : 4 * k + 4, :] = buf[4 * (s // 2) : 4 * (s // 2) + 4, first : first + 128]
 
 
-def expert_kernel(recv_ref, ids_ref, router_ref, up_ref, down_ref, out_ref):
+def expert_kernel(recv_ref, chosen_ref, picks_ref, place_ref, router_ref, up_ref, down_ref, out_ref):
     me = my_expert()
-    ids = ids_ref[...]
-    slots = slots_by_row(ids, me)
-    picks = pick_marks(slots, ids)
-    place = placing(slots, 128, 1)
-    chosen = by_chunk(dot(slots, spread_marks(256, 2)), 4).astype(BF16)
-    rows = dot(chosen, recv_ref[...])
+    rows = dot(chosen_ref[...], recv_ref[...])
     rows = jnp.concatenate([rows[8 * j : 8 * j + 8] for j in range(4)], axis=1).astype(BF16)
-    gates = gates_of(dot(rows, router_ref[...]), picks, me)
+    gates = gates_of(dot(rows, router_ref[...]), picks_ref[0], me)
     both = dot(rows, up_ref[0])
     inner = (silu(both[:, :FF]) * both[:, FF:]).astype(BF16)
     reply = dot(inner, down_ref[0])
@@ -217,7 +259,7 @@
         )
         for k in range(2)
     ]
-    sent = dot(place, jnp.concatenate(halves, axis=0).astype(BF16))
+    sent = dot(place_ref[...], jnp.concatenate(halves, axis=0).astype(BF16))
     for s in range(SEQ):
         block = sent[:, 128 * s : 128 * s + 128].reshape(EXP, 8, 128)
         out_ref[EXP * s : EXP * s + EXP] = block.astype(BF16)
@@ -230,7 +272,10 @@
 
 def talker_kernel(
     recv_ref,
-    ids_ref,
+    wanted_ref,
+    picks_ref,
+    keep_place_ref,
+    give_place_ref,
     gain_ref,
     proj_ref,
     router_ref,
@@ -240,40 +285,37 @@
     talk_ref,
     keep_ref,
     give_ref,
+    row_buf,
+    sem,
 ):
     me = my_expert()
-    group = lax.axis_index("exp")
-    core = group & 1
-    ids = ids_ref[...]
-    slots = slots_by_row(ids, me)
-    picks = pick_marks(slots, ids)
-    keep_place = placing(slots, 128, 2, core)
-    give_place = placing(slots, 128, 2, 1 - core)
-    slot = iota((8, ROWS), 0)
-    own = jnp.logical_and(iota((8, ROWS), 1) == OWN * group + slot, slot < OWN)
-    wanted = jnp.concatenate([slots, jnp.where(own, 1.0, 0.0)], axis=0)
-    chosen = by_chunk(dot(wanted, spread_marks(128, 1)), 2).astype(BF16)
-    talk_in = jnp.zeros((16, DT), F32)
+    chosen = wanted_ref[...]
+    parts = []
     for q in range(4):
         cols = []
         for s in (2 * q, 2 * q + 1):
             got = dot(chosen, recv_ref[128 * s : 128 * s + 128, :])
             cols += [got[:16], got[16:]]
-        part = jnp.concatenate(cols, axis=1)
-        thinker_ref[:, 512 * q : 512 * q + 512] = part[8 : 8 + OWN]
-        talk_in = talk_in + dot(part.astype(BF16), proj_ref[512 * q : 512 * q + 512, :])
+        parts.append(jnp.concatenate(cols, axis=1))
+        row_buf[:, 512 * q : 512 * q + 512] = parts[q][8 : 8 + OWN]
+    out = pltpu.make_async_copy(row_buf, thinker_ref, sem)
+    out.start()
+    talk_in = jnp.zeros((16, DT), F32)
+    for q in range(4):
+        talk_in = talk_in + dot(parts[q].astype(BF16), proj_ref[512 * q : 512 * q + 512, :])
     talk_ref[...] = talk_in[8 : 8 + OWN]
     talk_in = talk_in[:8]
     mean = jnp.mean(talk_in * talk_in, axis=1, keepdims=True)
     normed = (talk_in * lax.rsqrt(mean + EPS) * gain_ref[...]).astype(BF16)
-    gates = gates_of(dot(normed, router_ref[...]), picks, me)
+    gates = gates_of(dot(normed, router_ref[...]), picks_ref[1], me)
     both = dot(normed, up_ref[0])
     inner = (silu(both[:, :FT]) * both[:, FT:]).astype(BF16)
     reply = gates * dot(inner, down_ref[0]).astype(BF16).astype(F32)
     stacked = jnp.concatenate([reply[:, 256 * j : 256 * j + 256] for j in range(4)], axis=0)
     stacked = stacked.astype(BF16)
-    keep_ref[...] = dot(keep_place, stacked).reshape(8, 16, 256).astype(BF16)
-    give_ref[...] = dot(give_place, stacked).reshape(8, 16, 256).astype(BF16)
+    keep_ref[...] = dot(keep_place_ref[...], stacked).reshape(8, 16, 256).astype(BF16)
+    give_ref[...] = dot(give_place_ref[...], stacked).reshape(8, 16, 256).astype(BF16)
+    out.wait()
 
 
 def pair_kernel(keep_ref, got_ref, out_ref):
@@ -289,7 +331,7 @@
         out_ref[:, cols] = talk_ref[:, cols] + buf[4 * j : 4 * j + 4, :]
 
 
-def call(kernel, outs, args, where, scratch=(), mib=16, flops=COST):
+def call(kernel, outs, args, where, scratch=(), mib=16, flops=COST, outs_at=None):
     spaces = {"v": pltpu.VMEM, "s": pltpu.SMEM, "h": pltpu.HBM}
     many = isinstance(outs, list)
     whole = pl.BlockSpec(memory_space=pltpu.VMEM)
@@ -297,7 +339,7 @@
         kernel,
         out_shape=outs,
         in_specs=[pl.BlockSpec(memory_space=spaces[w]) for w in where],
-        out_specs=[whole] * len(outs) if many else whole,
+        out_specs=[pl.BlockSpec(memory_space=spaces[w]) for w in outs_at or "v" * len(outs)] if many else whole,
         scratch_shapes=list(scratch),
         cost_estimate=pl.CostEstimate(flops=flops, bytes_accessed=1 << 20, transcendentals=0),
         compiler_params=pltpu.CompilerParams(vmem_limit_bytes=mib << 20),
@@ -332,22 +374,32 @@
     talk_down,
 ):
     both = ("seq", "exp")
-    msg = call(
+    held = (lengths, queries, new_kv, expert_ids.T, talk_ids.T, kv_cache)
+    msg, chosen, wanted, picks, place, keep_place, give_place = call(
         attend_kernel,
-        array((SEQ, 16, 256), BF16),
-        (lengths, queries, new_kv, kv_cache),
-        "hhhh",
+        [
+            array((SEQ, 16, 256), BF16),
+            array((32, 256), BF16),
+            array((32, 128), BF16),
+            array((2, 8, EXPERTS), F32),
+            array((128, 16), BF16),
+            array((128, 32), BF16),
+            array((128, 32), BF16),
+        ],
+        tuple(pltpu.with_memory_space_constraint(x, pltpu.HBM) for x in held),
+        "hhhhhh",
         [
             pltpu.SMEM((OWN,), jnp.int32),
             pltpu.VMEM((OWN, HEADS * HD), BF16),
             pltpu.VMEM((2, OWN, KVH * HD), BF16),
+            pltpu.VMEM((8, ROWS), jnp.int32),
+            pltpu.VMEM((8, ROWS), jnp.int32),
             pltpu.VMEM((2, OWN, SPAN, KVH * HD), BF16),
             pltpu.VMEM((HEADS * OWN, HD), F32),
             pltpu.VMEM((HEADS * OWN, HD), F32),
             pltpu.VMEM((HEADS * OWN, HD), F32),
-            pltpu.SemaphoreType.DMA((3 + 2 * OWN,)),
+            pltpu.SemaphoreType.DMA((5 + 2 * OWN,)),
         ],
-        mib=60,
     )
     msg = call(
         project_kernel,
@@ -366,8 +418,8 @@
     msg = call(
         expert_kernel,
         array((SEQ * EXP, 8, 128), BF16),
-        (exchange(msg, "exp").reshape(256, 512), expert_ids.T, router, w_gate_up, w_down),
-        "vvvvv",
+        (exchange(msg, "exp").reshape(256, 512), chosen, picks, place, router, w_gate_up, w_down),
+        "vvvvvvv",
     )
     msg = call(
         total_kernel,
@@ -385,14 +437,19 @@
         ],
         (
             exchange(msg, both).reshape(1024, 128),
-            talk_ids.T,
+            wanted,
+            picks,
+            keep_place,
+            give_place,
             talk_gain.reshape(1, DT),
             talk_proj,
             talk_router,
             talk_gate_up,
             talk_down,
         ),
-        "vvvvvvv",
+        "vvvvvvvvvv",
+        [pltpu.VMEM((OWN, D), F32), pltpu.SemaphoreType.DMA],
+        outs_at="hvvv",
     )
     got = lax.ppermute(give, "exp", [(e, e ^ 1) for e in range(EXP)])
     msg = call(pair_kernel, array((64, 16, 256), BF16), (keep, got), "vv")

time: 99.3 us -> 96.8 us (0.975)
  Pallas kernels: 10.6 us -> 8.37 us
    pallas_call x8, Pallas kernels: 10.6 us -> 8.37 us  [call(): pl.pallas_call(kernel, out_shape=outs, in_specs=[pl.BlockSpec(memory_spac...]
where the time goes in v3:
time: 96.8 us; the launch traced here: 96.6 us
  blocking collectives  86.1 us (89%)
  Pallas kernels  8.37 us (9%)
  waiting for transfers between devices  1.16 us (1%)
    all_to_all x6, blocking collectives, exchange(): return lax.all_to_all(msg, axis, 0, 0, axis_index_groups=groups)  86.1 us
    pallas_call x8, Pallas kernels, call(): pl.pallas_call(kernel, out_shape=outs, in_specs=[pl.BlockSpec(memory_spac...  8.37 us
  transfers between devices with their start and end apart: 1, of which 1 were waited for; matrix products, arithmetic and copies ran while one was open for 0% of the time, Pallas kernels for 0%

profile of v3, /device:TPU:0, one launch (start us, length us, event | category | flops | bytes accessed | tf_op | source)
XLA Modules:
  0.0 96.6 jit_solution(8119594908822340627)
XLA Ops:
  0.6 0.0 copy-start.3
  0.6 3.2 %shard_map.176 = (bf16[8,16,256]{2,1,0:T(8,128)(2,1)S(1)}, bf16[32,256]{1,0:T(8,128)(2,1)S(1)}, bf16[32,128]{1,0:T(8,128)(2,1)S(1)}, f32[2,8,128]{2,1,0:T(8,128)...) custom-call(s32[4]{0:T(128)} %len_hbm.1, bf16[4,4096]{1,0:T(4,128)(2,1)} %q_hbm.1, ...), custom_call_target="tpu_custom_call" | custom-call | flops 99999997952 | bytes 1048576 | tf_op jit(solution)/shard_map/pallas_call | solution.py:338
  3.9 12.5 %all_to_all.30.recv_ref = bf16[8,16,256]{2,1,0:T(8,128)(2,1)S(1)} all-to-all(bf16[8,16,256]{2,1,0:T(8,128)(2,1)S(1)} %get-tuple-element.15), channel_id=1, replica_groups=mesh['seq'=8,'exp'=16] {'seq'}, dimensions={0} | all-to-all | bytes 131072 | tf_op jit(solution)/shard_map/all_to_all | solution.py:354
  16.4 0.0 copy-done.3
  16.4 0.0 copy-start.8
  16.4 0.0 copy-start.9
  16.4 0.6 shard_map.177
  17.0 9.0 %all_to_all.31.recv_ref = bf16[8,16,512]{2,1,0:T(8,128)(2,1)S(1)} all-to-all(bf16[8,16,512]{2,1,0:T(8,128)(2,1)S(1)} %shard_map.177), channel_id=1, replica_groups=mesh['seq'=8,'exp'=16] {'seq'}, dimensions={0} | all-to-all | bytes 262144 | tf_op jit(solution)/shard_map/all_to_all | solution.py:354
  26.0 0.0 copy-done.8
  26.0 0.0 copy-done.9
  26.0 0.0 copy-start
  26.0 0.0 copy-start.2
  26.0 0.0 copy-start.6
  26.0 0.2 shard_map.178
  26.2 16.4 %all_to_all.32 = bf16[16,16,512]{2,1,0:T(8,128)(2,1)S(1)} all-to-all(bf16[16,16,512]{2,1,0:T(8,128)(2,1)S(1)} %get-tuple-element.16), channel_id=1, replica_groups=mesh['seq'=8,'exp'=16] {'exp'}, dimensions={0} | all-to-all | bytes 524288 | tf_op jit(solution)/shard_map/all_to_all | solution.py:354
  42.6 0.0 copy-done
  42.6 0.0 copy-done.2
  42.6 0.0 copy-done.6
  42.6 1.7 %shard_map.179 = bf16[128,8,128]{2,1,0:T(8,128)(2,1)S(1)} custom-call(bf16[256,512]{1,0:T(8,128)(2,1)S(1)} %bitcast.7, bf16[32,256]{1,0:T(8,128)(2,1)S(1)} %get-tuple-element.17.chosen_ref, f32[2,8,128]{2,1,0:T(8,128)S(1)} %get-tuple-element.18.picks_ref, bf16[128,16]{1,0:T(8,128)(2,1)S(1)} %get-tuple-element.19.place_ref, bf16[2048,128]{1,0:T(8,128)(2,1)S(1)} %copy-done.6, ...), custom_call_target="tpu_custom_call" | custom-call | flops 99999997952 | bytes 1048576 | tf_op jit(solution)/shard_map/pallas_call | solution.py:338
  44.4 14.5 %all_to_all.33.recv_ref = bf16[128,8,128]{2,1,0:T(8,128)(2,1)S(1)} all-to-all(bf16[128,8,128]{2,1,0:T(8,128)(2,1)S(1)} %shard_map.179), channel_id=1, replica_groups=mesh['seq'=8,'exp'=16] {'seq','exp'}, dimensions={0} | all-to-all | bytes 524288 | tf_op jit(solution)/shard_map/all_to_all | solution.py:354
  58.9 0.0 copy-start.1
  58.9 0.0 copy-start.4
  58.9 0.0 copy-start.5
  58.9 0.0 copy-start.7
  58.9 0.0 copy-start.10
  58.9 0.2 shard_map.180
  59.1 15.4 %all_to_all.34 = bf16[128,8,128]{2,1,0:T(8,128)(2,1)S(1)} all-to-all(bf16[128,8,128]{2,1,0:T(8,128)(2,1)S(1)} %shard_map.180), channel_id=1, replica_groups=mesh['seq'=8,'exp'=16] {'seq','exp'}, dimensions={0} | all-to-all | bytes 524288 | tf_op jit(solution)/shard_map/all_to_all | solution.py:354
  74.5 0.0 copy-done.1
  74.5 0.0 copy-done.4
  74.5 0.0 copy-done.5
  74.5 0.0 copy-done.7
  74.5 0.0 copy-done.10
  74.5 1.7 %shard_map.181 = (f32[4,2048]{1,0:T(4,128)}, f32[4,1024]{1,0:T(4,128)S(1)}, bf16[8,16,256]{2,1,0:T(8,128)(2,1)S(1)}, bf16[8,16,256]{2,1,0:T(8,128)(2,1)S(1)}) custom-call(bf16[1024,128]{1,0:T(8,128)(2,1)S(1)} %bitcast.6, bf16[32,128]{1,0:T(8,128)(2,1)S(1)} %get-tuple-element.21.wanted_ref, f32[2,8,128]{2,1,0:T(8,128)S(1)} %get-tuple-element.18.picks_ref, ...), custom_call_target="tpu_custom_call" | custom-call | flops 99999997952 | bytes 1048576 | tf_op jit(solution)/shard_map/pallas_call | solution.py:338
  76.2 0.2 collective-permute-start
  76.3 1.2 %collective-permute-done.got_ref = bf16[8,16,256]{2,1,0:T(8,128)(2,1)S(1)} collective-permute-done((bf16[8,16,256]{2,1,0:T(8,128)(2,1)S(1)}, bf16[8,16,256]{2,1,0:T(8,128)(2,1)S(1)}, u32[]{:S(2)}, u32[]{:S(2)}) %collective-permute-start) | collective-permute-done | bytes 65568 | tf_op jit(solution)/shard_map/ppermute | solution.py:454
  77.5 18.4 %all_to_all.35.recv_ref = bf16[64,16,256]{2,1,0:T(8,128)(2,1)S(1)} all-to-all(bf16[64,16,256]{2,1,0:T(8,128)(2,1)S(1)} %shard_map.182), channel_id=1, replica_groups={{0,2,4,6,8,10,12,14,16,18,20,22,24,26,28,30,32,34,36,38,40,42,44,46,48,..., dimensions={0} | all-to-all | bytes 1048576 | tf_op jit(solution)/shard_map/all_to_all | solution.py:354
  95.9 0.7 shard_map.183
  (1 shorter events, 0.0 us)
Async XLA Ops:
  0.6 15.7 %copy-start.3 = (bf16[512,2048]{1,0:T(8,128)(2,1)S(1)}, bf16[512,2048]{1,0:T(8,128)(2,1)}, u32[]{:S(2)}) copy-start(bf16[512,2048]{1,0:T(8,128)(2,1)} %proj_ref.2) | copy-start | bytes 6291460
  16.4 9.6 %copy-start.8 = (f32[4,2048]{1,0:T(4,128)S(1)}, f32[4,2048]{1,0:T(4,128)}, u32[]{:S(2)}) copy-start(f32[4,2048]{1,0:T(4,128)} %hidden_ref.1) | copy-start | bytes 98308
  16.4 9.6 %copy-start.9 = (f32[2048]{0:T(1024)S(1)}, f32[2048]{0:T(1024)}, u32[]{:S(2)}) copy-start(f32[2048]{0:T(1024)} %param.23) | copy-start | bytes 24580
  26.0 16.6 %copy-start = (bf16[1,2048,1536]{2,1,0:T(8,128)(2,1)S(1)}, bf16[1,2048,1536]{2,1,0:T(8,128)(2,1)}, u32[]{:S(2)}) copy-start(bf16[1,2048,1536]{2,1,0:T(8,128)(2,1)} %up_ref.2) | copy-start | bytes 18874372
  26.0 16.6 %copy-start.2 = (bf16[1,768,2048]{2,1,0:T(8,128)(2,1)S(1)}, bf16[1,768,2048]{2,1,0:T(8,128)(2,1)}, u32[]{:S(2)}) copy-start(bf16[1,768,2048]{2,1,0:T(8,128)(2,1)} %down_ref.2) | copy-start | bytes 9437188
  26.0 16.6 %copy-start.6 = (bf16[2048,128]{1,0:T(8,128)(2,1)S(1)}, bf16[2048,128]{1,0:T(8,128)(2,1)}, u32[]{:S(2)}) copy-start(bf16[2048,128]{1,0:T(8,128)(2,1)} %router_ref.2) | copy-start | bytes 1572868
  58.9 15.6 %copy-start.1 = (bf16[2048,1024]{1,0:T(8,128)(2,1)S(1)}, bf16[2048,1024]{1,0:T(8,128)(2,1)}, u32[]{:S(2)}) copy-start(bf16[2048,1024]{1,0:T(8,128)(2,1)} %proj_ref.3) | copy-start | bytes 12582916
  58.9 15.6 %copy-start.4 = (bf16[1,1024,768]{2,1,0:T(8,128)(2,1)S(1)}, bf16[1,1024,768]{2,1,0:T(8,128)(2,1)}, u32[]{:S(2)}) copy-start(bf16[1,1024,768]{2,1,0:T(8,128)(2,1)} %up_ref.3) | copy-start | bytes 4718596
  58.9 15.6 %copy-start.5 = (bf16[1,384,1024]{2,1,0:T(8,128)(2,1)S(1)}, bf16[1,384,1024]{2,1,0:T(8,128)(2,1)}, u32[]{:S(2)}) copy-start(bf16[1,384,1024]{2,1,0:T(8,128)(2,1)} %down_ref.3) | copy-start | bytes 2359300
  58.9 15.6 %copy-start.7 = (bf16[1024,128]{1,0:T(8,128)(2,1)S(1)}, bf16[1024,128]{1,0:T(8,128)(2,1)}, u32[]{:S(2)}) copy-start(bf16[1024,128]{1,0:T(8,128)(2,1)} %router_ref.3) | copy-start | bytes 786436
  58.9 15.6 %copy-start.10 = (f32[1024]{0:T(1024)S(1)}, f32[1024]{0:T(1024)}, u32[]{:S(2)}) copy-start(f32[1024]{0:T(1024)} %param.29) | copy-start | bytes 12292
  76.2 1.3 %collective-permute-start = (bf16[8,16,256]{2,1,0:T(8,128)(2,1)S(1)}, bf16[8,16,256]{2,1,0:T(8,128)(2,1)S(1)}, u32[]{:S(2)}, u32[]{:S(2)}) collective-permute-start(bf16[8,16,256]{2,1,0:T(8,128)(2,1)S(1)} %get-tuple-element.26), channel_id=1, source_target_pairs={{0,1},{1,0},{2,3},{3,2},{4,5},{5,4},{6,7},{7,6},{8,9},{9,8},{10,11... | collective-permute-start | bytes 196616 | tf_op jit(solution)/shard_map/ppermute | solution.py:454

commit v4 on v3

--- a/solution.py
+++ b/solution.py
@@ -51,6 +51,16 @@
     return jnp.where(hit, 1.0, 0.0)
 
 
+def slots_of(ids, experts, slot):
+    match = jnp.zeros(experts.shape, F32)
+    for k in range(ids.shape[0]):
+        match = match + (ids[k : k + 1, :] == experts).astype(F32)
+    before = (iota((ROWS, ROWS), 0) < iota((ROWS, ROWS), 1)).astype(F32)
+    rank = dot(match, before)
+    hit = jnp.logical_and(rank == slot.astype(F32), match > 0.5)
+    return jnp.where(hit, 1.0, 0.0)
+
+
 def spread_marks(count, bits, group=None):
     r = iota((ROWS, count), 0)
     i = iota((ROWS, count), 1)
@@ -123,11 +133,13 @@
     kv_hbm,
     out_ref,
     chosen_ref,
-    wanted_ref,
     picks_ref,
-    place_ref,
+    sums_ref,
+    carry_ref,
+    state_ref,
     keep_ref,
     give_ref,
+    first_ref,
     len_ref,
     q_ref,
     new_ref,
@@ -154,18 +166,28 @@
     me = my_expert()
     group = lax.axis_index("exp")
     core = group & 1
-    slots = slots_by_row(ids_ref[...], me)
+    ids = ids_ref[...]
+    talk_ids = talk_ref[...]
+    slots = slots_by_row(ids, me)
     chosen_ref[...] = by_chunk(dot(slots, spread_marks(256, 2)), 4).astype(BF16)
-    picks_ref[0] = pick_marks(slots, ids_ref[...])
-    place_ref[...] = placing(slots, 128, 1)
-    slots = slots_by_row(talk_ref[...], me)
-    picks_ref[1] = pick_marks(slots, talk_ref[...])
-    keep_ref[...] = placing(slots, 128, 2, core)
-    give_ref[...] = placing(slots, 128, 2, 1 - core)
-    slot = iota((8, ROWS), 0)
-    own = jnp.logical_and(iota((8, ROWS), 1) == OWN * group + slot, slot < OWN)
-    wanted = jnp.concatenate([slots, jnp.where(own, 1.0, 0.0)], axis=0)
-    wanted_ref[...] = by_chunk(dot(wanted, spread_marks(128, 1)), 2).astype(BF16)
+    picks_ref[0] = pick_marks(slots, ids)
+    slots = slots_by_row(talk_ids, me)
+    picks_ref[1] = pick_marks(slots, talk_ids)
+    keep_ref[...] = placing(slots, 256, 3, core)
+    give_ref[...] = placing(slots, 256, 3, 1 - core)
+    first_ref[...] = dot_t(slots, jnp.broadcast_to((talk_ids[0:1, :] == me).astype(F32), (128, ROWS)))
+    line = iota((128, ROWS), 0)
+    came = slots_of(ids, (line >> 4) * EXP + group, line & 7)
+    needed = slots_of(talk_ids, seq * EXP + (line >> 3), line & 7)
+    half = (iota((128, 128), 1) >> 3) & 1
+    sums = dot_t(needed, came)
+    sums_ref[0] = jnp.where(half == 0, sums, 0.0).astype(BF16)
+    sums_ref[1] = jnp.where(half == 1, sums, 0.0).astype(BF16)
+    carry = dot_t(spread_marks_t(128, 1), came)
+    carry_ref[...] = jnp.where(half == 1, carry, 0.0).astype(BF16)
+    lane = iota((ROWS, 16), 1) - 8
+    mine = jnp.logical_and(iota((ROWS, 16), 0) == OWN * group + lane, (lane >= 0) & (lane < OWN))
+    state_ref[...] = dot(needed, jnp.where(mine, 1.0, 0.0)).astype(BF16)
 
     lane = iota((HEADS, KVH * HD), 1)
     diag = (iota((HEADS, KVH * HD), 0) >> 3) == (lane >> 7)
@@ -225,7 +247,7 @@
         out_ref[d] = msg
 
 
-def norm_kernel(recv_ref, hidden_ref, gain_ref, out_ref, state_ref, buf, gain_buf):
+def norm_kernel(recv_ref, hidden_ref, gain_ref, out_ref, state_ref, rows_ref, buf, gain_buf):
     for j in range(4):
         cols = slice(512 * j, 512 * j + 512)
         buf[4 * j : 4 * j + 4, :] = hidden_ref[:, cols]
@@ -238,13 +260,18 @@
     for d in range(EXP):
         out_ref[d] = normed
     buf[...] = state
+    for j in range(4):
+        rows_ref[0:4, 512 * j : 512 * j + 512] = buf[4 * j : 4 * j + 4, :]
+        rows_ref[4:8, 512 * j : 512 * j + 512] = jnp.zeros((4, 512), F32)
     for s in range(SEQ):
         for k in range(2):
             first = (s % 2) * 256 + k * 128
             state_ref[s, 4 * k : 4 * k + 4, :] = buf[4 * (s // 2) : 4 * (s // 2) + 4, first : first + 128]
 
 
-def expert_kernel(recv_ref, chosen_ref, picks_ref, place_ref, router_ref, up_ref, down_ref, out_ref):
+def expert_kernel(
+    recv_ref, chosen_ref, picks_ref, state_ref, router_ref, up_ref, down_ref, proj_ref, out_ref, mixed_ref
+):
     me = my_expert()
     rows = dot(chosen_ref[...], recv_ref[...])
     rows = jnp.concatenate([rows[8 * j : 8 * j + 8] for j in range(4)], axis=1).astype(BF16)
@@ -253,82 +280,83 @@
     inner = (silu(both[:, :FF]) * both[:, FF:]).astype(BF16)
     reply = dot(inner, down_ref[0])
     reply = gates * reply.astype(BF16).astype(F32)
-    halves = [
-        jnp.concatenate(
-            [reply[:, 256 * s + 128 * k : 256 * s + 128 * k + 128] for s in range(SEQ)], axis=1
-        )
-        for k in range(2)
-    ]
-    sent = dot(place_ref[...], jnp.concatenate(halves, axis=0).astype(BF16))
+    stacked = jnp.concatenate([reply, state_ref[...]], axis=0).astype(BF16)
+    mixed = dot(stacked, proj_ref[...])
+    mixed_ref[...] = mixed.astype(BF16)
     for s in range(SEQ):
-        block = sent[:, 128 * s : 128 * s + 128].reshape(EXP, 8, 128)
-        out_ref[EXP * s : EXP * s + EXP] = block.astype(BF16)
-
-
-def total_kernel(recv_ref, state_ref, out_ref):
-    total = jnp.sum(recv_ref[...].astype(F32), axis=0) + state_ref[lax.axis_index("seq")]
-    out_ref[...] = jnp.broadcast_to(total.astype(BF16)[None], out_ref.shape)
+        lower = jnp.concatenate([mixed[:8, 640:], reply[:, 256 * s : 256 * s + 256]], axis=1)
+        out_ref[s] = jnp.concatenate([mixed[:8, :640], lower], axis=0).astype(BF16)
+
+
+def route_kernel(recv_ref, sums_ref, carry_ref, state_mark_ref, mixed_ref, keep_ref, give_ref):
+    upper = dot(sums_ref[0], recv_ref[...])
+    lower = dot(sums_ref[1], recv_ref[:, :384])
+    talk = jnp.concatenate([upper, lower], axis=1) + dot(state_mark_ref[...], mixed_ref[...])
+    thinker = dot(carry_ref[...], recv_ref[:, 384:])
+    odd = ((iota((128, 128), 0) >> 2) & 1) == 1
+    thinker = jnp.where(odd, thinker[:, 128:], thinker[:, :128]).reshape(EXP, 8, 128)
+    top = jnp.concatenate([talk[:, :512].reshape(EXP, 8, 512), thinker], axis=2)
+    rest = jnp.concatenate([talk[:, 512:].reshape(EXP, 8, 512), jnp.zeros_like(thinker)], axis=2)
+    msg = jnp.concatenate([top, rest], axis=1).astype(BF16).reshape(8, 2, 16, 640)
+    first = (lax.axis_index("exp") & 1) == 0
+    keep_ref[...] = jnp.where(first, msg[:, 0], msg[:, 1])
+    give_ref[...] = jnp.where(first, msg[:, 1], msg[:, 0])
+
+
+def join_kernel(keep_ref, got_ref, out_ref):
+    out_ref[...] = (keep_ref[...].astype(F32) + got_ref[...].astype(F32)).astype(BF16)
 
 
 def talker_kernel(
     recv_ref,
-    wanted_ref,
+    state_ref,
     picks_ref,
     keep_place_ref,
     give_place_ref,
+    first_ref,
     gain_ref,
-    proj_ref,
     router_ref,
     up_ref,
     down_ref,
     thinker_ref,
-    talk_ref,
     keep_ref,
     give_ref,
-    row_buf,
-    sem,
 ):
     me = my_expert()
-    chosen = wanted_ref[...]
-    parts = []
-    for q in range(4):
-        cols = []
-        for s in (2 * q, 2 * q + 1):
-            got = dot(chosen, recv_ref[128 * s : 128 * s + 128, :])
-            cols += [got[:16], got[16:]]
-        parts.append(jnp.concatenate(cols, axis=1))
-        row_buf[:, 512 * q : 512 * q + 512] = parts[q][8 : 8 + OWN]
-    out = pltpu.make_async_copy(row_buf, thinker_ref, sem)
-    out.start()
-    talk_in = jnp.zeros((16, DT), F32)
-    for q in range(4):
-        talk_in = talk_in + dot(parts[q].astype(BF16), proj_ref[512 * q : 512 * q + 512, :])
-    talk_ref[...] = talk_in[8 : 8 + OWN]
-    talk_in = talk_in[:8]
+    got = jnp.sum(recv_ref[...].astype(F32), axis=0)
+    thinker_ref[...] = got[:8, 512:] + state_ref[lax.axis_index("seq")]
+    talk_in = jnp.concatenate([got[:8, :512], got[8:, :512]], axis=1)
     mean = jnp.mean(talk_in * talk_in, axis=1, keepdims=True)
     normed = (talk_in * lax.rsqrt(mean + EPS) * gain_ref[...]).astype(BF16)
     gates = gates_of(dot(normed, router_ref[...]), picks_ref[1], me)
     both = dot(normed, up_ref[0])
     inner = (silu(both[:, :FT]) * both[:, FT:]).astype(BF16)
     reply = gates * dot(inner, down_ref[0]).astype(BF16).astype(F32)
-    stacked = jnp.concatenate([reply[:, 256 * j : 256 * j + 256] for j in range(4)], axis=0)
+    reply = reply + first_ref[:, :1] * talk_in
+    stacked = jnp.concatenate([reply[:, 128 * j : 128 * j + 128] for j in range(8)], axis=0)
     stacked = stacked.astype(BF16)
-    keep_ref[...] = dot(keep_place_ref[...], stacked).reshape(8, 16, 256).astype(BF16)
-    give_ref[...] = dot(give_place_ref[...], stacked).reshape(8, 16, 256).astype(BF16)
-    out.wait()
-
-
-def pair_kernel(keep_ref, got_ref, out_ref):
+    keep_ref[...] = dot(keep_place_ref[...], stacked).reshape(8, 32, 128).astype(BF16)
+    give_ref[...] = dot(give_place_ref[...], stacked).reshape(8, 32, 128).astype(BF16)
+
+
+def pair_kernel(keep_ref, got_ref, thinker_ref, out_ref):
     total = (keep_ref[...].astype(F32) + got_ref[...].astype(F32)).astype(BF16)
+    thinker = jnp.broadcast_to(thinker_ref[...].astype(BF16)[None], (8, 8, 128))
     for s in range(SEQ):
-        out_ref[8 * s : 8 * s + 8] = total
-
-
-def finish_kernel(recv_ref, talk_ref, out_ref, buf):
-    buf[...] = jnp.sum(recv_ref[...].astype(F32), axis=0)
-    for j in range(4):
-        cols = slice(256 * j, 256 * j + 256)
-        out_ref[:, cols] = talk_ref[:, cols] + buf[4 * j : 4 * j + 4, :]
+        out_ref[8 * s : 8 * s + 8, :32, :] = total
+        out_ref[8 * s : 8 * s + 8, 32:, :] = thinker
+
+
+def finish_kernel(recv_ref, thinker_ref, out_ref, buf):
+    buf[...] = jnp.sum(recv_ref[:, :32, :].astype(F32), axis=0)
+    for j in range(8):
+        out_ref[:, 128 * j : 128 * j + 128] = buf[4 * j : 4 * j + 4, :]
+    pair = lax.axis_index("exp") >> 1
+    for s in range(SEQ):
+        block = recv_ref[8 * s + pair, 32:, :].astype(F32)
+        for k in range(2):
+            first = 256 * s + 128 * k
+            thinker_ref[:, first : first + 128] = block[4 * k : 4 * k + 4]
 
 
 def call(kernel, outs, args, where, scratch=(), mib=16, flops=COST, outs_at=None):
@@ -348,6 +376,13 @@
 
 def array(shape, dtype):
     return jax.ShapeDtypeStruct(shape, dtype)
+
+
+SIDES = [[2 * i + core for i in range(8)] for core in range(2)]
+
+
+def swap(msg):
+    return lax.ppermute(msg, "exp", [(e, e ^ 1) for e in range(EXP)])
 
 
 def exchange(msg, axis, groups=None):
@@ -375,16 +410,18 @@
 ):
     both = ("seq", "exp")
     held = (lengths, queries, new_kv, expert_ids.T, talk_ids.T, kv_cache)
-    msg, chosen, wanted, picks, place, keep_place, give_place = call(
+    msg, chosen, picks, sums, carry, state_mark, keep_place, give_place, first = call(
         attend_kernel,
         [
             array((SEQ, 16, 256), BF16),
             array((32, 256), BF16),
-            array((32, 128), BF16),
             array((2, 8, EXPERTS), F32),
+            array((2, 128, 128), BF16),
+            array((128, 128), BF16),
             array((128, 16), BF16),
-            array((128, 32), BF16),
-            array((128, 32), BF16),
+            array((256, 64), BF16),
+            array((256, 64), BF16),
+            array((8, 128), F32),
         ],
         tuple(pltpu.with_memory_space_constraint(x, pltpu.HBM) for x in held),
         "hhhhhh",
@@ -408,58 +445,62 @@
         "vv",
         [pltpu.VMEM((16, 512), F32)],
     )
-    msg, state = call(
+    msg, state, state_rows = call(
         norm_kernel,
-        [array((EXP, 16, 512), BF16), array((SEQ, 8, 128), F32)],
+        [array((EXP, 16, 512), BF16), array((SEQ, 8, 128), F32), array((8, D), F32)],
         (exchange(msg, "seq"), hidden_in, norm_gain.reshape(1, D)),
         "vvv",
         [pltpu.VMEM((16, 512), F32), pltpu.VMEM((16, 512), F32)],
     )
-    msg = call(
+    msg, mixed = call(
         expert_kernel,
-        array((SEQ * EXP, 8, 128), BF16),
-        (exchange(msg, "exp").reshape(256, 512), chosen, picks, place, router, w_gate_up, w_down),
-        "vvvvvvv",
-    )
-    msg = call(
-        total_kernel,
-        array((SEQ * EXP, 8, 128), BF16),
-        (exchange(msg, both), state),
-        "vv",
-    )
-    thinker, talk_in, keep, give = call(
+        [array((SEQ, 16, 640), BF16), array((16, DT), BF16)],
+        (
+            exchange(msg, "exp").reshape(256, 512),
+            chosen,
+            picks,
+            state_rows,
+            router,
+            w_gate_up,
+            w_down,
+            talk_proj,
+        ),
+        "vvvvvvvv",
+    )
+    keep, give = call(
+        route_kernel,
+        [array((8, 16, 640), BF16), array((8, 16, 640), BF16)],
+        (exchange(msg, "seq").reshape(128, 640), sums, carry, state_mark, mixed),
+        "vvvvv",
+    )
+    got = swap(give)
+    msg = call(join_kernel, array((8, 16, 640), BF16), (keep, got), "vv")
+    block, keep, give = call(
         talker_kernel,
-        [
-            array((OWN, D), F32),
-            array((OWN, DT), F32),
-            array((8, 16, 256), BF16),
-            array((8, 16, 256), BF16),
-        ],
+        [array((8, 128), F32), array((8, 32, 128), BF16), array((8, 32, 128), BF16)],
         (
-            exchange(msg, both).reshape(1024, 128),
-            wanted,
+            exchange(msg, "exp", SIDES),
+            state,
             picks,
             keep_place,
             give_place,
+            first,
             talk_gain.reshape(1, DT),
-            talk_proj,
             talk_router,
             talk_gate_up,
             talk_down,
         ),
         "vvvvvvvvvv",
-        [pltpu.VMEM((OWN, D), F32), pltpu.SemaphoreType.DMA],
-        outs_at="hvvv",
     )
     got = lax.ppermute(give, "exp", [(e, e ^ 1) for e in range(EXP)])
-    msg = call(pair_kernel, array((64, 16, 256), BF16), (keep, got), "vv")
+    msg = call(pair_kernel, array((64, 40, 128), BF16), (keep, got, block), "vvv")
     same_core = [[2 * i + core for i in range(64)] for core in range(2)]
-    talker = call(
+    thinker, talker = call(
         finish_kernel,
-        array((OWN, DT), F32),
-        (exchange(msg, both, same_core), talk_in),
-        "vv",
-        [pltpu.VMEM((16, 256), F32)],
+        [array((OWN, D), F32), array((OWN, DT), F32)],
+        (exchange(msg, both, same_core),),
+        "v",
+        [pltpu.VMEM((32, 128), F32)],
     )
     return (thinker, talker)
 

time: 96.8 us -> 88.6 us (0.915)
  blocking collectives: 86.1 us -> 76.4 us
  waiting for transfers between devices: 1.16 us -> 2.62 us
    all_to_all x6, blocking collectives: 86.1 us -> 76.4 us  [exchange(): return lax.all_to_all(msg, axis, 0, 0, axis_index_groups=groups)]
    ppermute x0 -> x1, waiting for transfers between devices: none -> 1.38 us  [swap(): return lax.ppermute(msg, 'exp', [(e, e ^ 1) for e in range(EXP)])]
    pallas_call x8 -> x9, Pallas kernels: 8.37 us -> 8.21 us  [call(): pl.pallas_call(kernel, out_shape=outs, in_specs=[pl.BlockSpec(memory_spac...]
  transfers between devices with their start and end apart: 1 -> 2, of which waited for: 1 -> 2; matrix products, arithmetic and copies ran while one was open for 0% -> 0% of each run, Pallas kernels for 0% -> 0%
where the time goes in v4:
time: 88.6 us; the launch traced here: 88.3 us
  blocking collectives  76.4 us (86%)
  Pallas kernels  8.21 us (9%)
  waiting for transfers between devices  2.62 us (3%)
    all_to_all x6, blocking collectives, exchange(): return lax.all_to_all(msg, axis, 0, 0, axis_index_groups=groups)  76.4 us
    pallas_call x9, Pallas kernels, call(): pl.pallas_call(kernel, out_shape=outs, in_specs=[pl.BlockSpec(memory_spac...  8.21 us
  transfers between devices with their start and end apart: 2, of which 2 were waited for; matrix products, arithmetic and copies ran while one was open for 0% of the time, Pallas kernels for 0%

profile of v4, /device:TPU:0, one launch (start us, length us, event | category | flops | bytes accessed | tf_op | source)
XLA Modules:
  0.0 88.3 jit_solution(11235213754875189940)
XLA Ops:
  0.6 0.0 copy-start.3
  0.6 3.2 %shard_map.176 = (bf16[8,16,256]{2,1,0:T(8,128)(2,1)S(1)}, bf16[32,256]{1,0:T(8,128)(2,1)S(1)}, f32[2,8,128]{2,1,0:T(8,128)S(1)}, bf16[2,128,128]{2,1,0:T(8,128)...) custom-call(s32[4]{0:T(128)} %len_hbm.1, ...), custom_call_target="tpu_custom_call" | custom-call | flops 99999997952 | bytes 1048576 | tf_op jit(solution)/shard_map/pallas_call | solution.py:366
  3.9 0.0 copy-start.11
  3.9 12.5 %all_to_all.30.recv_ref = bf16[8,16,256]{2,1,0:T(8,128)(2,1)S(1)} all-to-all(bf16[8,16,256]{2,1,0:T(8,128)(2,1)S(1)} %get-tuple-element.21), channel_id=1, replica_groups=mesh['seq'=8,'exp'=16] {'seq'}, dimensions={0} | all-to-all | bytes 131072 | tf_op jit(solution)/shard_map/all_to_all | solution.py:389
  16.4 0.0 copy-done.3
  16.4 0.0 copy-start.8
  16.4 0.0 copy-start.9
  16.4 0.6 shard_map.177
  17.0 9.0 %all_to_all.31.recv_ref = bf16[8,16,512]{2,1,0:T(8,128)(2,1)S(1)} all-to-all(bf16[8,16,512]{2,1,0:T(8,128)(2,1)S(1)} %shard_map.177), channel_id=1, replica_groups=mesh['seq'=8,'exp'=16] {'seq'}, dimensions={0} | all-to-all | bytes 262144 | tf_op jit(solution)/shard_map/all_to_all | solution.py:389
  26.0 0.0 copy-done.8
  26.0 0.0 copy-done.9
  26.0 0.0 copy-start
  26.0 0.0 copy-start.1
  26.0 0.0 copy-start.2
  26.0 0.0 copy-start.6
  26.0 0.2 shard_map.178
  26.3 16.4 %all_to_all.32 = bf16[16,16,512]{2,1,0:T(8,128)(2,1)S(1)} all-to-all(bf16[16,16,512]{2,1,0:T(8,128)(2,1)S(1)} %get-tuple-element.22), channel_id=1, replica_groups=mesh['seq'=8,'exp'=16] {'exp'}, dimensions={0} | all-to-all | bytes 524288 | tf_op jit(solution)/shard_map/all_to_all | solution.py:389
  42.6 0.0 copy-done.11
  42.6 0.0 copy-done
  42.6 0.0 copy-done.1
  42.6 0.0 copy-done.2
  42.6 0.0 copy-done.6
  42.7 2.1 %shard_map.179 = (bf16[8,16,640]{2,1,0:T(8,128)(2,1)S(1)}, bf16[16,1024]{1,0:T(8,128)(2,1)S(1)}) custom-call(bf16[256,512]{1,0:T(8,128)(2,1)S(1)} %bitcast.6, bf16[32,256]{1,0:T(8,128)(2,1)S(1)} %get-tuple-element.23.chosen_ref, f32[2,8,128]{2,1,0:T(8,128)S(1)} %get-tuple-element.24.picks_ref, f32[8,2048]{1,0:T(8,128)S(1)} %get-tuple-element.25.state_ref, ...), custom_call_target="tpu_custom_call" | custom-call | flops 99999997952 | bytes 1048576 | tf_op jit(solution)/shard_map/pallas_call | solution.py:366
  44.8 9.2 %all_to_all.33 = bf16[8,16,640]{2,1,0:T(8,128)(2,1)S(1)} all-to-all(bf16[8,16,640]{2,1,0:T(8,128)(2,1)S(1)} %get-tuple-element.26), channel_id=1, replica_groups=mesh['seq'=8,'exp'=16] {'seq'}, dimensions={0} | all-to-all | bytes 327680 | tf_op jit(solution)/shard_map/all_to_all | solution.py:389
  53.9 0.3 shard_map.180
  54.3 0.1 collective-permute-start
  54.3 1.4 %collective-permute-done.got_ref = bf16[8,16,640]{2,1,0:T(8,128)(2,1)S(1)} collective-permute-done((bf16[8,16,640]{2,1,0:T(8,128)(2,1)S(1)}, bf16[8,16,640]{2,1,0:T(8,128)(2,1)S(1)}, u32[]{:S(2)}, u32[]{:S(2)}) %collective-permute-start) | collective-permute-done | bytes 163872 | tf_op jit(solution)/shard_map/ppermute | solution.py:385
  55.7 0.0 copy-start.4
  55.7 0.0 copy-start.5
  55.7 0.0 copy-start.7
  55.7 0.0 copy-start.10
  55.7 0.0 copy-start.12
  55.8 10.9 %all_to_all.34.recv_ref = bf16[8,16,640]{2,1,0:T(8,128)(2,1)S(1)} all-to-all(bf16[8,16,640]{2,1,0:T(8,128)(2,1)S(1)} %shard_map.181), channel_id=1, replica_groups={{0,2,4,6,8,10,12,14},{1,3,5,7,9,11,13,15},{16,18,20,22,24,26,28,30},{17..., dimensions={0} | all-to-all | bytes 327680 | tf_op jit(solution)/shard_map/all_to_all | solution.py:389
  66.7 0.0 copy-done.4
  66.7 0.0 copy-done.5
  66.7 0.0 copy-done.7
  66.7 0.0 copy-done.10
  66.7 0.0 copy-done.12
  66.7 0.9 %shard_map.182 = (f32[8,128]{1,0:T(8,128)S(1)}, bf16[8,32,128]{2,1,0:T(8,128)(2,1)S(1)}, bf16[8,32,128]{2,1,0:T(8,128)(2,1)S(1)}) custom-call(bf16[8,16,640]{2,1,0:T(8,128)(2,1)S(1)} %all_to_all.34.recv_ref, f32[8,8,128]{2,1,0:T(8,128)S(1)} %get-tuple-element.33.state_ref, f32[2,8,128]{2,1,0:T(8,128)S(1)} %copy-done.12, ...), custom_call_target="tpu_custom_call" | custom-call | flops 99999997952 | bytes 1048576 | tf_op jit(solution)/shard_map/pallas_call | solution.py:366
  67.6 0.1 collective-permute-start.1
  67.7 1.2 %collective-permute-done.1.got_ref = bf16[8,32,128]{2,1,0:T(8,128)(2,1)S(1)} collective-permute-done((bf16[8,32,128]{2,1,0:T(8,128)(2,1)S(1)}, bf16[8,32,128]{2,1,0:T(8,128)(2,1)S(1)}, u32[]{:S(2)}, u32[]{:S(2)}) %collective-permute-start.1) | collective-permute-done | bytes 65568 | tf_op jit(solution)/shard_map/ppermute | solution.py:495
  68.9 0.1 shard_map.183
  69.0 18.6 %all_to_all.35.recv_ref = bf16[64,40,128]{2,1,0:T(8,128)(2,1)S(1)} all-to-all(bf16[64,40,128]{2,1,0:T(8,128)(2,1)S(1)} %shard_map.183), channel_id=1, replica_groups={{0,2,4,6,8,10,12,14,16,18,20,22,24,26,28,30,32,34,36,38,40,42,44,46,48,..., dimensions={0} | all-to-all | bytes 1310720 | tf_op jit(solution)/shard_map/all_to_all | solution.py:389
  87.6 0.7 shard_map.184
  (1 shorter events, 0.0 us)
Async XLA Ops:
  0.6 15.8 %copy-start.3 = (bf16[512,2048]{1,0:T(8,128)(2,1)S(1)}, bf16[512,2048]{1,0:T(8,128)(2,1)}, u32[]{:S(2)}) copy-start(bf16[512,2048]{1,0:T(8,128)(2,1)} %proj_ref.2) | copy-start | bytes 6291460
  3.9 38.7 %copy-start.11 = (f32[2,8,128]{2,1,0:T(8,128)}, f32[2,8,128]{2,1,0:T(8,128)S(1)}, u32[]{:S(2)}) copy-start(f32[2,8,128]{2,1,0:T(8,128)S(1)} %get-tuple-element.24.picks_ref) | copy-start | bytes 24580
  16.4 9.6 %copy-start.8 = (f32[4,2048]{1,0:T(4,128)S(1)}, f32[4,2048]{1,0:T(4,128)}, u32[]{:S(2)}) copy-start(f32[4,2048]{1,0:T(4,128)} %hidden_ref.1) | copy-start | bytes 98308
  16.4 9.6 %copy-start.9 = (f32[2048]{0:T(1024)S(1)}, f32[2048]{0:T(1024)}, u32[]{:S(2)}) copy-start(f32[2048]{0:T(1024)} %param.23) | copy-start | bytes 24580
  26.0 16.6 %copy-start = (bf16[1,2048,1536]{2,1,0:T(8,128)(2,1)S(1)}, bf16[1,2048,1536]{2,1,0:T(8,128)(2,1)}, u32[]{:S(2)}) copy-start(bf16[1,2048,1536]{2,1,0:T(8,128)(2,1)} %up_ref.2) | copy-start | bytes 18874372
  26.0 16.6 %copy-start.1 = (bf16[2048,1024]{1,0:T(8,128)(2,1)S(1)}, bf16[2048,1024]{1,0:T(8,128)(2,1)}, u32[]{:S(2)}) copy-start(bf16[2048,1024]{1,0:T(8,128)(2,1)} %proj_ref.3) | copy-start | bytes 12582916
  26.0 16.6 %copy-start.2 = (bf16[1,768,2048]{2,1,0:T(8,128)(2,1)S(1)}, bf16[1,768,2048]{2,1,0:T(8,128)(2,1)}, u32[]{:S(2)}) copy-start(bf16[1,768,2048]{2,1,0:T(8,128)(2,1)} %down_ref.2) | copy-start | bytes 9437188
  26.0 16.6 %copy-start.6 = (bf16[2048,128]{1,0:T(8,128)(2,1)S(1)}, bf16[2048,128]{1,0:T(8,128)(2,1)}, u32[]{:S(2)}) copy-start(bf16[2048,128]{1,0:T(8,128)(2,1)} %router_ref.2) | copy-start | bytes 1572868
  54.3 1.5 %collective-permute-start = (bf16[8,16,640]{2,1,0:T(8,128)(2,1)S(1)}, bf16[8,16,640]{2,1,0:T(8,128)(2,1)S(1)}, u32[]{:S(2)}, u32[]{:S(2)}) collective-permute-start(bf16[8,16,640]{2,1,0:T(8,128)(2,1)S(1)} %get-tuple-element.32), channel_id=1, source_target_pairs={{0,1},{1,0},{2,3},{3,2},{4,5},{5,4},{6,7},{7,6},{8,9},{9,8},{10,11... | collective-permute-start | bytes 491528 | tf_op jit(solution)/shard_map/ppermute | solution.py:385
  55.7 10.9 %copy-start.4 = (bf16[1,1024,768]{2,1,0:T(8,128)(2,1)S(1)}, bf16[1,1024,768]{2,1,0:T(8,128)(2,1)}, u32[]{:S(2)}) copy-start(bf16[1,1024,768]{2,1,0:T(8,128)(2,1)} %up_ref.3) | copy-start | bytes 4718596
  55.7 10.9 %copy-start.5 = (bf16[1,384,1024]{2,1,0:T(8,128)(2,1)S(1)}, bf16[1,384,1024]{2,1,0:T(8,128)(2,1)}, u32[]{:S(2)}) copy-start(bf16[1,384,1024]{2,1,0:T(8,128)(2,1)} %down_ref.3) | copy-start | bytes 2359300
  55.7 10.9 %copy-start.7 = (bf16[1024,128]{1,0:T(8,128)(2,1)S(1)}, bf16[1024,128]{1,0:T(8,128)(2,1)}, u32[]{:S(2)}) copy-start(bf16[1024,128]{1,0:T(8,128)(2,1)} %router_ref.3) | copy-start | bytes 786436
  55.7 10.9 %copy-start.10 = (f32[1024]{0:T(1024)S(1)}, f32[1024]{0:T(1024)}, u32[]{:S(2)}) copy-start(f32[1024]{0:T(1024)} %param.29) | copy-start | bytes 12292
  55.7 11.0 %copy-start.12 = (f32[2,8,128]{2,1,0:T(8,128)S(1)}, f32[2,8,128]{2,1,0:T(8,128)}, u32[]{:S(2)}) copy-start(f32[2,8,128]{2,1,0:T(8,128)} %copy-done.11) | copy-start | bytes 24580
  67.6 1.3 %collective-permute-start.1 = (bf16[8,32,128]{2,1,0:T(8,128)(2,1)S(1)}, bf16[8,32,128]{2,1,0:T(8,128)(2,1)S(1)}, u32[]{:S(2)}, u32[]{:S(2)}) collective-permute-start(bf16[8,32,128]{2,1,0:T(8,128)(2,1)S(1)} %get-tuple-element.38), channel_id=1, source_target_pairs={{0,1},{1,0},{2,3},{3,2},{4,5},{5,4},{6,7},{7,6},{8,9},{9,8},{10,11... | collective-permute-start | bytes 196616 | tf_op jit(solution)/shard_map/ppermute | solution.py:495

commit v5 on v4

v5 whole, which is shorter than its diff:
```python
import functools
import jax
import jax.numpy as jnp
from jax import lax
from jax.experimental import pallas as pl
from jax.experimental.pallas import tpu as pltpu
from jax.sharding import PartitionSpec as P

F32 = jnp.float32
BF16 = jnp.bfloat16
HEADS = 32
KVH = 4
HD = 128
D = 2048
DT = 1024
FF = 768
FT = 384
EXPERTS = 128
ROWS = 64
SEQ = 8
EXP = 16
OWN = 4
SPAN = 512
EPS = 1e-6
COST = 10**11
NEG = -1e30


def iota(shape, dim):
    return lax.broadcasted_iota(jnp.int32, shape, dim)


def dot(a, b):
    return jnp.dot(a, b, preferred_element_type=F32)


def dot_t(a, b):
    return lax.dot_general(a, b, (((1,), (1,)), ((), ())), preferred_element_type=F32)


def my_expert():
    return lax.axis_index("seq") * EXP + lax.axis_index("exp")


def expert_of(far, near):
    return (far & 7) * EXP + (far >> 3) * 8 + near


NEAR = [[expert_of(far, near) for near in range(8)] for far in range(16)]
FAR = [[expert_of(far, near) for far in range(16)] for near in range(8)]


def slots_by_row(ids, me):
    match = jnp.sum((ids == me).astype(F32), axis=0, keepdims=True)
    match = jnp.broadcast_to(match, (8, ROWS))
    before = (iota((ROWS, ROWS), 0) < iota((ROWS, ROWS), 1)).astype(F32)
    rank = dot(match, before)
    hit = jnp.logical_and(rank == iota((8, ROWS), 0).astype(F32), match > 0.5)
    return jnp.where(hit, 1.0, 0.0)


def slots_of(ids, experts, slot):
    match = jnp.zeros(experts.shape, F32)
    for k in range(ids.shape[0]):
        match = match + (ids[k : k + 1, :] == experts).astype(F32)
    before = (iota((ROWS, ROWS), 0) < iota((ROWS, ROWS), 1)).astype(F32)
    rank = dot(match, before)
    hit = jnp.logical_and(rank == slot.astype(F32), match > 0.5)
    return jnp.where(hit, 1.0, 0.0)


def spread_marks(count, bits):
    r = iota((ROWS, count), 0)
    i = iota((ROWS, count), 1)
    same = jnp.logical_and((i >> (2 + bits)) == (r >> 2), (i & 3) == (r & 3))
    return jnp.where(same, 1.0, 0.0)


def by_chunk(marks, chunks):
    i = iota(marks.shape, 1)
    return jnp.concatenate(
        [jnp.where(((i >> 2) & (chunks - 1)) == j, marks, 0.0) for j in range(chunks)], axis=0
    )


def pick_marks(slots, ids):
    expert = iota((EXPERTS, ROWS), 0)
    named = jnp.zeros((EXPERTS, ROWS), F32)
    for k in range(ids.shape[0]):
        named = named + (ids[k : k + 1, :] == expert).astype(F32)
    return dot_t(slots, named)


def gates_of(logits, picks, me):
    sig = 1.0 / (1.0 + jnp.exp(-logits))
    total = jnp.sum(sig * picks, axis=1, keepdims=True)
    own = jnp.sum(jnp.where(iota(sig.shape, 1) == me, sig, 0.0), axis=1, keepdims=True)
    return jnp.where(total > 0.0, own / total, 0.0)


def silu(a):
    return a / (1.0 + jnp.exp(-a))


def start_all(pairs, sems):
    copies = []
    for k, (src, dst) in enumerate(pairs):
        copy = pltpu.make_async_copy(src, dst, sems.at[k])
        copy.start()
        copies.append(copy)
    return copies


def attend_kernel(
    len_hbm,
    q_hbm,
    new_hbm,
    ids_hbm,
    talk_hbm,
    kv_hbm,
    out_ref,
    chosen_ref,
    picks_ref,
    sums_ref,
    carry_ref,
    place_ref,
    first_ref,
    len_ref,
    q_ref,
    new_ref,
    ids_ref,
    talk_ref,
    kv_ref,
    q_buf,
    o_buf,
    t_buf,
    sems,
):
    pairs = [(q_hbm, q_ref), (ids_hbm, ids_ref), (talk_hbm, talk_ref), (new_hbm, new_ref), (len_hbm, len_ref)]
    pairs += [(kv_hbm.at[t, c], kv_ref.at[t, c]) for t in range(2) for c in range(OWN)]
    copies = start_all(pairs, sems)
    small, keys, values = copies[:5], copies[5 : 5 + OWN], copies[5 + OWN :]
    for copy in small:
        copy.wait()
    seq = lax.axis_index("seq")
    scale = HD ** (-0.5)
    query = q_ref[...].astype(F32)
    for h in range(HEADS):
        q_buf[4 * h : 4 * h + 4, :] = query[:, HD * h : HD * h + HD]

    me = my_expert()
    near = lax.axis_index("exp") & 7
    far = (lax.axis_index("exp") >> 3) * 8 + seq
    ids = ids_ref[...]
    talk_ids = talk_ref[...]
    slots = slots_by_row(ids, me)
    talk_slots = slots_by_row(talk_ids, me)
    picks_ref[0] = pick_marks(slots, ids)
    picks_ref[1] = pick_marks(talk_slots, talk_ids)
    both = jnp.concatenate([slots, talk_slots], axis=0)
    chosen_ref[...] = by_chunk(dot(both, spread_marks(256, 2)), 4).astype(BF16)
    first = (talk_ids[0:1, :] == me).astype(F32)
    first_ref[...] = dot_t(talk_slots, jnp.broadcast_to(first, (128, ROWS)))
    line = iota((128, ROWS), 0)
    came = slots_of(ids, expert_of(far, line >> 4), line & 7)
    needed = slots_of(talk_ids, expert_of(line >> 3, near), line & 7)
    half = (iota((128, 128), 1) >> 3) & 1
    sums = dot_t(needed, came)
    sums_ref[0] = jnp.where(half == 0, sums, 0.0).astype(BF16)
    sums_ref[1] = jnp.where(half == 1, sums, 0.0).astype(BF16)
    line = iota((ROWS, ROWS), 0)
    row = ((line >> 2) & 1) * 32 + (line >> 3) * 4 + (line & 3)
    turn = jnp.where(row == iota((ROWS, ROWS), 1), 1.0, 0.0)
    line = iota((128, ROWS), 0)
    carry_ref[...] = dot_t(turn, slots_of(ids, expert_of(line >> 3, near), line & 7)).astype(BF16)
    place_ref[...] = dot_t(turn, jnp.concatenate([talk_slots, jnp.zeros_like(talk_slots)], axis=0)).astype(BF16)

    lane = iota((HEADS, KVH * HD), 1)
    diag = (iota((HEADS, KVH * HD), 0) >> 3) == (lane >> 7)
    place = lane + seq * SPAN
    tail_lane = iota((HEADS, HD), 1)
    parts = []
    for c in range(OWN):
        q = q_buf[pl.ds(c, HEADS, stride=4), :]
        wide = jnp.where(diag, jnp.concatenate([q] * KVH, axis=1), 0.0)
        fresh_key = new_ref[0, c : c + 1, :].astype(F32)
        fresh = jnp.sum(wide * fresh_key, axis=1, keepdims=True) * scale
        parts.append((wide.astype(BF16), jnp.where(seq == 0, fresh, NEG)))
    for copy in keys:
        copy.wait()
    done = []
    for c in range(OWN):
        wide, fresh = parts[c]
        valid = place < len_ref[c]
        scores = jnp.where(valid, dot_t(wide, kv_ref[0, c]) * scale, NEG)
        peak = jnp.maximum(jnp.max(scores, axis=1, keepdims=True), fresh)
        peak = peak.astype(BF16).astype(F32)
        weights = jnp.where(valid, jnp.exp(scores - peak), 0.0).astype(BF16)
        fresh_weight = jnp.where(seq == 0, jnp.exp(fresh - peak), 0.0)
        total = jnp.sum(weights.astype(F32), axis=1, keepdims=True) + fresh_weight
        upper = total.astype(BF16).astype(F32)
        tail = jnp.where(tail_lane == 0, peak, jnp.where(tail_lane == 1, upper, total - upper))
        t_buf[pl.ds(c, HEADS, stride=4), :] = tail
        done.append((weights, fresh_weight))
    for copy in values:
        copy.wait()
    for c in range(OWN):
        weights, fresh_weight = done[c]
        fresh_value = new_ref[1, c : c + 1, :].astype(F32)
        mixed = dot(weights, kv_ref[1, c]) + fresh_weight * fresh_value
        mixed = jnp.where(diag, mixed, 0.0)
        mixed = (mixed[:, :HD] + mixed[:, HD : 2 * HD]) + (
            mixed[:, 2 * HD : 3 * HD] + mixed[:, 3 * HD :]
        )
        o_buf[pl.ds(c, HEADS, stride=4), :] = mixed
    out_ref[:, :, :HD] = o_buf[...].reshape(SEQ, 16, HD).astype(BF16)
    out_ref[:, :, HD:] = t_buf[...].reshape(SEQ, 16, HD).astype(BF16)


def project_kernel(recv_ref, proj_ref, out_ref, row_buf):
    got = recv_ref[...].astype(F32)
    peak = got[:, :, HD : HD + 1]
    total = got[:, :, HD + 1 : HD + 2] + got[:, :, HD + 2 : HD + 3]
    scale = jnp.exp(peak - jnp.max(peak, axis=0, keepdims=True))
    total = jnp.sum(scale * total, axis=0)
    mixed = jnp.sum(scale * got[:, :, :HD], axis=0) / total
    attn = jnp.concatenate([mixed[4 * h : 4 * h + 4] for h in range(4)], axis=1).astype(BF16)
    part = dot(attn, proj_ref[...])
    for j in range(4):
        row_buf[4 * j : 4 * j + 4, :] = part[:, 512 * j : 512 * j + 512]
    msg = row_buf[...].astype(BF16)
    for d in range(SEQ):
        out_ref[d] = msg


def state_kernel(recv_ref, hidden_ref, out_ref, rows_ref, buf):
    for j in range(4):
        buf[4 * j : 4 * j + 4, :] = hidden_ref[:, 512 * j : 512 * j + 512]
    buf[...] = buf[...] + jnp.sum(recv_ref[...].astype(F32), axis=0)
    msg = buf[...].astype(BF16)
    for d in range(EXP):
        out_ref[d] = msg
    for j in range(4):
        rows_ref[:, 512 * j : 512 * j + 512] = buf[4 * j : 4 * j + 4, :]


def normed(stream, gain):
    mean = jnp.mean(stream * stream, axis=1, keepdims=True)
    return (stream * lax.rsqrt(mean + EPS) * gain).astype(BF16)


def expert_kernel(
    recv_ref,
    chosen_ref,
    picks_ref,
    gain_ref,
    router_ref,
    up_ref,
    down_ref,
    proj_ref,
    out_ref,
    reply_ref,
    talk_ref,
):
    me = my_expert()
    rows = dot(chosen_ref[...], recv_ref[...])
    rows = jnp.concatenate([rows[16 * j : 16 * j + 16] for j in range(4)], axis=1)
    own = normed(rows[:8], gain_ref[...])
    gates = gates_of(dot(own, router_ref[...]), picks_ref[0], me)
    both = dot(own, up_ref[0])
    inner = (silu(both[:, :FF]) * both[:, FF:]).astype(BF16)
    reply = dot(inner, down_ref[0])
    reply = gates * reply.astype(BF16).astype(F32)
    mixed = dot(jnp.concatenate([reply, rows[8:]], axis=0).astype(BF16), proj_ref[...])
    talk_ref[...] = mixed[8:]
    msg = jnp.concatenate([mixed[:8, :512], mixed[:8, 512:]], axis=0).astype(BF16)
    for d in range(8):
        out_ref[d] = msg
    for d in range(16):
        reply_ref[d] = reply[:, 128 * d : 128 * d + 128]


def route_kernel(recv_ref, sums_ref, reply_ref, out_ref):
    upper = dot(sums_ref[0], recv_ref[...])
    lower = dot(sums_ref[1], recv_ref[...])
    talk = [upper[:, 128 * k : 128 * k + 128].reshape(16, 8, 128) for k in range(4)]
    talk += [lower[:, 128 * k : 128 * k + 128].reshape(16, 8, 128) for k in range(4)]
    out_ref[...] = jnp.concatenate(talk + [reply_ref[...]], axis=1).astype(BF16)


def talker_kernel(
    recv_ref,
    talk_ref,
    picks_ref,
    carry_ref,
    place_ref,
    first_ref,
    gain_ref,
    router_ref,
    up_ref,
    down_ref,
    out_ref,
):
    me = my_expert()
    got = jnp.sum(recv_ref[:, :64, :].astype(F32), axis=0)
    talk_in = jnp.concatenate([got[8 * k : 8 * k + 8] for k in range(8)], axis=1) + talk_ref[...]
    own = normed(talk_in, gain_ref[...])
    gates = gates_of(dot(own, router_ref[...]), picks_ref[1], me)
    both = dot(own, up_ref[0])
    inner = (silu(both[:, :FT]) * both[:, FT:]).astype(BF16)
    reply = gates * dot(inner, down_ref[0]).astype(BF16).astype(F32)
    reply = reply + first_ref[:, :1] * talk_in
    reply = jnp.concatenate([reply, jnp.zeros_like(reply)], axis=0).astype(BF16)
    sent = dot(place_ref[...], reply)
    sent = [sent[:, 128 * k : 128 * k + 128].reshape(8, 8, 128) for k in range(8)]
    came = recv_ref[:, 64:, :].astype(F32).reshape(128, 128).astype(BF16)
    thinker = dot(carry_ref[...], came).reshape(8, 8, 128)
    out_ref[...] = jnp.concatenate(sent + [thinker], axis=1).astype(BF16)


def pass_kernel(recv_ref, out_ref, got_buf, buf):
    got_buf[...] = jnp.sum(recv_ref[...].astype(F32), axis=0)
    for side in range(2):
        for k in range(9):
            buf[side, 4 * k : 4 * k + 4, :] = got_buf[8 * k + 4 * side : 8 * k + 4 * side + 4, :]
        buf[side, 36:, :] = jnp.zeros((4, 128), F32)
    for d in range(16):
        out_ref[d] = buf[d >> 3].astype(BF16)


def finish_kernel(recv_ref, state_ref, thinker_ref, out_ref, buf):
    buf[...] = jnp.sum(recv_ref[:, :32, :].astype(F32), axis=0)
    for k in range(8):
        out_ref[:, 128 * k : 128 * k + 128] = buf[4 * k : 4 * k + 4, :]
    for d in range(16):
        cols = slice(128 * d, 128 * d + 128)
        thinker_ref[:, cols] = state_ref[:, cols] + recv_ref[d, 32:, :].astype(F32)[:OWN]


def call(kernel, outs, args, where, scratch=(), mib=16, flops=COST, outs_at=None):
    spaces = {"v": pltpu.VMEM, "s": pltpu.SMEM, "h": pltpu.HBM}
    many = isinstance(outs, list)
    whole = pl.BlockSpec(memory_space=pltpu.VMEM)
    return pl.pallas_call(
        kernel,
        out_shape=outs,
        in_specs=[pl.BlockSpec(memory_space=spaces[w]) for w in where],
        out_specs=[pl.BlockSpec(memory_space=spaces[w]) for w in outs_at or "v" * len(outs)] if many else whole,
        scratch_shapes=list(scratch),
        cost_estimate=pl.CostEstimate(flops=flops, bytes_accessed=1 << 20, transcendentals=0),
        compiler_params=pltpu.CompilerParams(vmem_limit_bytes=mib << 20),
    )(*args)


def array(shape, dtype):
    return jax.ShapeDtypeStruct(shape, dtype)


def exchange(msg, axis, groups=None):
    return lax.all_to_all(msg, axis, 0, 0, axis_index_groups=groups)


def on_device(
    queries,
    new_kv,
    kv_cache,
    lengths,
    out_proj,
    hidden_in,
    norm_gain,
    router,
    expert_ids,
    w_gate_up,
    w_down,
    talk_proj,
    talk_gain,
    talk_router,
    talk_ids,
    talk_gate_up,
    talk_down,
):
    both = ("seq", "exp")
    held = (lengths, queries, new_kv, expert_ids.T, talk_ids.T, kv_cache)
    msg, chosen, picks, sums, carry, place, first = call(
        attend_kernel,
        [
            array((SEQ, 16, 256), BF16),
            array((64, 256), BF16),
            array((2, 8, EXPERTS), F32),
            array((2, 128, 128), BF16),
            array((64, 128), BF16),
            array((64, 16), BF16),
            array((8, 128), F32),
        ],
        tuple(pltpu.with_memory_space_constraint(x, pltpu.HBM) for x in held),
        "hhhhhh",
        [
            pltpu.SMEM((OWN,), jnp.int32),
            pltpu.VMEM((OWN, HEADS * HD), BF16),
            pltpu.VMEM((2, OWN, KVH * HD), BF16),
            pltpu.VMEM((8, ROWS), jnp.int32),
            pltpu.VMEM((8, ROWS), jnp.int32),
            pltpu.VMEM((2, OWN, SPAN, KVH * HD), BF16),
            pltpu.VMEM((HEADS * OWN, HD), F32),
            pltpu.VMEM((HEADS * OWN, HD), F32),
            pltpu.VMEM((HEADS * OWN, HD), F32),
            pltpu.SemaphoreType.DMA((5 + 2 * OWN,)),
        ],
    )
    msg = call(
        project_kernel,
        array((SEQ, 16, 512), BF16),
        (exchange(msg, "seq"), out_proj),
        "vv",
        [pltpu.VMEM((16, 512), F32)],
    )
    msg, state = call(
        state_kernel,
        [array((EXP, 16, 512), BF16), array((OWN, D), F32)],
        (exchange(msg, "seq"), hidden_in),
        "vv",
        [pltpu.VMEM((16, 512), F32)],
    )
    msg, reply, talk_in = call(
        expert_kernel,
        [array((8, 16, 512), BF16), array((16, 8, 128), F32), array((8, DT), F32)],
        (
            exchange(msg, "exp").reshape(256, 512),
            chosen,
            picks,
            norm_gain.reshape(1, D),
            router,
            w_gate_up,
            w_down,
            talk_proj,
        ),
        "vvvvvvvv",
    )
    msg = call(
        route_kernel,
        array((16, 72, 128), BF16),
        (exchange(msg, both, NEAR).reshape(128, 512), sums, reply),
        "vvv",
    )
    msg = call(
        talker_kernel,
        array((8, 72, 128), BF16),
        (
            exchange(msg, both, FAR),
            talk_in,
            picks,
            carry,
            place,
            first,
            talk_gain.reshape(1, DT),
            talk_router,
            talk_gate_up,
            talk_down,
        ),
        "vvvvvvvvvv",
    )
    msg = call(
        pass_kernel,
        array((16, 40, 128), BF16),
        (exchange(msg, both, NEAR),),
        "v",
        [pltpu.VMEM((72, 128), F32), pltpu.VMEM((2, 40, 128), F32)],
    )
    thinker, talker = call(
        finish_kernel,
        [array((OWN, D), F32), array((OWN, DT), F32)],
        (exchange(msg, both, FAR), state),
        "vv",
        [pltpu.VMEM((32, 128), F32)],
    )
    return (thinker, talker)


def solution(mesh):
    placed = (
        P("exp", None),
        P(None, "exp", None),
        P(None, "exp", "seq", None),
        P("exp"),
        P("seq", None),
        P("exp", None),
        P(),
        P(),
        P(),
        P(("seq", "exp"), None, None),
        P(("seq", "exp"), None, None),
        P(),
        P(),
        P(),
        P(),
        P(("seq", "exp"), None, None),
        P(("seq", "exp"), None, None),
    )
    return jax.shard_map(
        on_device,
        mesh=mesh,
        in_specs=placed,
        out_specs=(P("exp", None), P("exp", None)),
        check_vma=False,
    )
```

time: 88.6 us -> 87.2 us (0.984)
  waiting for transfers between devices: 2.62 us -> 0 us
  blocking collectives: 76.4 us -> 78.1 us
    ppermute x2 -> x0, waiting for transfers between devices: 2.62 us -> none  [the longest x1 1.38 us: swap(): return lax.ppermute(msg, 'exp', [(e, e ^ 1) for e in range(EXP)])]
    all_to_all x6 -> x7, blocking collectives: 76.4 us -> 78.1 us  [exchange(): return lax.all_to_all(msg, axis, 0, 0, axis_index_groups=groups)]
    pallas_call x9 -> x8, Pallas kernels: 8.21 us -> 7.96 us  [call(): pl.pallas_call(kernel, out_shape=outs, in_specs=[pl.BlockSpec(memory_spac...]
  transfers between devices with their start and end apart: 2 -> 0, of which waited for: 2 -> 0; matrix products, arithmetic and copies ran while one was open for 0% -> 0% of each run, Pallas kernels for 0% -> 0%
where the time goes in v5:
time: 87.2 us; the launch traced here: 86.9 us
  blocking collectives  78.1 us (90%)
  Pallas kernels  7.96 us (9%)
    all_to_all x7, blocking collectives, exchange(): return lax.all_to_all(msg, axis, 0, 0, axis_index_groups=groups)  78.1 us
    pallas_call x8, Pallas kernels, call(): pl.pallas_call(kernel, out_shape=outs, in_specs=[pl.BlockSpec(memory_spac...  7.96 us

profile of v5, /device:TPU:0, one launch (start us, length us, event | category | flops | bytes accessed | tf_op | source)
XLA Modules:
  0.0 86.9 jit_solution(10931766689180710068)
XLA Ops:
  0.6 0.0 copy-start.3
  0.6 3.2 %shard_map.176 = (bf16[8,16,256]{2,1,0:T(8,128)(2,1)S(1)}, bf16[64,256]{1,0:T(8,128)(2,1)S(1)}, f32[2,8,128]{2,1,0:T(8,128)S(1)}, bf16[2,128,128]{2,1,0:T(8,128)...) custom-call(s32[4]{0:T(128)} %len_hbm.1, bf16[4,4096]{1,0:T(4,128)(2,1)} %q_hbm.1, ...), custom_call_target="tpu_custom_call" | custom-call | flops 99999997952 | bytes 1048576 | tf_op jit(solution)/shard_map/pallas_call | solution.py:344
  3.9 12.5 %all_to_all.35.recv_ref = bf16[8,16,256]{2,1,0:T(8,128)(2,1)S(1)} all-to-all(bf16[8,16,256]{2,1,0:T(8,128)(2,1)S(1)} %get-tuple-element.14), channel_id=1, replica_groups=mesh['seq'=8,'exp'=16] {'seq'}, dimensions={0} | all-to-all | bytes 131072 | tf_op jit(solution)/shard_map/all_to_all | solution.py:360
  16.4 0.0 copy-done.3
  16.4 0.0 copy-start.8
  16.4 0.6 shard_map.177
  17.0 9.0 %all_to_all.36.recv_ref = bf16[8,16,512]{2,1,0:T(8,128)(2,1)S(1)} all-to-all(bf16[8,16,512]{2,1,0:T(8,128)(2,1)S(1)} %shard_map.177), channel_id=1, replica_groups=mesh['seq'=8,'exp'=16] {'seq'}, dimensions={0} | all-to-all | bytes 262144 | tf_op jit(solution)/shard_map/all_to_all | solution.py:360
  26.0 0.0 copy-done.8
  26.0 0.0 copy-start
  26.0 0.0 copy-start.1
  26.0 0.0 copy-start.2
  26.0 0.0 copy-start.6
  26.0 0.0 copy-start.9
  26.1 16.4 %all_to_all.37 = bf16[16,16,512]{2,1,0:T(8,128)(2,1)S(1)} all-to-all(bf16[16,16,512]{2,1,0:T(8,128)(2,1)S(1)} %get-tuple-element.15), channel_id=1, replica_groups=mesh['seq'=8,'exp'=16] {'exp'}, dimensions={0} | all-to-all | bytes 524288 | tf_op jit(solution)/shard_map/all_to_all | solution.py:360
  42.4 0.0 copy-done
  42.4 0.0 copy-done.1
  42.4 0.0 copy-done.2
  42.4 0.0 copy-done.6
  42.5 0.0 copy-done.9
  42.5 2.2 %shard_map.179 = (bf16[8,16,512]{2,1,0:T(8,128)(2,1)S(1)}, f32[16,8,128]{2,1,0:T(8,128)S(1)}, f32[8,1024]{1,0:T(8,128)S(1)}) custom-call(bf16[256,512]{1,0:T(8,128)(2,1)S(1)} %bitcast.6, bf16[64,256]{1,0:T(8,128)(2,1)S(1)} %get-tuple-element.16.chosen_ref, f32[2,8,128]{2,1,0:T(8,128)S(1)} %get-tuple-element.17.picks_ref, f32[1,2048]{1,0:T(1,128)S(1)} %bitcast.8, ...), custom_call_target="tpu_custom_call" | custom-call | flops 99999997952 | bytes 1048576 | tf_op jit(solution)/shard_map/pallas_call | solution.py:344
  44.7 8.5 %all_to_all.38 = bf16[8,16,512]{2,1,0:T(8,128)(2,1)S(1)} all-to-all(bf16[8,16,512]{2,1,0:T(8,128)(2,1)S(1)} %get-tuple-element.18), channel_id=1, replica_groups={{0,1,2,3,4,5,6,7},{16,17,18,19,20,21,22,23},{32,33,34,35,36,37,38,39},{..., dimensions={0} | all-to-all | bytes 262144 | tf_op jit(solution)/shard_map/all_to_all | solution.py:360
  53.2 0.0 copy-start.4
  53.2 0.0 copy-start.5
  53.2 0.0 copy-start.7
  53.2 0.0 copy-start.10
  53.2 0.2 shard_map.180
  53.5 11.6 %all_to_all.39.recv_ref = bf16[16,72,128]{2,1,0:T(8,128)(2,1)S(1)} all-to-all(bf16[16,72,128]{2,1,0:T(8,128)(2,1)S(1)} %shard_map.180), channel_id=1, replica_groups={{0,16,32,48,64,80,96,112,8,24,40,56,72,88,104,120},{1,17,33,49,65,81,97..., dimensions={0} | all-to-all | bytes 589824 | tf_op jit(solution)/shard_map/all_to_all | solution.py:360
  65.1 0.0 copy-done.4
  65.1 0.0 copy-done.5
  65.1 0.0 copy-done.7
  65.1 0.0 copy-done.10
  65.1 0.9 %shard_map.181 = bf16[8,72,128]{2,1,0:T(8,128)(2,1)S(1)} custom-call(bf16[16,72,128]{2,1,0:T(8,128)(2,1)S(1)} %all_to_all.39.recv_ref, f32[8,1024]{1,0:T(8,128)S(1)} %get-tuple-element.21.talk_ref, f32[2,8,128]{2,1,0:T(8,128)S(1)} %get-tuple-element.17.picks_ref, bf16[64,128]{1,0:T(8,128)(2,1)S(1)} %get-tuple-element.22.carry_ref, ...), custom_call_target="tpu_custom_call" | custom-call | flops 99999997952 | bytes 1048576 | tf_op jit(solution)/shard_map/pallas_call | solution.py:344
  66.0 8.7 %all_to_all.40.recv_ref = bf16[8,72,128]{2,1,0:T(8,128)(2,1)S(1)} all-to-all(bf16[8,72,128]{2,1,0:T(8,128)(2,1)S(1)} %shard_map.181), channel_id=1, replica_groups={{0,1,2,3,4,5,6,7},{16,17,18,19,20,21,22,23},{32,33,34,35,36,37,38,39},{..., dimensions={0} | all-to-all | bytes 294912 | tf_op jit(solution)/shard_map/all_to_all | solution.py:360
  74.7 0.1 shard_map.182
  74.8 11.5 %all_to_all.41.recv_ref = bf16[16,40,128]{2,1,0:T(8,128)(2,1)S(1)} all-to-all(bf16[16,40,128]{2,1,0:T(8,128)(2,1)S(1)} %shard_map.182), channel_id=1, replica_groups={{0,16,32,48,64,80,96,112,8,24,40,56,72,88,104,120},{1,17,33,49,65,81,97..., dimensions={0} | all-to-all | bytes 327680 | tf_op jit(solution)/shard_map/all_to_all | solution.py:360
  86.2 0.6 shard_map.183
  (1 shorter events, 0.0 us)
Async XLA Ops:
  0.6 15.7 %copy-start.3 = (bf16[512,2048]{1,0:T(8,128)(2,1)S(1)}, bf16[512,2048]{1,0:T(8,128)(2,1)}, u32[]{:S(2)}) copy-start(bf16[512,2048]{1,0:T(8,128)(2,1)} %proj_ref.2) | copy-start | bytes 6291460
  16.4 9.6 %copy-start.8 = (f32[4,2048]{1,0:T(4,128)S(1)}, f32[4,2048]{1,0:T(4,128)}, u32[]{:S(2)}) copy-start(f32[4,2048]{1,0:T(4,128)} %hidden_ref.1) | copy-start | bytes 98308
  26.0 16.5 %copy-start = (bf16[1,2048,1536]{2,1,0:T(8,128)(2,1)S(1)}, bf16[1,2048,1536]{2,1,0:T(8,128)(2,1)}, u32[]{:S(2)}) copy-start(bf16[1,2048,1536]{2,1,0:T(8,128)(2,1)} %up_ref.2) | copy-start | bytes 18874372
  26.0 16.5 %copy-start.1 = (bf16[2048,1024]{1,0:T(8,128)(2,1)S(1)}, bf16[2048,1024]{1,0:T(8,128)(2,1)}, u32[]{:S(2)}) copy-start(bf16[2048,1024]{1,0:T(8,128)(2,1)} %proj_ref.3) | copy-start | bytes 12582916
  26.0 16.5 %copy-start.2 = (bf16[1,768,2048]{2,1,0:T(8,128)(2,1)S(1)}, bf16[1,768,2048]{2,1,0:T(8,128)(2,1)}, u32[]{:S(2)}) copy-start(bf16[1,768,2048]{2,1,0:T(8,128)(2,1)} %down_ref.2) | copy-start | bytes 9437188
  26.0 16.5 %copy-start.6 = (bf16[2048,128]{1,0:T(8,128)(2,1)S(1)}, bf16[2048,128]{1,0:T(8,128)(2,1)}, u32[]{:S(2)}) copy-start(bf16[2048,128]{1,0:T(8,128)(2,1)} %router_ref.2) | copy-start | bytes 1572868
  26.0 16.4 %copy-start.9 = (f32[2048]{0:T(1024)S(1)}, f32[2048]{0:T(1024)}, u32[]{:S(2)}) copy-start(f32[2048]{0:T(1024)} %param.23) | copy-start | bytes 24580
  53.2 11.9 %copy-start.4 = (bf16[1,1024,768]{2,1,0:T(8,128)(2,1)S(1)}, bf16[1,1024,768]{2,1,0:T(8,128)(2,1)}, u32[]{:S(2)}) copy-start(bf16[1,1024,768]{2,1,0:T(8,128)(2,1)} %up_ref.3) | copy-start | bytes 4718596
  53.2 11.9 %copy-start.5 = (bf16[1,384,1024]{2,1,0:T(8,128)(2,1)S(1)}, bf16[1,384,1024]{2,1,0:T(8,128)(2,1)}, u32[]{:S(2)}) copy-start(bf16[1,384,1024]{2,1,0:T(8,128)(2,1)} %down_ref.3) | copy-start | bytes 2359300
  53.2 11.9 %copy-start.7 = (bf16[1024,128]{1,0:T(8,128)(2,1)S(1)}, bf16[1024,128]{1,0:T(8,128)(2,1)}, u32[]{:S(2)}) copy-start(bf16[1024,128]{1,0:T(8,128)(2,1)} %router_ref.3) | copy-start | bytes 786436
  53.2 11.9 %copy-start.10 = (f32[1024]{0:T(1024)S(1)}, f32[1024]{0:T(1024)}, u32[]{:S(2)}) copy-start(f32[1024]{0:T(1024)} %param.29) | copy-start | bytes 12292

commit v6 on v5

--- a/solution.py
+++ b/solution.py
@@ -244,9 +244,8 @@
         rows_ref[:, 512 * j : 512 * j + 512] = buf[4 * j : 4 * j + 4, :]
 
 
-def normed(stream, gain):
-    mean = jnp.mean(stream * stream, axis=1, keepdims=True)
-    return (stream * lax.rsqrt(mean + EPS) * gain).astype(BF16)
+def inverse(stream):
+    return lax.rsqrt(jnp.mean(stream * stream, axis=1, keepdims=True) + EPS)
 
 
 def expert_kernel(
@@ -265,9 +264,10 @@
     me = my_expert()
     rows = dot(chosen_ref[...], recv_ref[...])
     rows = jnp.concatenate([rows[16 * j : 16 * j + 16] for j in range(4)], axis=1)
-    own = normed(rows[:8], gain_ref[...])
-    gates = gates_of(dot(own, router_ref[...]), picks_ref[0], me)
-    both = dot(own, up_ref[0])
+    inv = inverse(rows[:8])
+    own = (rows[:8] * gain_ref[...]).astype(BF16)
+    gates = gates_of(dot(own, router_ref[...]) * inv, picks_ref[0], me)
+    both = dot(own, up_ref[0]) * inv
     inner = (silu(both[:, :FF]) * both[:, FF:]).astype(BF16)
     reply = dot(inner, down_ref[0])
     reply = gates * reply.astype(BF16).astype(F32)
@@ -304,9 +304,10 @@
     me = my_expert()
     got = jnp.sum(recv_ref[:, :64, :].astype(F32), axis=0)
     talk_in = jnp.concatenate([got[8 * k : 8 * k + 8] for k in range(8)], axis=1) + talk_ref[...]
-    own = normed(talk_in, gain_ref[...])
-    gates = gates_of(dot(own, router_ref[...]), picks_ref[1], me)
-    both = dot(own, up_ref[0])
+    inv = inverse(talk_in)
+    own = (talk_in * gain_ref[...]).astype(BF16)
+    gates = gates_of(dot(own, router_ref[...]) * inv, picks_ref[1], me)
+    both = dot(own, up_ref[0]) * inv
     inner = (silu(both[:, :FT]) * both[:, FT:]).astype(BF16)
     reply = gates * dot(inner, down_ref[0]).astype(BF16).astype(F32)
     reply = reply + first_ref[:, :1] * talk_in

time: 87.2 us -> 87 us (level)
  no operation moved by 1% of the time
where the time goes in v6:
time: 87 us; the launch traced here: 86.7 us
  blocking collectives  78.1 us (90%)
  Pallas kernels  7.77 us (9%)
    all_to_all x7, blocking collectives, exchange(): return lax.all_to_all(msg, axis, 0, 0, axis_index_groups=groups)  78.1 us
    pallas_call x8, Pallas kernels, call(): pl.pallas_call(kernel, out_shape=outs, in_specs=[pl.BlockSpec(memory_spac...  7.77 us

profile of v6, /device:TPU:0, one launch (start us, length us, event | category | flops | bytes accessed | tf_op | source)
XLA Modules:
  0.0 86.7 jit_solution(11266543020081265748)
XLA Ops:
  0.6 0.0 copy-start.3
  0.6 3.2 %shard_map.176 = (bf16[8,16,256]{2,1,0:T(8,128)(2,1)S(1)}, bf16[64,256]{1,0:T(8,128)(2,1)S(1)}, f32[2,8,128]{2,1,0:T(8,128)S(1)}, bf16[2,128,128]{2,1,0:T(8,128)...) custom-call(s32[4]{0:T(128)} %len_hbm.1, bf16[4,4096]{1,0:T(4,128)(2,1)} %q_hbm.1, ...), custom_call_target="tpu_custom_call" | custom-call | flops 99999997952 | bytes 1048576 | tf_op jit(solution)/shard_map/pallas_call | solution.py:345
  3.9 12.5 %all_to_all.35.recv_ref = bf16[8,16,256]{2,1,0:T(8,128)(2,1)S(1)} all-to-all(bf16[8,16,256]{2,1,0:T(8,128)(2,1)S(1)} %get-tuple-element.14), channel_id=1, replica_groups=mesh['seq'=8,'exp'=16] {'seq'}, dimensions={0} | all-to-all | bytes 131072 | tf_op jit(solution)/shard_map/all_to_all | solution.py:361
  16.4 0.0 copy-done.3
  16.4 0.0 copy-start.8
  16.4 0.6 shard_map.177
  17.0 9.0 %all_to_all.36.recv_ref = bf16[8,16,512]{2,1,0:T(8,128)(2,1)S(1)} all-to-all(bf16[8,16,512]{2,1,0:T(8,128)(2,1)S(1)} %shard_map.177), channel_id=1, replica_groups=mesh['seq'=8,'exp'=16] {'seq'}, dimensions={0} | all-to-all | bytes 262144 | tf_op jit(solution)/shard_map/all_to_all | solution.py:361
  26.0 0.0 copy-done.8
  26.0 0.0 copy-start
  26.0 0.0 copy-start.1
  26.0 0.0 copy-start.2
  26.0 0.0 copy-start.6
  26.0 0.0 copy-start.9
  26.1 16.4 %all_to_all.37 = bf16[16,16,512]{2,1,0:T(8,128)(2,1)S(1)} all-to-all(bf16[16,16,512]{2,1,0:T(8,128)(2,1)S(1)} %get-tuple-element.15), channel_id=1, replica_groups=mesh['seq'=8,'exp'=16] {'exp'}, dimensions={0} | all-to-all | bytes 524288 | tf_op jit(solution)/shard_map/all_to_all | solution.py:361
  42.4 0.0 copy-done
  42.4 0.0 copy-done.1
  42.4 0.0 copy-done.2
  42.4 0.0 copy-done.6
  42.5 0.0 copy-done.9
  42.5 2.1 %shard_map.179 = (bf16[8,16,512]{2,1,0:T(8,128)(2,1)S(1)}, f32[16,8,128]{2,1,0:T(8,128)S(1)}, f32[8,1024]{1,0:T(8,128)S(1)}) custom-call(bf16[256,512]{1,0:T(8,128)(2,1)S(1)} %bitcast.6, bf16[64,256]{1,0:T(8,128)(2,1)S(1)} %get-tuple-element.16.chosen_ref, f32[2,8,128]{2,1,0:T(8,128)S(1)} %get-tuple-element.17.picks_ref, f32[1,2048]{1,0:T(1,128)S(1)} %bitcast.8, ...), custom_call_target="tpu_custom_call" | custom-call | flops 99999997952 | bytes 1048576 | tf_op jit(solution)/shard_map/pallas_call | solution.py:345
  44.6 8.5 %all_to_all.38 = bf16[8,16,512]{2,1,0:T(8,128)(2,1)S(1)} all-to-all(bf16[8,16,512]{2,1,0:T(8,128)(2,1)S(1)} %get-tuple-element.18), channel_id=1, replica_groups={{0,1,2,3,4,5,6,7},{16,17,18,19,20,21,22,23},{32,33,34,35,36,37,38,39},{..., dimensions={0} | all-to-all | bytes 262144 | tf_op jit(solution)/shard_map/all_to_all | solution.py:361
  53.1 0.0 copy-start.4
  53.1 0.0 copy-start.5
  53.1 0.0 copy-start.7
  53.1 0.0 copy-start.10
  53.1 0.2 shard_map.180
  53.4 11.6 %all_to_all.39.recv_ref = bf16[16,72,128]{2,1,0:T(8,128)(2,1)S(1)} all-to-all(bf16[16,72,128]{2,1,0:T(8,128)(2,1)S(1)} %shard_map.180), channel_id=1, replica_groups={{0,16,32,48,64,80,96,112,8,24,40,56,72,88,104,120},{1,17,33,49,65,81,97..., dimensions={0} | all-to-all | bytes 589824 | tf_op jit(solution)/shard_map/all_to_all | solution.py:361
  65.0 0.0 copy-done.4
  65.0 0.0 copy-done.5
  65.0 0.0 copy-done.7
  65.0 0.0 copy-done.10
  65.0 0.8 shard_map.181
  65.8 8.7 %all_to_all.40.recv_ref = bf16[8,72,128]{2,1,0:T(8,128)(2,1)S(1)} all-to-all(bf16[8,72,128]{2,1,0:T(8,128)(2,1)S(1)} %shard_map.181), channel_id=1, replica_groups={{0,1,2,3,4,5,6,7},{16,17,18,19,20,21,22,23},{32,33,34,35,36,37,38,39},{..., dimensions={0} | all-to-all | bytes 294912 | tf_op jit(solution)/shard_map/all_to_all | solution.py:361
  74.5 0.1 shard_map.182
  74.6 11.5 %all_to_all.41.recv_ref = bf16[16,40,128]{2,1,0:T(8,128)(2,1)S(1)} all-to-all(bf16[16,40,128]{2,1,0:T(8,128)(2,1)S(1)} %shard_map.182), channel_id=1, replica_groups={{0,16,32,48,64,80,96,112,8,24,40,56,72,88,104,120},{1,17,33,49,65,81,97..., dimensions={0} | all-to-all | bytes 327680 | tf_op jit(solution)/shard_map/all_to_all | solution.py:361
  86.0 0.6 shard_map.183
  (1 shorter events, 0.0 us)
Async XLA Ops:
  0.6 15.7 %copy-start.3 = (bf16[512,2048]{1,0:T(8,128)(2,1)S(1)}, bf16[512,2048]{1,0:T(8,128)(2,1)}, u32[]{:S(2)}) copy-start(bf16[512,2048]{1,0:T(8,128)(2,1)} %proj_ref.2) | copy-start | bytes 6291460
  16.4 9.6 %copy-start.8 = (f32[4,2048]{1,0:T(4,128)S(1)}, f32[4,2048]{1,0:T(4,128)}, u32[]{:S(2)}) copy-start(f32[4,2048]{1,0:T(4,128)} %hidden_ref.1) | copy-start | bytes 98308
  26.0 16.5 %copy-start = (bf16[1,2048,1536]{2,1,0:T(8,128)(2,1)S(1)}, bf16[1,2048,1536]{2,1,0:T(8,128)(2,1)}, u32[]{:S(2)}) copy-start(bf16[1,2048,1536]{2,1,0:T(8,128)(2,1)} %up_ref.2) | copy-start | bytes 18874372
  26.0 16.5 %copy-start.1 = (bf16[2048,1024]{1,0:T(8,128)(2,1)S(1)}, bf16[2048,1024]{1,0:T(8,128)(2,1)}, u32[]{:S(2)}) copy-start(bf16[2048,1024]{1,0:T(8,128)(2,1)} %proj_ref.3) | copy-start | bytes 12582916
  26.0 16.5 %copy-start.2 = (bf16[1,768,2048]{2,1,0:T(8,128)(2,1)S(1)}, bf16[1,768,2048]{2,1,0:T(8,128)(2,1)}, u32[]{:S(2)}) copy-start(bf16[1,768,2048]{2,1,0:T(8,128)(2,1)} %down_ref.2) | copy-start | bytes 9437188
  26.0 16.5 %copy-start.6 = (bf16[2048,128]{1,0:T(8,128)(2,1)S(1)}, bf16[2048,128]{1,0:T(8,128)(2,1)}, u32[]{:S(2)}) copy-start(bf16[2048,128]{1,0:T(8,128)(2,1)} %router_ref.2) | copy-start | bytes 1572868
  26.0 16.4 %copy-start.9 = (f32[2048]{0:T(1024)S(1)}, f32[2048]{0:T(1024)}, u32[]{:S(2)}) copy-start(f32[2048]{0:T(1024)} %param.23) | copy-start | bytes 24580
  53.1 11.9 %copy-start.4 = (bf16[1,1024,768]{2,1,0:T(8,128)(2,1)S(1)}, bf16[1,1024,768]{2,1,0:T(8,128)(2,1)}, u32[]{:S(2)}) copy-start(bf16[1,1024,768]{2,1,0:T(8,128)(2,1)} %up_ref.3) | copy-start | bytes 4718596
  53.1 11.9 %copy-start.5 = (bf16[1,384,1024]{2,1,0:T(8,128)(2,1)S(1)}, bf16[1,384,1024]{2,1,0:T(8,128)(2,1)}, u32[]{:S(2)}) copy-start(bf16[1,384,1024]{2,1,0:T(8,128)(2,1)} %down_ref.3) | copy-start | bytes 2359300
  53.1 11.9 %copy-start.7 = (bf16[1024,128]{1,0:T(8,128)(2,1)S(1)}, bf16[1024,128]{1,0:T(8,128)(2,1)}, u32[]{:S(2)}) copy-start(bf16[1024,128]{1,0:T(8,128)(2,1)} %router_ref.3) | copy-start | bytes 786436
  53.1 11.9 %copy-start.10 = (f32[1024]{0:T(1024)S(1)}, f32[1024]{0:T(1024)}, u32[]{:S(2)}) copy-start(f32[1024]{0:T(1024)} %param.29) | copy-start | bytes 12292

commit v7 on v6

--- a/solution.py
+++ b/solution.py
@@ -46,8 +46,19 @@
     return (far & 7) * EXP + (far >> 3) * 8 + near
 
 
-NEAR = [[expert_of(far, near) for near in range(8)] for far in range(16)]
-FAR = [[expert_of(far, near) for far in range(16)] for near in range(8)]
+def at(order, index):
+    found = jnp.zeros_like(index)
+    for k, member in enumerate(order):
+        found = jnp.where(index == k, member, found)
+    return found
+
+
+SEQ_ORDER = (7, 6, 5, 4, 3, 1, 0, 2)
+ALL_ORDER = (0, 1, 2, 3, 4, 5, 6, 7, 8, 9, 10, 11, 12, 13, 14, 15)
+NEAR_ORDER = (1, 4, 2, 3, 7, 5, 6, 0)
+FAR_ORDER = (2, 0, 14, 9, 3, 4, 8, 13, 11, 12, 7, 5, 15, 6, 1, 10)
+NEAR = [[expert_of(far, near) for near in NEAR_ORDER] for far in range(16)]
+FAR = [[expert_of(far, near) for far in FAR_ORDER] for near in range(8)]
 
 
 def slots_by_row(ids, me):
@@ -72,7 +83,7 @@
 def spread_marks(count, bits):
     r = iota((ROWS, count), 0)
     i = iota((ROWS, count), 1)
-    same = jnp.logical_and((i >> (2 + bits)) == (r >> 2), (i & 3) == (r & 3))
+    same = jnp.logical_and(at(ALL_ORDER, i >> (2 + bits)) == (r >> 2), (i & 3) == (r & 3))
     return jnp.where(same, 1.0, 0.0)
 
 
@@ -162,17 +173,17 @@
     first = (talk_ids[0:1, :] == me).astype(F32)
     first_ref[...] = dot_t(talk_slots, jnp.broadcast_to(first, (128, ROWS)))
     line = iota((128, ROWS), 0)
-    came = slots_of(ids, expert_of(far, line >> 4), line & 7)
-    needed = slots_of(talk_ids, expert_of(line >> 3, near), line & 7)
+    came = slots_of(ids, expert_of(far, at(NEAR_ORDER, line >> 4)), line & 7)
+    needed = slots_of(talk_ids, expert_of(at(FAR_ORDER, line >> 3), near), line & 7)
     half = (iota((128, 128), 1) >> 3) & 1
     sums = dot_t(needed, came)
     sums_ref[0] = jnp.where(half == 0, sums, 0.0).astype(BF16)
     sums_ref[1] = jnp.where(half == 1, sums, 0.0).astype(BF16)
     line = iota((ROWS, ROWS), 0)
-    row = ((line >> 2) & 1) * 32 + (line >> 3) * 4 + (line & 3)
+    row = ((line >> 2) & 1) * 32 + at(NEAR_ORDER, line >> 3) * 4 + (line & 3)
     turn = jnp.where(row == iota((ROWS, ROWS), 1), 1.0, 0.0)
     line = iota((128, ROWS), 0)
-    carry_ref[...] = dot_t(turn, slots_of(ids, expert_of(line >> 3, near), line & 7)).astype(BF16)
+    carry_ref[...] = dot_t(turn, slots_of(ids, expert_of(at(FAR_ORDER, line >> 3), near), line & 7)).astype(BF16)
     place_ref[...] = dot_t(turn, jnp.concatenate([talk_slots, jnp.zeros_like(talk_slots)], axis=0)).astype(BF16)
 
     lane = iota((HEADS, KVH * HD), 1)
@@ -213,8 +224,9 @@
             mixed[:, 2 * HD : 3 * HD] + mixed[:, 3 * HD :]
         )
         o_buf[pl.ds(c, HEADS, stride=4), :] = mixed
-    out_ref[:, :, :HD] = o_buf[...].reshape(SEQ, 16, HD).astype(BF16)
-    out_ref[:, :, HD:] = t_buf[...].reshape(SEQ, 16, HD).astype(BF16)
+    for d, s in enumerate(SEQ_ORDER):
+        out_ref[d, :, :HD] = o_buf[16 * s : 16 * s + 16, :].astype(BF16)
+        out_ref[d, :, HD:] = t_buf[16 * s : 16 * s + 16, :].astype(BF16)
 
 
 def project_kernel(recv_ref, proj_ref, out_ref, row_buf):
@@ -276,8 +288,8 @@
     msg = jnp.concatenate([mixed[:8, :512], mixed[:8, 512:]], axis=0).astype(BF16)
     for d in range(8):
         out_ref[d] = msg
-    for d in range(16):
-        reply_ref[d] = reply[:, 128 * d : 128 * d + 128]
+    for d, far in enumerate(FAR_ORDER):
+        reply_ref[d] = reply[:, 128 * far : 128 * far + 128]
 
 
 def route_kernel(recv_ref, sums_ref, reply_ref, out_ref):
@@ -325,16 +337,16 @@
         for k in range(9):
             buf[side, 4 * k : 4 * k + 4, :] = got_buf[8 * k + 4 * side : 8 * k + 4 * side + 4, :]
         buf[side, 36:, :] = jnp.zeros((4, 128), F32)
-    for d in range(16):
-        out_ref[d] = buf[d >> 3].astype(BF16)
+    for d, far in enumerate(FAR_ORDER):
+        out_ref[d] = buf[far >> 3].astype(BF16)
 
 
 def finish_kernel(recv_ref, state_ref, thinker_ref, out_ref, buf):
     buf[...] = jnp.sum(recv_ref[:, :32, :].astype(F32), axis=0)
     for k in range(8):
         out_ref[:, 128 * k : 128 * k + 128] = buf[4 * k : 4 * k + 4, :]
-    for d in range(16):
-        cols = slice(128 * d, 128 * d + 128)
+    for d, far in enumerate(FAR_ORDER):
+        cols = slice(128 * far, 128 * far + 128)
         thinker_ref[:, cols] = state_ref[:, cols] + recv_ref[d, 32:, :].astype(F32)[:OWN]
 
 
@@ -411,14 +423,14 @@
     msg = call(
         project_kernel,
         array((SEQ, 16, 512), BF16),
-        (exchange(msg, "seq"), out_proj),
+        (exchange(msg, "seq", [list(SEQ_ORDER)]), out_proj),
         "vv",
         [pltpu.VMEM((16, 512), F32)],
     )
     msg, state = call(
         state_kernel,
         [array((EXP, 16, 512), BF16), array((OWN, D), F32)],
-        (exchange(msg, "seq"), hidden_in),
+        (exchange(msg, "seq", [list(SEQ_ORDER)]), hidden_in),
         "vv",
         [pltpu.VMEM((16, 512), F32)],
     )
@@ -426,7 +438,7 @@
         expert_kernel,
         [array((8, 16, 512), BF16), array((16, 8, 128), F32), array((8, DT), F32)],
         (
-            exchange(msg, "exp").reshape(256, 512),
+            exchange(msg, "exp", [list(ALL_ORDER)]).reshape(256, 512),
             chosen,
             picks,
             norm_gain.reshape(1, D),

time: 87 us -> 83.9 us (0.964)
  blocking collectives: 78.1 us -> 75 us
    all_to_all x7, blocking collectives: 78.1 us -> 75 us  [exchange(): return lax.all_to_all(msg, axis, 0, 0, axis_index_groups=groups)]
where the time goes in v7:
time: 83.9 us; the launch traced here: 83.5 us
  blocking collectives  75 us (89%)
  Pallas kernels  7.77 us (9%)
    all_to_all x7, blocking collectives, exchange(): return lax.all_to_all(msg, axis, 0, 0, axis_index_groups=groups)  75 us
    pallas_call x8, Pallas kernels, call(): pl.pallas_call(kernel, out_shape=outs, in_specs=[pl.BlockSpec(memory_spac...  7.77 us

profile of v7, /device:TPU:0, one launch (start us, length us, event | category | flops | bytes accessed | tf_op | source)
XLA Modules:
  0.0 83.5 jit_solution(3658518591916044492)
XLA Ops:
  0.6 0.0 copy-start.3
  0.6 3.2 %shard_map.176 = (bf16[8,16,256]{2,1,0:T(8,128)(2,1)S(1)}, bf16[64,256]{1,0:T(8,128)(2,1)S(1)}, f32[2,8,128]{2,1,0:T(8,128)S(1)}, bf16[2,128,128]{2,1,0:T(8,128)...) custom-call(s32[4]{0:T(128)} %len_hbm.1, bf16[4,4096]{1,0:T(4,128)(2,1)} %q_hbm.1, ...), custom_call_target="tpu_custom_call" | custom-call | flops 99999997952 | bytes 1048576 | tf_op jit(solution)/shard_map/pallas_call | solution.py:357
  3.9 10.9 %all_to_all.35.recv_ref = bf16[8,16,256]{2,1,0:T(8,128)(2,1)S(1)} all-to-all(bf16[8,16,256]{2,1,0:T(8,128)(2,1)S(1)} %get-tuple-element.14), channel_id=1, replica_groups={{112,96,80,64,48,16,0,32},{113,97,81,65,49,17,1,33},{114,98,82,66,50,18..., dimensions={0} | all-to-all | bytes 131072 | tf_op jit(solution)/shard_map/all_to_all | solution.py:373
  14.8 0.0 copy-done.3
  14.8 0.0 copy-start.8
  14.8 0.6 shard_map.177
  15.4 9.1 %all_to_all.36.recv_ref = bf16[8,16,512]{2,1,0:T(8,128)(2,1)S(1)} all-to-all(bf16[8,16,512]{2,1,0:T(8,128)(2,1)S(1)} %shard_map.177), channel_id=1, replica_groups={{112,96,80,64,48,16,0,32},{113,97,81,65,49,17,1,33},{114,98,82,66,50,18..., dimensions={0} | all-to-all | bytes 262144 | tf_op jit(solution)/shard_map/all_to_all | solution.py:373
  24.5 0.0 copy-done.8
  24.5 0.0 copy-start
  24.5 0.0 copy-start.1
  24.5 0.0 copy-start.2
  24.5 0.0 copy-start.6
  24.5 0.0 copy-start.9
  24.6 16.4 %all_to_all.37 = bf16[16,16,512]{2,1,0:T(8,128)(2,1)S(1)} all-to-all(bf16[16,16,512]{2,1,0:T(8,128)(2,1)S(1)} %get-tuple-element.15), channel_id=1, replica_groups={{0,1,2,3,4,5,6,7,8,9,10,11,12,13,14,15},{16,17,18,19,20,21,22,23,24,25,..., dimensions={0} | all-to-all | bytes 524288 | tf_op jit(solution)/shard_map/all_to_all | solution.py:373
  40.9 0.0 copy-done
  40.9 0.0 copy-done.1
  40.9 0.0 copy-done.2
  40.9 0.0 copy-done.6
  40.9 0.0 copy-done.9
  40.9 2.1 %shard_map.179 = (bf16[8,16,512]{2,1,0:T(8,128)(2,1)S(1)}, f32[16,8,128]{2,1,0:T(8,128)S(1)}, f32[8,1024]{1,0:T(8,128)S(1)}) custom-call(bf16[256,512]{1,0:T(8,128)(2,1)S(1)} %bitcast.6, bf16[64,256]{1,0:T(8,128)(2,1)S(1)} %get-tuple-element.16.chosen_ref, f32[2,8,128]{2,1,0:T(8,128)S(1)} %get-tuple-element.17.picks_ref, f32[1,2048]{1,0:T(1,128)S(1)} %bitcast.8, ...), custom_call_target="tpu_custom_call" | custom-call | flops 99999997952 | bytes 1048576 | tf_op jit(solution)/shard_map/pallas_call | solution.py:357
  43.1 7.7 %all_to_all.38 = bf16[8,16,512]{2,1,0:T(8,128)(2,1)S(1)} all-to-all(bf16[8,16,512]{2,1,0:T(8,128)(2,1)S(1)} %get-tuple-element.18), channel_id=1, replica_groups={{1,4,2,3,7,5,6,0},{17,20,18,19,23,21,22,16},{33,36,34,35,39,37,38,32},{..., dimensions={0} | all-to-all | bytes 262144 | tf_op jit(solution)/shard_map/all_to_all | solution.py:373
  50.8 0.0 copy-start.4
  50.8 0.0 copy-start.5
  50.8 0.0 copy-start.7
  50.8 0.0 copy-start.10
  50.8 0.2 shard_map.180
  51.0 11.6 %all_to_all.39.recv_ref = bf16[16,72,128]{2,1,0:T(8,128)(2,1)S(1)} all-to-all(bf16[16,72,128]{2,1,0:T(8,128)(2,1)S(1)} %shard_map.180), channel_id=1, replica_groups={{32,0,104,24,48,64,8,88,56,72,112,80,120,96,16,40},{33,1,105,25,49,65,9..., dimensions={0} | all-to-all | bytes 589824 | tf_op jit(solution)/shard_map/all_to_all | solution.py:373
  62.6 0.0 copy-done.4
  62.6 0.0 copy-done.5
  62.6 0.0 copy-done.7
  62.6 0.0 copy-done.10
  62.7 0.8 shard_map.181
  63.5 8.2 %all_to_all.40.recv_ref = bf16[8,72,128]{2,1,0:T(8,128)(2,1)S(1)} all-to-all(bf16[8,72,128]{2,1,0:T(8,128)(2,1)S(1)} %shard_map.181), channel_id=1, replica_groups={{1,4,2,3,7,5,6,0},{17,20,18,19,23,21,22,16},{33,36,34,35,39,37,38,32},{..., dimensions={0} | all-to-all | bytes 294912 | tf_op jit(solution)/shard_map/all_to_all | solution.py:373
  71.6 0.1 shard_map.182
  71.7 11.2 %all_to_all.41.recv_ref = bf16[16,40,128]{2,1,0:T(8,128)(2,1)S(1)} all-to-all(bf16[16,40,128]{2,1,0:T(8,128)(2,1)S(1)} %shard_map.182), channel_id=1, replica_groups={{32,0,104,24,48,64,8,88,56,72,112,80,120,96,16,40},{33,1,105,25,49,65,9..., dimensions={0} | all-to-all | bytes 327680 | tf_op jit(solution)/shard_map/all_to_all | solution.py:373
  82.9 0.6 shard_map.183
  (1 shorter events, 0.0 us)
Async XLA Ops:
  0.6 14.2 %copy-start.3 = (bf16[512,2048]{1,0:T(8,128)(2,1)S(1)}, bf16[512,2048]{1,0:T(8,128)(2,1)}, u32[]{:S(2)}) copy-start(bf16[512,2048]{1,0:T(8,128)(2,1)} %proj_ref.2) | copy-start | bytes 6291460
  14.8 9.7 %copy-start.8 = (f32[4,2048]{1,0:T(4,128)S(1)}, f32[4,2048]{1,0:T(4,128)}, u32[]{:S(2)}) copy-start(f32[4,2048]{1,0:T(4,128)} %hidden_ref.1) | copy-start | bytes 98308
  24.5 16.5 %copy-start = (bf16[1,2048,1536]{2,1,0:T(8,128)(2,1)S(1)}, bf16[1,2048,1536]{2,1,0:T(8,128)(2,1)}, u32[]{:S(2)}) copy-start(bf16[1,2048,1536]{2,1,0:T(8,128)(2,1)} %up_ref.2) | copy-start | bytes 18874372
  24.5 16.5 %copy-start.1 = (bf16[2048,1024]{1,0:T(8,128)(2,1)S(1)}, bf16[2048,1024]{1,0:T(8,128)(2,1)}, u32[]{:S(2)}) copy-start(bf16[2048,1024]{1,0:T(8,128)(2,1)} %proj_ref.3) | copy-start | bytes 12582916
  24.5 16.5 %copy-start.2 = (bf16[1,768,2048]{2,1,0:T(8,128)(2,1)S(1)}, bf16[1,768,2048]{2,1,0:T(8,128)(2,1)}, u32[]{:S(2)}) copy-start(bf16[1,768,2048]{2,1,0:T(8,128)(2,1)} %down_ref.2) | copy-start | bytes 9437188
  24.5 16.5 %copy-start.6 = (bf16[2048,128]{1,0:T(8,128)(2,1)S(1)}, bf16[2048,128]{1,0:T(8,128)(2,1)}, u32[]{:S(2)}) copy-start(bf16[2048,128]{1,0:T(8,128)(2,1)} %router_ref.2) | copy-start | bytes 1572868
  24.5 16.4 %copy-start.9 = (f32[2048]{0:T(1024)S(1)}, f32[2048]{0:T(1024)}, u32[]{:S(2)}) copy-start(f32[2048]{0:T(1024)} %param.23) | copy-start | bytes 24580
  50.8 11.8 %copy-start.4 = (bf16[1,1024,768]{2,1,0:T(8,128)(2,1)S(1)}, bf16[1,1024,768]{2,1,0:T(8,128)(2,1)}, u32[]{:S(2)}) copy-start(bf16[1,1024,768]{2,1,0:T(8,128)(2,1)} %up_ref.3) | copy-start | bytes 4718596
  50.8 11.8 %copy-start.5 = (bf16[1,384,1024]{2,1,0:T(8,128)(2,1)S(1)}, bf16[1,384,1024]{2,1,0:T(8,128)(2,1)}, u32[]{:S(2)}) copy-start(bf16[1,384,1024]{2,1,0:T(8,128)(2,1)} %down_ref.3) | copy-start | bytes 2359300
  50.8 11.8 %copy-start.7 = (bf16[1024,128]{1,0:T(8,128)(2,1)S(1)}, bf16[1024,128]{1,0:T(8,128)(2,1)}, u32[]{:S(2)}) copy-start(bf16[1024,128]{1,0:T(8,128)(2,1)} %router_ref.3) | copy-start | bytes 786436
  50.8 11.8 %copy-start.10 = (f32[1024]{0:T(1024)S(1)}, f32[1024]{0:T(1024)}, u32[]{:S(2)}) copy-start(f32[1024]{0:T(1024)} %param.29) | copy-start | bytes 12292

commit v8 on v7

--- a/solution.py
+++ b/solution.py
@@ -55,8 +55,8 @@
 
 SEQ_ORDER = (7, 6, 5, 4, 3, 1, 0, 2)
 ALL_ORDER = (0, 1, 2, 3, 4, 5, 6, 7, 8, 9, 10, 11, 12, 13, 14, 15)
-NEAR_ORDER = (1, 4, 2, 3, 7, 5, 6, 0)
-FAR_ORDER = (2, 0, 14, 9, 3, 4, 8, 13, 11, 12, 7, 5, 15, 6, 1, 10)
+NEAR_ORDER = (1, 0, 2, 3, 7, 5, 6, 4)
+FAR_ORDER = (6, 1, 4, 0, 13, 10, 7, 14, 9, 2, 5, 12, 8, 15, 11, 3)
 NEAR = [[expert_of(far, near) for near in NEAR_ORDER] for far in range(16)]
 FAR = [[expert_of(far, near) for far in FAR_ORDER] for near in range(8)]
 

time: 83.9 us -> 82.7 us (0.986)
  blocking collectives: 75 us -> 73.9 us
    all_to_all x7, blocking collectives: 75 us -> 73.9 us  [exchange(): return lax.all_to_all(msg, axis, 0, 0, axis_index_groups=groups)]
where the time goes in v8:
time: 82.7 us; the launch traced here: 82.4 us
  blocking collectives  73.9 us (89%)
  Pallas kernels  7.76 us (9%)
    all_to_all x7, blocking collectives, exchange(): return lax.all_to_all(msg, axis, 0, 0, axis_index_groups=groups)  73.9 us
    pallas_call x8, Pallas kernels, call(): pl.pallas_call(kernel, out_shape=outs, in_specs=[pl.BlockSpec(memory_spac...  7.76 us

profile of v8, /device:TPU:0, one launch (start us, length us, event | category | flops | bytes accessed | tf_op | source)
XLA Modules:
  0.0 82.4 jit_solution(9549806503493280995)
XLA Ops:
  0.6 0.0 copy-start.3
  0.6 3.2 %shard_map.176 = (bf16[8,16,256]{2,1,0:T(8,128)(2,1)S(1)}, bf16[64,256]{1,0:T(8,128)(2,1)S(1)}, f32[2,8,128]{2,1,0:T(8,128)S(1)}, bf16[2,128,128]{2,1,0:T(8,128)...) custom-call(s32[4]{0:T(128)} %len_hbm.1, bf16[4,4096]{1,0:T(4,128)(2,1)} %q_hbm.1, ...), custom_call_target="tpu_custom_call" | custom-call | flops 99999997952 | bytes 1048576 | tf_op jit(solution)/shard_map/pallas_call | solution.py:357
  3.9 10.9 %all_to_all.35.recv_ref = bf16[8,16,256]{2,1,0:T(8,128)(2,1)S(1)} all-to-all(bf16[8,16,256]{2,1,0:T(8,128)(2,1)S(1)} %get-tuple-element.14), channel_id=1, replica_groups={{112,96,80,64,48,16,0,32},{113,97,81,65,49,17,1,33},{114,98,82,66,50,18..., dimensions={0} | all-to-all | bytes 131072 | tf_op jit(solution)/shard_map/all_to_all | solution.py:373
  14.8 0.0 copy-done.3
  14.8 0.0 copy-start.8
  14.8 0.6 shard_map.177
  15.4 9.1 %all_to_all.36.recv_ref = bf16[8,16,512]{2,1,0:T(8,128)(2,1)S(1)} all-to-all(bf16[8,16,512]{2,1,0:T(8,128)(2,1)S(1)} %shard_map.177), channel_id=1, replica_groups={{112,96,80,64,48,16,0,32},{113,97,81,65,49,17,1,33},{114,98,82,66,50,18..., dimensions={0} | all-to-all | bytes 262144 | tf_op jit(solution)/shard_map/all_to_all | solution.py:373
  24.5 0.0 copy-done.8
  24.5 0.0 copy-start
  24.5 0.0 copy-start.1
  24.5 0.0 copy-start.2
  24.5 0.0 copy-start.6
  24.5 0.0 copy-start.9
  24.6 16.4 %all_to_all.37 = bf16[16,16,512]{2,1,0:T(8,128)(2,1)S(1)} all-to-all(bf16[16,16,512]{2,1,0:T(8,128)(2,1)S(1)} %get-tuple-element.15), channel_id=1, replica_groups={{0,1,2,3,4,5,6,7,8,9,10,11,12,13,14,15},{16,17,18,19,20,21,22,23,24,25,..., dimensions={0} | all-to-all | bytes 524288 | tf_op jit(solution)/shard_map/all_to_all | solution.py:373
  40.9 0.0 copy-done
  40.9 0.0 copy-done.1
  40.9 0.0 copy-done.2
  40.9 0.0 copy-done.6
  40.9 0.0 copy-done.9
  40.9 2.1 %shard_map.179 = (bf16[8,16,512]{2,1,0:T(8,128)(2,1)S(1)}, f32[16,8,128]{2,1,0:T(8,128)S(1)}, f32[8,1024]{1,0:T(8,128)S(1)}) custom-call(bf16[256,512]{1,0:T(8,128)(2,1)S(1)} %bitcast.6, bf16[64,256]{1,0:T(8,128)(2,1)S(1)} %get-tuple-element.16.chosen_ref, f32[2,8,128]{2,1,0:T(8,128)S(1)} %get-tuple-element.17.picks_ref, f32[1,2048]{1,0:T(1,128)S(1)} %bitcast.8, ...), custom_call_target="tpu_custom_call" | custom-call | flops 99999997952 | bytes 1048576 | tf_op jit(solution)/shard_map/pallas_call | solution.py:357
  43.1 7.5 %all_to_all.38 = bf16[8,16,512]{2,1,0:T(8,128)(2,1)S(1)} all-to-all(bf16[8,16,512]{2,1,0:T(8,128)(2,1)S(1)} %get-tuple-element.18), channel_id=1, replica_groups={{1,0,2,3,7,5,6,4},{17,16,18,19,23,21,22,20},{33,32,34,35,39,37,38,36},{..., dimensions={0} | all-to-all | bytes 262144 | tf_op jit(solution)/shard_map/all_to_all | solution.py:373
  50.6 0.0 copy-start.4
  50.6 0.0 copy-start.5
  50.6 0.0 copy-start.7
  50.6 0.0 copy-start.10
  50.6 0.2 shard_map.180
  50.8 11.7 %all_to_all.39.recv_ref = bf16[16,72,128]{2,1,0:T(8,128)(2,1)S(1)} all-to-all(bf16[16,72,128]{2,1,0:T(8,128)(2,1)S(1)} %shard_map.180), channel_id=1, replica_groups={{96,16,64,0,88,40,112,104,24,32,80,72,8,120,56,48},{97,17,65,1,89,41,11..., dimensions={0} | all-to-all | bytes 589824 | tf_op jit(solution)/shard_map/all_to_all | solution.py:373
  62.6 0.0 copy-done.4
  62.6 0.0 copy-done.5
  62.6 0.0 copy-done.7
  62.6 0.0 copy-done.10
  62.6 0.8 shard_map.181
  63.4 7.7 %all_to_all.40.recv_ref = bf16[8,72,128]{2,1,0:T(8,128)(2,1)S(1)} all-to-all(bf16[8,72,128]{2,1,0:T(8,128)(2,1)S(1)} %shard_map.181), channel_id=1, replica_groups={{1,0,2,3,7,5,6,4},{17,16,18,19,23,21,22,20},{33,32,34,35,39,37,38,36},{..., dimensions={0} | all-to-all | bytes 294912 | tf_op jit(solution)/shard_map/all_to_all | solution.py:373
  71.1 0.1 shard_map.182
  71.2 10.6 %all_to_all.41.recv_ref = bf16[16,40,128]{2,1,0:T(8,128)(2,1)S(1)} all-to-all(bf16[16,40,128]{2,1,0:T(8,128)(2,1)S(1)} %shard_map.182), channel_id=1, replica_groups={{96,16,64,0,88,40,112,104,24,32,80,72,8,120,56,48},{97,17,65,1,89,41,11..., dimensions={0} | all-to-all | bytes 327680 | tf_op jit(solution)/shard_map/all_to_all | solution.py:373
  81.8 0.6 shard_map.183
  (1 shorter events, 0.0 us)
Async XLA Ops:
  0.6 14.2 %copy-start.3 = (bf16[512,2048]{1,0:T(8,128)(2,1)S(1)}, bf16[512,2048]{1,0:T(8,128)(2,1)}, u32[]{:S(2)}) copy-start(bf16[512,2048]{1,0:T(8,128)(2,1)} %proj_ref.2) | copy-start | bytes 6291460
  14.8 9.7 %copy-start.8 = (f32[4,2048]{1,0:T(4,128)S(1)}, f32[4,2048]{1,0:T(4,128)}, u32[]{:S(2)}) copy-start(f32[4,2048]{1,0:T(4,128)} %hidden_ref.1) | copy-start | bytes 98308
  24.5 16.5 %copy-start = (bf16[1,2048,1536]{2,1,0:T(8,128)(2,1)S(1)}, bf16[1,2048,1536]{2,1,0:T(8,128)(2,1)}, u32[]{:S(2)}) copy-start(bf16[1,2048,1536]{2,1,0:T(8,128)(2,1)} %up_ref.2) | copy-start | bytes 18874372
  24.5 16.5 %copy-start.1 = (bf16[2048,1024]{1,0:T(8,128)(2,1)S(1)}, bf16[2048,1024]{1,0:T(8,128)(2,1)}, u32[]{:S(2)}) copy-start(bf16[2048,1024]{1,0:T(8,128)(2,1)} %proj_ref.3) | copy-start | bytes 12582916
  24.5 16.5 %copy-start.2 = (bf16[1,768,2048]{2,1,0:T(8,128)(2,1)S(1)}, bf16[1,768,2048]{2,1,0:T(8,128)(2,1)}, u32[]{:S(2)}) copy-start(bf16[1,768,2048]{2,1,0:T(8,128)(2,1)} %down_ref.2) | copy-start | bytes 9437188
  24.5 16.5 %copy-start.6 = (bf16[2048,128]{1,0:T(8,128)(2,1)S(1)}, bf16[2048,128]{1,0:T(8,128)(2,1)}, u32[]{:S(2)}) copy-start(bf16[2048,128]{1,0:T(8,128)(2,1)} %router_ref.2) | copy-start | bytes 1572868
  24.5 16.4 %copy-start.9 = (f32[2048]{0:T(1024)S(1)}, f32[2048]{0:T(1024)}, u32[]{:S(2)}) copy-start(f32[2048]{0:T(1024)} %param.23) | copy-start | bytes 24580
  50.6 12.0 %copy-start.4 = (bf16[1,1024,768]{2,1,0:T(8,128)(2,1)S(1)}, bf16[1,1024,768]{2,1,0:T(8,128)(2,1)}, u32[]{:S(2)}) copy-start(bf16[1,1024,768]{2,1,0:T(8,128)(2,1)} %up_ref.3) | copy-start | bytes 4718596
  50.6 12.0 %copy-start.5 = (bf16[1,384,1024]{2,1,0:T(8,128)(2,1)S(1)}, bf16[1,384,1024]{2,1,0:T(8,128)(2,1)}, u32[]{:S(2)}) copy-start(bf16[1,384,1024]{2,1,0:T(8,128)(2,1)} %down_ref.3) | copy-start | bytes 2359300
  50.6 12.0 %copy-start.7 = (bf16[1024,128]{1,0:T(8,128)(2,1)S(1)}, bf16[1024,128]{1,0:T(8,128)(2,1)}, u32[]{:S(2)}) copy-start(bf16[1024,128]{1,0:T(8,128)(2,1)} %router_ref.3) | copy-start | bytes 786436
  50.6 12.0 %copy-start.10 = (f32[1024]{0:T(1024)S(1)}, f32[1024]{0:T(1024)}, u32[]{:S(2)}) copy-start(f32[1024]{0:T(1024)} %param.29) | copy-start | bytes 12292

commit v9 on v8

--- a/solution.py
+++ b/solution.py
@@ -54,8 +54,8 @@
 
 
 SEQ_ORDER = (7, 6, 5, 4, 3, 1, 0, 2)
-ALL_ORDER = (0, 1, 2, 3, 4, 5, 6, 7, 8, 9, 10, 11, 12, 13, 14, 15)
-NEAR_ORDER = (1, 0, 2, 3, 7, 5, 6, 4)
+ALL_ORDER = (4, 1, 2, 3, 0, 5, 6, 7, 8, 9, 10, 11, 12, 13, 14, 15)
+NEAR_ORDER = (5, 7, 0, 3, 6, 1, 4, 2)
 FAR_ORDER = (6, 1, 4, 0, 13, 10, 7, 14, 9, 2, 5, 12, 8, 15, 11, 3)
 NEAR = [[expert_of(far, near) for near in NEAR_ORDER] for far in range(16)]
 FAR = [[expert_of(far, near) for far in FAR_ORDER] for near in range(8)]

time: 82.7 us -> 81.2 us (0.982)
  blocking collectives: 73.9 us -> 72.4 us
    all_to_all x7, blocking collectives: 73.9 us -> 72.4 us  [exchange(): return lax.all_to_all(msg, axis, 0, 0, axis_index_groups=groups)]
where the time goes in v9:
time: 81.2 us; the launch traced here: 80.9 us
  blocking collectives  72.4 us (89%)
  Pallas kernels  7.77 us (10%)
    all_to_all x7, blocking collectives, exchange(): return lax.all_to_all(msg, axis, 0, 0, axis_index_groups=groups)  72.4 us
    pallas_call x8, Pallas kernels, call(): pl.pallas_call(kernel, out_shape=outs, in_specs=[pl.BlockSpec(memory_spac...  7.77 us

profile of v9, /device:TPU:0, one launch (start us, length us, event | category | flops | bytes accessed | tf_op | source)
XLA Modules:
  0.0 80.9 jit_solution(5058853539761190564)
XLA Ops:
  0.6 0.0 copy-start.3
  0.6 3.2 %shard_map.176 = (bf16[8,16,256]{2,1,0:T(8,128)(2,1)S(1)}, bf16[64,256]{1,0:T(8,128)(2,1)S(1)}, f32[2,8,128]{2,1,0:T(8,128)S(1)}, bf16[2,128,128]{2,1,0:T(8,128)...) custom-call(s32[4]{0:T(128)} %len_hbm.1, bf16[4,4096]{1,0:T(4,128)(2,1)} %q_hbm.1, ...), custom_call_target="tpu_custom_call" | custom-call | flops 99999997952 | bytes 1048576 | tf_op jit(solution)/shard_map/pallas_call | solution.py:357
  3.9 10.9 %all_to_all.35.recv_ref = bf16[8,16,256]{2,1,0:T(8,128)(2,1)S(1)} all-to-all(bf16[8,16,256]{2,1,0:T(8,128)(2,1)S(1)} %get-tuple-element.14), channel_id=1, replica_groups={{112,96,80,64,48,16,0,32},{113,97,81,65,49,17,1,33},{114,98,82,66,50,18..., dimensions={0} | all-to-all | bytes 131072 | tf_op jit(solution)/shard_map/all_to_all | solution.py:373
  14.8 0.0 copy-done.3
  14.8 0.0 copy-start.8
  14.8 0.6 shard_map.177
  15.4 9.1 %all_to_all.36.recv_ref = bf16[8,16,512]{2,1,0:T(8,128)(2,1)S(1)} all-to-all(bf16[8,16,512]{2,1,0:T(8,128)(2,1)S(1)} %shard_map.177), channel_id=1, replica_groups={{112,96,80,64,48,16,0,32},{113,97,81,65,49,17,1,33},{114,98,82,66,50,18..., dimensions={0} | all-to-all | bytes 262144 | tf_op jit(solution)/shard_map/all_to_all | solution.py:373
  24.5 0.0 copy-done.8
  24.5 0.0 copy-start
  24.5 0.0 copy-start.1
  24.5 0.0 copy-start.2
  24.5 0.0 copy-start.6
  24.5 0.0 copy-start.9
  24.6 14.1 %all_to_all.37 = bf16[16,16,512]{2,1,0:T(8,128)(2,1)S(1)} all-to-all(bf16[16,16,512]{2,1,0:T(8,128)(2,1)S(1)} %get-tuple-element.15), channel_id=1, replica_groups={{4,1,2,3,0,5,6,7,8,9,10,11,12,13,14,15},{20,17,18,19,16,21,22,23,24,25,..., dimensions={0} | all-to-all | bytes 524288 | tf_op jit(solution)/shard_map/all_to_all | solution.py:373
  38.7 0.0 copy-done
  38.7 0.0 copy-done.1
  38.7 0.0 copy-done.2
  38.7 0.0 copy-done.6
  38.7 0.0 copy-done.9
  38.7 2.1 %shard_map.179 = (bf16[8,16,512]{2,1,0:T(8,128)(2,1)S(1)}, f32[16,8,128]{2,1,0:T(8,128)S(1)}, f32[8,1024]{1,0:T(8,128)S(1)}) custom-call(bf16[256,512]{1,0:T(8,128)(2,1)S(1)} %bitcast.6, bf16[64,256]{1,0:T(8,128)(2,1)S(1)} %get-tuple-element.16.chosen_ref, f32[2,8,128]{2,1,0:T(8,128)S(1)} %get-tuple-element.17.picks_ref, f32[1,2048]{1,0:T(1,128)S(1)} %bitcast.8, ...), custom_call_target="tpu_custom_call" | custom-call | flops 99999997952 | bytes 1048576 | tf_op jit(solution)/shard_map/pallas_call | solution.py:357
  40.9 8.3 %all_to_all.38 = bf16[8,16,512]{2,1,0:T(8,128)(2,1)S(1)} all-to-all(bf16[8,16,512]{2,1,0:T(8,128)(2,1)S(1)} %get-tuple-element.18), channel_id=1, replica_groups={{5,7,0,3,6,1,4,2},{21,23,16,19,22,17,20,18},{37,39,32,35,38,33,36,34},{..., dimensions={0} | all-to-all | bytes 262144 | tf_op jit(solution)/shard_map/all_to_all | solution.py:373
  49.2 0.0 copy-start.4
  49.2 0.0 copy-start.5
  49.2 0.0 copy-start.7
  49.2 0.0 copy-start.10
  49.2 0.2 shard_map.180
  49.4 11.5 %all_to_all.39.recv_ref = bf16[16,72,128]{2,1,0:T(8,128)(2,1)S(1)} all-to-all(bf16[16,72,128]{2,1,0:T(8,128)(2,1)S(1)} %shard_map.180), channel_id=1, replica_groups={{96,16,64,0,88,40,112,104,24,32,80,72,8,120,56,48},{97,17,65,1,89,41,11..., dimensions={0} | all-to-all | bytes 589824 | tf_op jit(solution)/shard_map/all_to_all | solution.py:373
  60.9 0.0 copy-done.4
  60.9 0.0 copy-done.5
  60.9 0.0 copy-done.7
  60.9 0.0 copy-done.10
  61.0 0.8 %shard_map.181 = bf16[8,72,128]{2,1,0:T(8,128)(2,1)S(1)} custom-call(bf16[16,72,128]{2,1,0:T(8,128)(2,1)S(1)} %all_to_all.39.recv_ref, f32[8,1024]{1,0:T(8,128)S(1)} %get-tuple-element.21.talk_ref, f32[2,8,128]{2,1,0:T(8,128)S(1)} %get-tuple-element.17.picks_ref, bf16[64,128]{1,0:T(8,128)(2,1)S(1)} %get-tuple-element.22.carry_ref, ...), custom_call_target="tpu_custom_call" | custom-call | flops 99999997952 | bytes 1048576 | tf_op jit(solution)/shard_map/pallas_call | solution.py:357
  61.8 7.9 %all_to_all.40.recv_ref = bf16[8,72,128]{2,1,0:T(8,128)(2,1)S(1)} all-to-all(bf16[8,72,128]{2,1,0:T(8,128)(2,1)S(1)} %shard_map.181), channel_id=1, replica_groups={{5,7,0,3,6,1,4,2},{21,23,16,19,22,17,20,18},{37,39,32,35,38,33,36,34},{..., dimensions={0} | all-to-all | bytes 294912 | tf_op jit(solution)/shard_map/all_to_all | solution.py:373
  69.7 0.1 shard_map.182
  69.7 10.6 %all_to_all.41.recv_ref = bf16[16,40,128]{2,1,0:T(8,128)(2,1)S(1)} all-to-all(bf16[16,40,128]{2,1,0:T(8,128)(2,1)S(1)} %shard_map.182), channel_id=1, replica_groups={{96,16,64,0,88,40,112,104,24,32,80,72,8,120,56,48},{97,17,65,1,89,41,11..., dimensions={0} | all-to-all | bytes 327680 | tf_op jit(solution)/shard_map/all_to_all | solution.py:373
  80.3 0.6 shard_map.183
  (1 shorter events, 0.0 us)
Async XLA Ops:
  0.6 14.2 %copy-start.3 = (bf16[512,2048]{1,0:T(8,128)(2,1)S(1)}, bf16[512,2048]{1,0:T(8,128)(2,1)}, u32[]{:S(2)}) copy-start(bf16[512,2048]{1,0:T(8,128)(2,1)} %proj_ref.2) | copy-start | bytes 6291460
  14.8 9.7 %copy-start.8 = (f32[4,2048]{1,0:T(4,128)S(1)}, f32[4,2048]{1,0:T(4,128)}, u32[]{:S(2)}) copy-start(f32[4,2048]{1,0:T(4,128)} %hidden_ref.1) | copy-start | bytes 98308
  24.5 14.2 %copy-start = (bf16[1,2048,1536]{2,1,0:T(8,128)(2,1)S(1)}, bf16[1,2048,1536]{2,1,0:T(8,128)(2,1)}, u32[]{:S(2)}) copy-start(bf16[1,2048,1536]{2,1,0:T(8,128)(2,1)} %up_ref.2) | copy-start | bytes 18874372
  24.5 14.2 %copy-start.1 = (bf16[2048,1024]{1,0:T(8,128)(2,1)S(1)}, bf16[2048,1024]{1,0:T(8,128)(2,1)}, u32[]{:S(2)}) copy-start(bf16[2048,1024]{1,0:T(8,128)(2,1)} %proj_ref.3) | copy-start | bytes 12582916
  24.5 14.2 %copy-start.2 = (bf16[1,768,2048]{2,1,0:T(8,128)(2,1)S(1)}, bf16[1,768,2048]{2,1,0:T(8,128)(2,1)}, u32[]{:S(2)}) copy-start(bf16[1,768,2048]{2,1,0:T(8,128)(2,1)} %down_ref.2) | copy-start | bytes 9437188
  24.5 14.2 %copy-start.6 = (bf16[2048,128]{1,0:T(8,128)(2,1)S(1)}, bf16[2048,128]{1,0:T(8,128)(2,1)}, u32[]{:S(2)}) copy-start(bf16[2048,128]{1,0:T(8,128)(2,1)} %router_ref.2) | copy-start | bytes 1572868
  24.5 14.2 %copy-start.9 = (f32[2048]{0:T(1024)S(1)}, f32[2048]{0:T(1024)}, u32[]{:S(2)}) copy-start(f32[2048]{0:T(1024)} %param.23) | copy-start | bytes 24580
  49.2 11.7 %copy-start.4 = (bf16[1,1024,768]{2,1,0:T(8,128)(2,1)S(1)}, bf16[1,1024,768]{2,1,0:T(8,128)(2,1)}, u32[]{:S(2)}) copy-start(bf16[1,1024,768]{2,1,0:T(8,128)(2,1)} %up_ref.3) | copy-start | bytes 4718596
  49.2 11.7 %copy-start.5 = (bf16[1,384,1024]{2,1,0:T(8,128)(2,1)S(1)}, bf16[1,384,1024]{2,1,0:T(8,128)(2,1)}, u32[]{:S(2)}) copy-start(bf16[1,384,1024]{2,1,0:T(8,128)(2,1)} %down_ref.3) | copy-start | bytes 2359300
  49.2 11.7 %copy-start.7 = (bf16[1024,128]{1,0:T(8,128)(2,1)S(1)}, bf16[1024,128]{1,0:T(8,128)(2,1)}, u32[]{:S(2)}) copy-start(bf16[1024,128]{1,0:T(8,128)(2,1)} %router_ref.3) | copy-start | bytes 786436
  49.2 11.7 %copy-start.10 = (f32[1024]{0:T(1024)S(1)}, f32[1024]{0:T(1024)}, u32[]{:S(2)}) copy-start(f32[1024]{0:T(1024)} %param.29) | copy-start | bytes 12292
